TPU v7x, 512 devices: a whole 4x4x16 slice. The times are simulated.
512 devices in a mesh: dp: 8 (over y, x_lo), fsdp: 64 (over x_hi, z, core).
Axes of the slice: x: 4 (x_hi: 2, x_lo: 2; x = x_hi * 2 + x_lo), y: 4, z: 16, core: 2. Of those that a mesh axis runs over, the one named last changes fastest.
Arguments:
- hidden_in: bfloat16 [2048, 8192], P('dp', 'fsdp'), may hold values from -4 to 4
- out_grad: bfloat16 [2048, 8192], P('dp', 'fsdp'), may hold values from -6 to 6
- snapshot_ids: int32 [8, 256], P('dp'), may hold values from 0 to 3, never falling along the last dimension, each value on 1 to 128 neighbouring positions
- norm_gain: bfloat16 [8192], P('fsdp'), may hold values from 0.5 to 1.5
- wq_codes: bfloat16 [8192, 8192], P(None, 'fsdp'), may hold values from -0.044194174 to 0.044194174
- wq_scales: bfloat16 [256, 8192], P(None, 'fsdp'), may hold values from 0.5 to 2
- wkv_codes: bfloat16 [8192, 2048], P(None, 'fsdp'), may hold values from -0.044194174 to 0.044194174
- wkv_scales: bfloat16 [256, 2048], P(None, 'fsdp'), may hold values from 0.5 to 2
- wo_codes: bfloat16 [8192, 8192], P('fsdp'), may hold values from -0.0625 to 0.0625
- wo_scales: bfloat16 [256, 8192], P('fsdp'), may hold values from 0.5 to 2
- a_query: bfloat16 [64, 8192], P(None, 'fsdp'), may hold values from -0.0625 to 0.0625
- query_up_weight: bfloat16 [64, 8192], P(None, 'fsdp'), may hold values from -0.75 to 0.75
- a_value: bfloat16 [64, 8192], P(None, 'fsdp'), may hold values from -0.0625 to 0.0625
- value_up_weight: bfloat16 [64, 1024], P(None, 'fsdp'), may hold values from -0.75 to 0.75
Outputs:
- grad_a_query: float32 [8192, 64], P('fsdp')
- query_up_gradient: float32 [64, 8192], P(None, 'fsdp')
- grad_a_value: float32 [8192, 64], P('fsdp')
- grad_b_value: float32 [64, 1024], P(None, 'fsdp')
Inputs may be any that keep to these rules, and one draw needn't show every extreme that they name: `snapshot_ids`: snapshot numbers never fall along a row; each snapshot spans 1 to 128 positions, and one spans exactly 128.
All inputs are finite; a program needn't handle non-finite values.
Results may differ from a plain program's by a relative error of at most 0.017.
The roundings to bfloat16 on the way count: a program that leaves them out, or rounds other values in their place, can miss the bound.
Values may be sent and summed in bfloat16 or wider, within the bound.
No kernel may reach another device: no remote copies, remote signals or barrier semaphores. Data moves between devices by JAX's collectives and lax.ppermute only.
A program may use at most 64 MiB of HBM per device.

v0:
```python
import math

import jax
import jax.numpy as jnp
from jax import lax
from jax.sharding import PartitionSpec as P

GROUP = 8


EPS = 1e-05
ADAPTER_SCALE = 0.5
ROPE_BASE = 500000.0
MASKED = -1e30


def from_partner(value, axis, apart):
    mask = 2**apart
    pairs = [(source, source ^ mask) for source in range(lax.axis_size(axis))]
    return lax.ppermute(value, axis, pairs)


def dequantize(codes, scales, block_axis):
    block_rows = codes.shape[block_axis] // scales.shape[block_axis]
    scale_wide = jnp.repeat(scales.astype(jnp.float32), block_rows, axis=block_axis)
    return (codes.astype(jnp.float32) * scale_wide).astype(jnp.bfloat16)


def rope_tables(length, head_dim):
    half_width = head_dim // 2
    positions = jnp.arange(length).astype(jnp.float32)[:, None]
    frequency = jnp.exp(
        jnp.arange(half_width).astype(jnp.float32) * (-2.0 * math.log(ROPE_BASE) / head_dim)
    )
    angles = positions * frequency[None, :]
    return (jnp.cos(angles), jnp.sin(angles))


def rotate(values_in, cosine_table, sine_table):
    half_width = values_in.shape[-1] // 2
    front_half = values_in[..., :half_width]
    back_half = values_in[..., half_width:]
    return jnp.concatenate(
        [
            front_half * cosine_table - back_half * sine_table,
            back_half * cosine_table + front_half * sine_table,
        ],
        axis=-1,
    )


def unrotate(grads_in, cosine_table, sine_table):
    half_width = grads_in.shape[-1] // 2
    front_half = grads_in[..., :half_width]
    back_half = grads_in[..., half_width:]
    return jnp.concatenate(
        [
            front_half * cosine_table + back_half * sine_table,
            back_half * cosine_table - front_half * sine_table,
        ],
        axis=-1,
    )


def contract_matrices(left_arr, right_arr, left_dim, right_dim):
    return lax.dot_general(
        left_arr,
        right_arr,
        (((left_dim,), (right_dim,)), ((), ())),
        preferred_element_type=jnp.float32,
    )


def contract_exact(left_arr, right_arr):
    return lax.dot_general(
        left_arr,
        right_arr,
        (((0,), (0,)), ((), ())),
        precision=lax.Precision.HIGHEST,
        preferred_element_type=jnp.float32,
    )


def normalize(whole_x, whole_gain):
    hidden_f = whole_x.astype(jnp.float32)
    mean_sq = jnp.mean(hidden_f * hidden_f, axis=1, keepdims=True)
    return (hidden_f * lax.rsqrt(mean_sq + EPS) * whole_gain.astype(jnp.float32)).astype(
        jnp.bfloat16
    )


def fold_group(value_contribution, head_index):
    running = value_contribution
    for level_bit in range(GROUP.bit_length() - 2, -1, -1):
        half_width = running.shape[1] // 2
        upper_side = head_index // (1 << level_bit) % 2 == 1
        kept_part = jnp.where(upper_side, running[:, half_width:], running[:, :half_width])
        sent_part = jnp.where(upper_side, running[:, :half_width], running[:, half_width:])
        running = kept_part + from_partner(sent_part, "fsdp", level_bit)
    return running


def collect_group(own_columns, head_index):
    running = own_columns
    for level_bit in range(GROUP.bit_length() - 1):
        partner = from_partner(running, "fsdp", level_bit)
        upper_side = head_index // (1 << level_bit) % 2 == 1
        running = jnp.where(
            upper_side,
            jnp.concatenate([partner, running], axis=1),
            jnp.concatenate([running, partner], axis=1),
        )
    return running


def local(
    hidden_in,
    out_grad,
    snapshot_ids,
    norm_gain,
    wq_codes,
    wq_scales,
    wkv_codes,
    wkv_scales,
    wo_codes,
    wo_scales,
    a_query,
    query_up_weight,
    a_value,
    value_up_weight,
):
    head_index = lax.axis_index("fsdp")
    length = hidden_in.shape[0]
    head_dim = wq_codes.shape[1]
    rank_size = a_query.shape[0]
    position_width = wkv_codes.shape[1]
    key_positions = head_dim // position_width
    group_index = head_index // GROUP
    inside_group_index = head_index % GROUP
    whole_x, whole_dy, whole_gain, down_q, down_v, value_up_output = (
        lax.all_gather(hidden_in, "fsdp", axis=1, tiled=True),
        lax.all_gather(out_grad, "fsdp", axis=1, tiled=True),
        lax.all_gather(norm_gain[None, :], "fsdp", axis=1, tiled=True),
        lax.all_gather(a_query, "fsdp", axis=1, tiled=True),
        lax.all_gather(a_value, "fsdp", axis=1, tiled=True),
        lax.all_gather(value_up_weight, "fsdp", axis=1, tiled=True),
    )
    normalized_input = normalize(whole_x, whole_gain)
    query_rank_rows = contract_matrices(normalized_input, down_q, 1, 1).astype(jnp.bfloat16)
    value_rank_rows = contract_matrices(normalized_input, down_v, 1, 1).astype(jnp.bfloat16)
    wq_panel = dequantize(wq_codes, wq_scales, 0)
    wkv_panel = dequantize(wkv_codes, wkv_scales, 0)
    key_value_portion = jnp.dot(normalized_input, wkv_panel, preferred_element_type=jnp.float32)
    leading_column = (
        group_index * head_dim + jnp.maximum(inside_group_index - key_positions, 0) * position_width
    )
    adapter_columns = lax.dynamic_slice_in_dim(value_up_output, leading_column, position_width, 1)
    adapter_contribution = ADAPTER_SCALE * jnp.dot(
        value_rank_rows, adapter_columns, preferred_element_type=jnp.float32
    )
    key_value_portion = key_value_portion + jnp.where(
        inside_group_index >= key_positions, adapter_contribution, 0.0
    )
    kv_group = collect_group(key_value_portion.astype(jnp.bfloat16), head_index)
    query_linear = jnp.dot(
        normalized_input, wq_panel, preferred_element_type=jnp.float32
    ) + ADAPTER_SCALE * jnp.dot(
        query_rank_rows, query_up_weight, preferred_element_type=jnp.float32
    )
    cosine_table, sine_table = rope_tables(length, head_dim)
    queries = rotate(query_linear, cosine_table, sine_table).astype(jnp.bfloat16)
    keys_rot = rotate(kv_group[:, :head_dim].astype(jnp.float32), cosine_table, sine_table).astype(
        jnp.bfloat16
    )
    values_grp = kv_group[:, head_dim:]
    score_scale = head_dim ** (-0.5)
    scores = contract_matrices(queries, keys_rot, 1, 1) * score_scale
    positions = jnp.arange(length)
    causal = positions[None, :] <= positions[:, None]
    segment = snapshot_ids[0]
    allowed = jnp.logical_and(causal, segment[:, None] == segment[None, :])
    scores = jnp.where(allowed, scores, MASKED)
    row_top = jnp.max(scores, axis=-1, keepdims=True)
    weights_raw = jnp.exp(scores - row_top)
    prob = weights_raw / jnp.sum(weights_raw, axis=-1, keepdims=True)
    prob_b = prob.astype(jnp.bfloat16)
    wo_panel = dequantize(wo_codes, wo_scales, 0)
    grad_ctx = contract_matrices(whole_dy, wo_panel, 1, 1).astype(jnp.bfloat16)
    grad_prob = contract_matrices(grad_ctx, values_grp, 1, 1)
    value_gradient = contract_matrices(prob_b, grad_ctx, 0, 0).astype(jnp.bfloat16)
    grad_score = (prob * (grad_prob - jnp.sum(prob * grad_prob, axis=-1, keepdims=True))).astype(
        jnp.bfloat16
    )
    grad_query = jnp.dot(grad_score, keys_rot, preferred_element_type=jnp.float32) * score_scale
    query_linear_gradient = unrotate(grad_query, cosine_table, sine_table).astype(jnp.bfloat16)
    query_up_output = ADAPTER_SCALE * contract_matrices(
        query_rank_rows, query_linear_gradient, 0, 0
    )
    value_contribution = ADAPTER_SCALE * contract_matrices(value_rank_rows, value_gradient, 0, 0)
    grouped_up_weight = lax.dynamic_slice_in_dim(
        value_up_output, group_index * head_dim, head_dim, 1
    )
    grad_low = jnp.concatenate(
        [
            ADAPTER_SCALE * contract_matrices(query_linear_gradient, query_up_weight, 1, 1),
            ADAPTER_SCALE * contract_matrices(value_gradient, grouped_up_weight, 1, 1),
        ],
        axis=1,
    )
    column_block = normalized_input.astype(jnp.float32)
    rows_here = lax.psum_scatter(
        contract_exact(column_block, grad_low), "fsdp", scatter_dimension=0, tiled=True
    )
    value_here = fold_group(value_contribution, head_index)
    rows_total, query_total, value_total = (
        lax.psum(rows_here.astype(jnp.bfloat16), "dp").astype(jnp.float32),
        lax.psum(query_up_output.astype(jnp.bfloat16), "dp").astype(jnp.float32),
        lax.psum(value_here.astype(jnp.bfloat16), "dp").astype(jnp.float32),
    )
    return (rows_total[:, :rank_size], query_total, rows_total[:, rank_size:], value_total)


def solution(mesh):
    in_specs = (
        P("dp", "fsdp"),
        P("dp", "fsdp"),
        P("dp", None),
        P("fsdp"),
        P(None, "fsdp"),
        P(None, "fsdp"),
        P(None, "fsdp"),
        P(None, "fsdp"),
        P("fsdp", None),
        P("fsdp", None),
        P(None, "fsdp"),
        P(None, "fsdp"),
        P(None, "fsdp"),
        P(None, "fsdp"),
    )
    out_specs = (P("fsdp", None), P(None, "fsdp"), P("fsdp", None), P(None, "fsdp"))
    return jax.shard_map(local, mesh=mesh, in_specs=in_specs, out_specs=out_specs, check_vma=False)
```

profile of v0, /device:TPU:32, one launch (start us, length us, event | category | flops | bytes accessed | tf_op | source)
XLA Modules:
  0.0 839.4 jit_solution(10529867327911418951)
XLA Ops:
  10.1 78.5 %all-gather.1 = bf16[64,1,128]{2,1,0:T(2,128)(2,1)S(1)} all-gather(bf16[1,1,128]{2,1,0:T(2,128)(2,1)} %bitcast.34), channel_id=2, replica_groups=mesh['dp'=8,'fsdp'=64] {'fsdp'}, dimensions={0}, use_global_device_ids=true | all-gather | bytes 16640 | tf_op jit(solution)/shard_map/all_gather | solution.py:143
  89.5 3.3 broadcast_in_dim.30
  92.8 3.5 reshape.40
  98.4 3.4 fusion.4
  101.9 76.8 %all_gather.22 = bf16[64,1024]{0,1:T(8,128)(2,1)S(1)} all-gather(bf16[64,16]{0,1:T(8,128)(2,1)S(1)} %copy-done.7), channel_id=1, replica_groups=mesh['dp'=8,'fsdp'=64] {'fsdp'}, dimensions={1}, use_global_device_ids=true | all-gather | bytes 133120 | tf_op jit(solution)/shard_map/all_gather | solution.py:146
  178.7 3.3 fusion
  182.2 3.2 fusion.2
  185.3 106.7 %all-gather.11.cloned.1.call-done = bf16[64,8192]{1,0:T(8,128)(2,1)} async-done(((bf16[64,128]{1,0:T(8,128)(2,1)}), bf16[64,8192]{1,0:T(8,128)(2,1)}) %all-gather.11.cloned.1.call-update) | async-done | bytes 1048592 | tf_op jit(solution)/shard_map/all_gather | solution.py:145
  292.0 4.0 convolution_convert_fusion.2
  297.5 2.2 collective-permute-start
  299.7 122.3 %all-gather.9.cloned.1.call-done = bf16[64,8192]{1,0:T(8,128)(2,1)} async-done(((bf16[64,128]{1,0:T(8,128)(2,1)}), bf16[64,8192]{1,0:T(8,128)(2,1)}) %all-gather.9.cloned.1.call-update) | async-done | bytes 1048592 | tf_op jit(solution)/shard_map/all_gather | solution.py:144
  422.0 4.0 convolution_convert_fusion.3
  426.3 2.6 collective-permute-start.1
  428.9 3.1 convolution_add_fusion
  432.1 4.2 collective-permute-start.2
  436.4 131.5 %all-gather.13.cloned.1.call-done = bf16[256,8192]{1,0:T(8,128)(2,1)} async-done(((bf16[256,128]{1,0:T(8,128)(2,1)}), bf16[256,8192]{1,0:T(8,128)(2,1)}) %all-gather.13.cloned.1.call-update) | async-done | bytes 4194320 | tf_op jit(solution)/shard_map/all_gather | solution.py:142
  567.8 3.7 convolution_convert_fusion
  573.8 5.9 fusion.14
  579.9 4.1 collective-permute-start.3
  584.0 2.6 collective-permute-done.3
  586.8 2.4 collective-permute-start.4
  589.2 3.4 collective-permute-done.4
  595.9 199.2 %reduce-scatter.2.cloned.1.call-done = f32[128,128]{1,0:T(8,128)} async-done(((f32[8192,128]{1,0:T(8,128)}), f32[128,128]{1,0:T(8,128)}) %reduce-scatter.2.cloned.1.call-update) | async-done | bytes 65552 | tf_op jit(solution)/shard_map/reduce_scatter | solution.py:211
  796.0 34.0 %all-reduce = (bf16[128,128]{1,0:T(8,128)(2,1)S(1)}, bf16[64,16]{1,0:T(8,128)(2,1)S(1)}, bf16[64,128]{1,0:T(8,128)(2,1)S(1)}) all-reduce(bf16[128,128]{1,0:T(8,128)(2,1)S(1)} %convert_element_type.160, bf16[64,16]{1,0:T(8,128)(2,1)S(1)} %add_convert_fusion, bf16[64,128]{1,0:T(8,128)(2,1)S(1)} %fusion.8), channel_id=1, replica_groups=mesh['dp'=8,'fsdp'=64] {'dp'}, use_global_device_ids=true, to_apply=%region_5.6 | all-reduce | flops 25600 | bytes 102400 | tf_op jit(solution)/shard_map/psum | solution.py:216
  (71 shorter events, 17.2 us)
Async XLA Ops:
  7.2 418.9 %copy-start = (bf16[64,128]{1,0:T(8,128)(2,1)S(1)}, bf16[64,128]{1,0:T(8,128)(2,1)}, u32[]{:S(2)}) copy-start(bf16[64,128]{1,0:T(8,128)(2,1)} %param.25) | copy-start | bytes 49156
  7.2 171.5 %all-gather.7.cloned.1.call-start = ((), (), s32[]{:S(2)}) async-start(), calls=%async_computation.1 | async-start | bytes 4259840 | tf_op jit(solution)/shard_map/all_gather | solution.py:141
  7.9 284.1 %all-gather.11.cloned.1.call-start = ((), (), s32[]{:S(2)}) async-start(), calls=%async_computation.3 | async-start | bytes 1064960 | tf_op jit(solution)/shard_map/all_gather | solution.py:145
  8.7 413.4 %all-gather.9.cloned.1.call-start = ((), (), s32[]{:S(2)}) async-start(), calls=%async_computation.2 | async-start | bytes 1064960 | tf_op jit(solution)/shard_map/all_gather | solution.py:144
  9.4 558.4 %all-gather.13.cloned.1.call-start = ((), (), s32[]{:S(2)}) async-start(), calls=%async_computation.4 | async-start | bytes 4259840 | tf_op jit(solution)/shard_map/all_gather | solution.py:142
  10.0 785.2 %reduce-scatter.2.cloned.1.call-start = ((), (), s32[]{:S(2)}) async-start(), calls=%async_computation.5 | async-start | bytes 4259840 | tf_op jit(solution)/shard_map/reduce_scatter | solution.py:211
  89.5 6.9 copy-start.6
  96.4 5.5 copy-start.7
  178.7 3.5 copy-start.4
  292.0 4.0 copy-start.1
  292.0 4.0 copy-start.5
  297.5 128.8 %collective-permute-start = (bf16[256,32]{0,1:T(8,128)(2,1)S(1)}, bf16[256,32]{0,1:T(8,128)(2,1)S(1)}, u32[]{:S(2)}, u32[]{:S(2)}) collective-permute-start(bf16[256,32]{0,1:T(8,128)(2,1)S(1)} %fusion.9), channel_id=1, source_target_pairs={{0,1},{1,0},{2,3},{3,2},{4,5},{5,4},{6,7},{7,6},{8,9},{9,8},{10,11... | collective-permute-start | bytes 49160 | tf_op jit(solution)/shard_map/ppermute | solution.py:20
  422.0 6.9 copy-start.2
  426.3 5.8 collective-permute-start.1
  432.0 140.0 %copy-start.8 = (s32[1,256]{1,0:T(1,128)S(1)}, s32[1,256]{1,0:T(1,128)}, u32[]{:S(2)}) copy-start(s32[1,256]{1,0:T(1,128)} %param.16) | copy-start | bytes 3076
  432.1 139.4 %collective-permute-start.2 = (bf16[256,128]{0,1:T(8,128)(2,1)S(1)}, bf16[256,128]{0,1:T(8,128)(2,1)S(1)}, u32[]{:S(2)}, u32[]{:S(2)}) collective-permute-start(bf16[256,128]{0,1:T(8,128)(2,1)S(1)} %maximum_select_fusion.1), channel_id=1, source_target_pairs={{0,4},{1,5},{2,6},{3,7},{4,0},{5,1},{6,2},{7,3},{8,12},{9,13},{10,... | collective-permute-start | bytes 196616 | tf_op jit(solution)/shard_map/ppermute | solution.py:20
  571.6 2.2 copy-start.3
  579.9 6.7 collective-permute-start.3
  586.8 5.8 collective-permute-start.4
  592.7 3.1 collective-permute-start.5
Sparse Core Ops, SparseCore 0:
  11.0 151.6 all-gather.6
  165.7 126.2 all-gather.10
  295.0 126.9 all-gather.8
  424.9 142.9 all-gather.12
  579.8 215.2 reduce-scatter.1
where the time goes:
time: 841 us; the launch traced here: 839 us
  waiting for transfers between devices  569 us (68%)
  blocking collectives  189 us (22%)
  matrix products  24 us (3%)
  starting transfers between devices  17.5 us (2%)
  other arithmetic  15.5 us (2%)
  between operations  14.2 us (2%)
  local copies, waits for them, and re-layouts  9.27 us (1%)
    reduce_scatter x1, waiting for transfers between devices, local(): lax.psum_scatter(contract_exact(column_block, grad_low), 'fsdp', scatter_...  199 us
    all_gather x1, waiting for transfers between devices, local(): lax.all_gather(out_grad, 'fsdp', axis=1, tiled=True)  131 us
    all_gather x1, waiting for transfers between devices, local(): lax.all_gather(a_query, 'fsdp', axis=1, tiled=True)  122 us
    all_gather x1, waiting for transfers between devices, local(): lax.all_gather(a_value, 'fsdp', axis=1, tiled=True)  107 us
    all_gather x1, blocking collectives, local(): lax.all_gather(norm_gain[None, :], 'fsdp', axis=1, tiled=True)  78.5 us
    all_gather x1, blocking collectives, local(): lax.all_gather(value_up_weight, 'fsdp', axis=1, tiled=True)  76.8 us
    psum x1, blocking collectives, local(): lax.psum(rows_here.astype(jnp.bfloat16), 'dp').astype(jnp.float32)  34 us
    ppermute x6, starting transfers between devices, from_partner(): return lax.ppermute(value, axis, pairs)  17.3 us
  transfers between devices with their start and end apart: 11, of which 8 were waited for; matrix products, arithmetic and copies ran while one was open for 4% of the time, Pallas kernels for 0%

commit v1 on v0

v1 whole, which is shorter than its diff:
```python
import math

import jax
import jax.numpy as jnp
from jax import lax
from jax.sharding import PartitionSpec as P

GROUP = 8
EPS = 1e-05
ADAPTER_SCALE = 0.5
ROPE_BASE = 500000.0
MASKED = -1e30

NX, NZ, NC = 2, 16, 2
MASKS = (1, 32, 33)


def place(a, z, c):
    return a * (NZ * NC) + z * NC + c


Z_GROUPS = [[place(a, z, c) for z in range(NZ)] for a in range(NX) for c in range(NC)]
NEAR_GROUPS = [[GROUP * g + i for i in range(GROUP)] for g in range(8)]
FAR_GROUPS = [
    [place(a, z + 4 * k, c) for a in range(NX) for k in range(4)] for z in range(4) for c in range(NC)
]


def xor_pairs(mask):
    return [(i, i ^ mask) for i in range(NX * NZ * NC)]


def z_pairs(step):
    return [
        (place(a, z, c), place(a, (z + step) % NZ, c))
        for a in range(NX)
        for z in range(NZ)
        for c in range(NC)
    ]


def swap(value, mask):
    return lax.ppermute(value, "fsdp", xor_pairs(mask))


def rope_tables(length, head_dim):
    half_width = head_dim // 2
    positions = jnp.arange(length).astype(jnp.float32)[:, None]
    frequency = jnp.exp(
        jnp.arange(half_width).astype(jnp.float32) * (-2.0 * math.log(ROPE_BASE) / head_dim)
    )
    angles = positions * frequency[None, :]
    return (jnp.cos(angles), jnp.sin(angles))


def rotate(values_in, cosine_table, sine_table):
    half_width = values_in.shape[-1] // 2
    front_half = values_in[..., :half_width]
    back_half = values_in[..., half_width:]
    return jnp.concatenate(
        [
            front_half * cosine_table - back_half * sine_table,
            back_half * cosine_table + front_half * sine_table,
        ],
        axis=-1,
    )


def unrotate(grads_in, cosine_table, sine_table):
    return rotate(grads_in, cosine_table, -sine_table)


def contract(left_arr, right_arr, left_dim, right_dim):
    return lax.dot_general(
        left_arr,
        right_arr,
        (((left_dim,), (right_dim,)), ((), ())),
        preferred_element_type=jnp.float32,
    )


def two_terms(value):
    high = lax.reduce_precision(value, 8, 7)
    return high.astype(jnp.bfloat16), (value - high).astype(jnp.bfloat16)


def collect_group(own_columns, head_index):
    running = own_columns
    for level_bit in range(GROUP.bit_length() - 1):
        partner = swap(running, 1 << level_bit)
        upper_side = head_index // (1 << level_bit) % 2 == 1
        running = jnp.where(
            upper_side,
            jnp.concatenate([partner, running], axis=1),
            jnp.concatenate([running, partner], axis=1),
        )
    return running


def relative_order(blocks, z_index, axis):
    flipped = jnp.roll(jnp.flip(blocks, axis), 1, axis)
    doubled = jnp.concatenate([flipped, flipped], axis=axis)
    return lax.dynamic_slice_in_dim(doubled, (NZ - z_index) % NZ, NZ, axis)


def quarter(blocks, x_index, core_index, axis):
    taken = lax.dynamic_index_in_dim(blocks, x_index, axis, keepdims=False)
    return lax.dynamic_index_in_dim(taken, core_index, axis + 1, keepdims=False)


def spread(value, number):
    return jnp.broadcast_to(value[None], (number,) + value.shape)


def exchange(value, axis, groups=None):
    return lax.all_to_all(value, axis, 0, 0, axis_index_groups=groups)


def local(
    hidden_in,
    out_grad,
    snapshot_ids,
    norm_gain,
    wq_codes,
    wq_scales,
    wkv_codes,
    wkv_scales,
    wo_codes,
    wo_scales,
    a_query,
    query_up_weight,
    a_value,
    value_up_weight,
):
    f32, bf16 = jnp.float32, jnp.bfloat16
    head_index = lax.axis_index("fsdp")
    x_index = head_index // (NZ * NC)
    z_index = head_index // NC % NZ
    core_index = head_index % NC
    member = head_index % GROUP
    length, width = hidden_in.shape
    features = wq_codes.shape[0]
    rank = a_query.shape[0]
    kv_width = wkv_codes.shape[1]
    key_members = 128 // kv_width

    hidden_f = hidden_in.astype(f32)
    square_own = jnp.sum(hidden_f * hidden_f, axis=1)
    gained = (hidden_f * norm_gain.astype(f32)[None, :]).astype(bf16)
    square_high, square_low = two_terms(square_own)
    packet = jnp.concatenate(
        [
            gained,
            a_query,
            a_value,
            square_high.reshape(2, 128),
            square_low.reshape(2, 128),
            jnp.zeros((12, 128), bf16),
        ],
        axis=0,
    )
    dy_quarter = lax.all_gather(out_grad, "fsdp", axis=1, tiled=True, axis_index_groups=Z_GROUPS)

    forward, backward = [packet], [packet]
    for step in range(NZ // 2):
        forward.append(lax.ppermute(forward[-1], "fsdp", z_pairs(1)))
        if step < NZ // 2 - 1:
            backward.append(lax.ppermute(backward[-1], "fsdp", z_pairs(-1)))
    pieces = forward + backward[:0:-1]

    wq_blocks = wq_codes.reshape(NX, NZ, NC, 4, 32, 128)
    wq_levels = wq_scales.reshape(NX, NZ, NC, 4, 1, 128)
    wkv_blocks = wkv_codes.reshape(NX, NZ, NC, 4, 32, kv_width)
    wkv_levels = wkv_scales.reshape(NX, NZ, NC, 4, 1, kv_width)
    wo_blocks = wo_codes.reshape(4, 32, NX, NZ, NC, 128)
    wo_levels = wo_scales.reshape(4, 1, NX, NZ, NC, 128)

    def projection_of(mask):
        of_x, of_c = x_index ^ (mask // 32), core_index ^ (mask % 2)
        wq_part = (
            quarter(wq_blocks, of_x, of_c, 0).astype(f32) * quarter(wq_levels, of_x, of_c, 0).astype(f32)
        ).astype(bf16)
        wq_part = relative_order(wq_part.reshape(NZ, 128, 128), z_index, 0)
        wkv_part = (
            quarter(wkv_blocks, of_x, of_c, 0).astype(f32) * quarter(wkv_levels, of_x, of_c, 0).astype(f32)
        ).astype(bf16)
        wkv_part = jnp.transpose(wkv_part.reshape(NZ, 128, kv_width), (2, 0, 1))
        wkv_part = relative_order(wkv_part, z_index, 1)
        return jnp.concatenate(
            [wq_part.reshape(NZ * 128, 128), wkv_part.reshape(kv_width * NZ, 128)], axis=0
        )

    def output_of(mask):
        of_x, of_c = x_index ^ (mask // 32), core_index ^ (mask % 2)
        part = quarter(wo_blocks, of_x, of_c, 2).astype(f32) * quarter(wo_levels, of_x, of_c, 2).astype(f32)
        return part.astype(bf16).reshape(128, NZ * 128)

    projections = [projection_of(0)] + [swap(projection_of(mask), mask) for mask in MASKS]
    outputs = [output_of(0)] + [swap(output_of(mask), mask) for mask in MASKS]
    value_up_group = collect_group(value_up_weight, head_index)

    wq_all = jnp.concatenate([p[: NZ * 128] for p in projections], axis=1)
    wkv_all = jnp.concatenate([p[NZ * 128 :].reshape(kv_width, NZ * 128) for p in projections], axis=0)
    wo_all = jnp.concatenate(outputs, axis=0)

    inputs = jnp.concatenate([p[:length] for p in pieces], axis=1)
    downs = jnp.concatenate([p[length : length + 2 * rank] for p in pieces], axis=1)
    squares = sum(
        p[length + 2 * rank : length + 2 * rank + 2].astype(f32)
        + p[length + 2 * rank + 2 : length + 2 * rank + 4].astype(f32)
        for p in pieces
    )
    q_parts = contract(inputs, wq_all, 1, 0)
    kv_parts = contract(inputs, wkv_all, 1, 1)
    low_part = contract(inputs, downs, 1, 1)
    squares_high, squares_low = two_terms(squares)

    def parcel(slot):
        kv_part = kv_parts[:, slot * kv_width : (slot + 1) * kv_width]
        kv_part = jnp.concatenate([kv_part[64 * j : 64 * j + 64] for j in range(4)], axis=1)
        return jnp.concatenate(
            [
                q_parts[:, slot * 128 : (slot + 1) * 128].astype(bf16),
                low_part.astype(bf16),
                kv_part.astype(bf16),
                squares_high,
                squares_low,
                jnp.zeros((12, 128), bf16),
            ],
            axis=0,
        )

    arrived = [swap(parcel(slot + 1), mask) for slot, mask in enumerate(MASKS)]
    q_sum = q_parts[:, :128] + sum(p[:length].astype(f32) for p in arrived)
    low_sum = low_part + sum(p[length : 2 * length].astype(f32) for p in arrived)
    kv_own = kv_parts[:, :kv_width]
    kv_own = jnp.concatenate([kv_own[64 * j : 64 * j + 64] for j in range(4)], axis=1)
    kv_sum = kv_own + sum(p[2 * length : 2 * length + 64].astype(f32) for p in arrived)
    square_sum = squares + sum(
        p[2 * length + 64 : 2 * length + 66].astype(f32) + p[2 * length + 66 : 2 * length + 68].astype(f32)
        for p in arrived
    )
    inverse = lax.rsqrt(square_sum.reshape(length, 1) / features + EPS)
    low_both = (low_sum * inverse).astype(bf16)
    query_rank_rows, value_rank_rows = low_both[:, :rank], low_both[:, rank:]

    kv_columns = jnp.concatenate([kv_sum[:, 32 * j : 32 * j + 32] for j in range(4)], axis=0) * inverse
    adapter_columns = lax.dynamic_slice_in_dim(
        value_up_group, jnp.maximum(member - key_members, 0) * kv_width, kv_width, 1
    )
    adapter_contribution = ADAPTER_SCALE * contract(value_rank_rows, adapter_columns, 1, 0)
    kv_columns = (kv_columns + jnp.where(member >= key_members, adapter_contribution, 0.0)).astype(bf16)
    kv_group = exchange(spread(kv_columns.reshape(64, 128), GROUP), "fsdp", NEAR_GROUPS)
    kv_group = jnp.transpose(kv_group.reshape(GROUP, length, kv_width), (1, 0, 2)).reshape(length, -1)
    head_dim = 128
    query_linear = q_sum * inverse + ADAPTER_SCALE * contract(query_rank_rows, query_up_weight, 1, 0)

    cosine_table, sine_table = rope_tables(length, head_dim)
    queries = rotate(query_linear, cosine_table, sine_table).astype(bf16)
    keys_rot = rotate(kv_group[:, :head_dim].astype(f32), cosine_table, sine_table).astype(bf16)
    values_grp = kv_group[:, head_dim:]
    score_scale = head_dim ** (-0.5)
    scores = contract(queries, keys_rot, 1, 1) * score_scale
    positions = jnp.arange(length)
    causal = positions[None, :] <= positions[:, None]
    segment = snapshot_ids[0]
    allowed = jnp.logical_and(causal, segment[:, None] == segment[None, :])
    scores = jnp.where(allowed, scores, MASKED)
    row_top = jnp.max(scores, axis=-1, keepdims=True)
    weights_raw = jnp.exp(scores - row_top)
    prob = weights_raw / jnp.sum(weights_raw, axis=-1, keepdims=True)
    prob_b = prob.astype(bf16)

    ctx_parts = contract(dy_quarter, wo_all, 1, 1)
    ctx_arrived = [
        swap(ctx_parts[:, 128 * (slot + 1) : 128 * (slot + 2)].astype(bf16), mask)
        for slot, mask in enumerate(MASKS)
    ]
    grad_ctx = (ctx_parts[:, :128] + sum(p.astype(f32) for p in ctx_arrived)).astype(bf16)

    grad_prob = contract(grad_ctx, values_grp, 1, 1)
    value_gradient = contract(prob_b, grad_ctx, 0, 0).astype(bf16)
    grad_score = (prob * (grad_prob - jnp.sum(prob * grad_prob, axis=-1, keepdims=True))).astype(bf16)
    grad_query = contract(grad_score, keys_rot, 1, 0) * score_scale
    query_linear_gradient = unrotate(grad_query, cosine_table, sine_table).astype(bf16)
    query_up_output = ADAPTER_SCALE * contract(query_rank_rows, query_linear_gradient, 0, 0)
    value_contribution = ADAPTER_SCALE * contract(value_rank_rows, value_gradient, 0, 0)
    grad_low = jnp.concatenate(
        [
            ADAPTER_SCALE * contract(query_linear_gradient, query_up_weight, 1, 1),
            ADAPTER_SCALE * contract(value_gradient, value_up_group, 1, 1),
        ],
        axis=1,
    )

    slice_rows = length // GROUP
    own_width = head_dim // GROUP
    value_slices = jnp.transpose(value_contribution.reshape(rank, GROUP, own_width), (1, 0, 2))
    outgoing = jnp.concatenate(
        [
            grad_low.astype(bf16).reshape(GROUP, slice_rows, 128),
            value_slices.reshape(GROUP, 8, 128).astype(bf16),
        ],
        axis=1,
    )
    near = jnp.sum(exchange(outgoing, "fsdp", NEAR_GROUPS).astype(f32), axis=0)
    low_near, value_here = near[:slice_rows], near[slice_rows:]
    far = exchange(spread(low_near.astype(bf16), 8), "fsdp", FAR_GROUPS)
    low_slice = jnp.sum(far.astype(f32), axis=0).astype(bf16)
    low_total = exchange(spread(low_slice, GROUP), "fsdp", NEAR_GROUPS).reshape(length, 128)
    normalized = (hidden_f * inverse * norm_gain.astype(f32)[None, :]).astype(bf16)
    rows_here = contract(normalized, low_total, 0, 0)

    mine = jnp.concatenate([rows_here, query_up_output, value_here], axis=0).astype(bf16)
    total = jnp.sum(exchange(spread(mine, 8), "dp").astype(f32), axis=0)
    rows_total = total[:width]
    return (
        rows_total[:, :rank],
        total[width : width + rank],
        rows_total[:, rank:],
        total[width + rank :].reshape(rank, own_width),
    )


def solution(mesh):
    in_specs = (
        P("dp", "fsdp"),
        P("dp", "fsdp"),
        P("dp", None),
        P("fsdp"),
        P(None, "fsdp"),
        P(None, "fsdp"),
        P(None, "fsdp"),
        P(None, "fsdp"),
        P("fsdp", None),
        P("fsdp", None),
        P(None, "fsdp"),
        P(None, "fsdp"),
        P(None, "fsdp"),
        P(None, "fsdp"),
    )
    out_specs = (P("fsdp", None), P(None, "fsdp"), P("fsdp", None), P(None, "fsdp"))
    return jax.shard_map(local, mesh=mesh, in_specs=in_specs, out_specs=out_specs, check_vma=False)
```

time: 841 us -> 306 us (0.36)
  the two profiles are of different devices: /device:TPU:32 before, /device:TPU:1 now
where the time goes in v1:
time: 306 us; the launch traced here: 303 us
  starting transfers between devices  116 us (38%)
  local copies, waits for them, and re-layouts  54.4 us (18%)
  blocking collectives  43.8 us (14%)
  other arithmetic  36.4 us (12%)
  waiting for transfers between devices  28.5 us (9%)
  between operations  15.9 us (5%)
  matrix products  8.29 us (3%)
    ppermute x15, starting transfers between devices, swap(): return lax.ppermute(value, 'fsdp', xor_pairs(mask))  51.9 us
    all_to_all x3, blocking collectives, exchange(): return lax.all_to_all(value, axis, 0, 0, axis_index_groups=groups)  43.8 us
    ppermute x7, starting transfers between devices, local(): backward.append(lax.ppermute(backward[-1], 'fsdp', z_pairs(-1)))  37.3 us
    ppermute x8, starting transfers between devices, local(): forward.append(lax.ppermute(forward[-1], 'fsdp', z_pairs(1)))  17.8 us
    unnamed x140, local copies, waits for them, and re-layouts  15.6 us
    convert_element_type x1, other arithmetic, output_of(): quarter(wo_blocks, of_x, of_c, 2).astype(f32)  14.2 us
    ppermute x15, waiting for transfers between devices, swap(): return lax.ppermute(value, 'fsdp', xor_pairs(mask))  11.6 us
    all_to_all x2, waiting for transfers between devices, exchange(): return lax.all_to_all(value, axis, 0, 0, axis_index_groups=groups)  9.67 us
  transfers between devices with their start and end apart: 33, of which 13 were waited for; matrix products, arithmetic and copies ran while one was open for 28% of the time, Pallas kernels for 0%

profile of v1, /device:TPU:1, one launch (start us, length us, event | category | flops | bytes accessed | tf_op | source)
XLA Modules:
  0.0 303.3 jit_solution(8567580257840632069)
XLA Ops:
  12.2 4.4 %collective-permute-start = (bf16[400,128]{0,1:T(8,128)(2,1)}, bf16[400,128]{0,1:T(8,128)(2,1)}, u32[]{:S(2)}, u32[]{:S(2)}) collective-permute-start(bf16[400,128]{0,1:T(8,128)(2,1)} %concatenate.149), channel_id=1, source_target_pairs={{0,2},{1,3},{2,4},{3,5},{4,6},{5,7},{6,8},{7,9},{8,10},{9,11},{10,... | collective-permute-start | bytes 307208 | tf_op jit(solution)/shard_map/ppermute | solution.py:166
  16.6 9.5 %collective-permute-start.8 = (bf16[400,128]{0,1:T(8,128)(2,1)}, bf16[400,128]{0,1:T(8,128)(2,1)}, u32[]{:S(2)}, u32[]{:S(2)}) collective-permute-start(bf16[400,128]{0,1:T(8,128)(2,1)} %concatenate.149), channel_id=1, source_target_pairs={{0,30},{1,31},{2,0},{3,1},{4,2},{5,3},{6,4},{7,5},{8,6},{9,7},{10,... | collective-permute-start | bytes 307208 | tf_op jit(solution)/shard_map/ppermute | solution.py:168
  55.9 4.6 %collective-permute-start.16 = (bf16[2560,128]{1,0:T(8,128)(2,1)}, bf16[2560,128]{1,0:T(8,128)(2,1)}, u32[]{:S(2)}, u32[]{:S(2)}) collective-permute-start(bf16[2560,128]{1,0:T(8,128)(2,1)} %pad_maximum_fusion.1), channel_id=1, source_target_pairs={{0,32},{1,33},{2,34},{3,35},{4,36},{5,37},{6,38},{7,39},{8,40},{9,... | collective-permute-start | bytes 1966088 | tf_op jit(solution)/shard_map/ppermute | solution.py:43
  71.4 14.2 %convert_reduce_fusion.3 = (f32[4,32,16,128]{3,2,1,0:T(8,128)S(1)}, f32[4,32,16,128]{3,2,1,0:T(8,128)}, f32[4,32,16,128]{3,2,1,0:T(8,128)}, f32[4,32,16,128]{3,2,1,0:T(8,128)}) fusion(bf16[4,32,2,16,2,128]{5,4,3,2,1,0:T(2,128)(2,1)S(1)} %reshape.370, s32[]{:T(128)S(6)} %select_n.182, s32[]{:T(128)S(6)} %select_n.185, s32[]{:T(128)S(6)} %select_n.193, ...), kind=kLoop, calls=%fused_computation.70 | loop fusion | flops 1048576 | bytes 6291472 | tf_op jit(solution)/shard_map/convert_element_type | solution.py:195
  104.4 4.1 %collective-permute-start.17 = (bf16[2560,128]{1,0:T(8,128)(2,1)S(1)}, bf16[2560,128]{1,0:T(8,128)(2,1)S(1)}, u32[]{:S(2)}, u32[]{:S(2)}) collective-permute-start(bf16[2560,128]{1,0:T(8,128)(2,1)S(1)} %pad_maximum_fusion.2), channel_id=1, source_target_pairs={{0,33},{1,32},{2,35},{3,34},{4,37},{5,36},{6,39},{7,38},{8,41},{9,... | collective-permute-start | bytes 1966088 | tf_op jit(solution)/shard_map/ppermute | solution.py:43
  111.2 4.6 %collective-permute-start.9 = (bf16[400,128]{0,1:T(8,128)(2,1)}, bf16[400,128]{0,1:T(8,128)(2,1)S(1)}, u32[]{:S(2)}, u32[]{:S(2)}) collective-permute-start(bf16[400,128]{0,1:T(8,128)(2,1)} %collective-permute-done.8), channel_id=1, source_target_pairs={{0,30},{1,31},{2,0},{3,1},{4,2},{5,3},{6,4},{7,5},{8,6},{9,7},{10,... | collective-permute-start | bytes 307208 | tf_op jit(solution)/shard_map/ppermute | solution.py:168
  119.6 4.6 %collective-permute-start.10 = (bf16[400,128]{0,1:T(8,128)(2,1)S(1)}, bf16[400,128]{0,1:T(8,128)(2,1)S(1)}, u32[]{:S(2)}, u32[]{:S(2)}) collective-permute-start(bf16[400,128]{0,1:T(8,128)(2,1)S(1)} %collective-permute-done.9), channel_id=1, source_target_pairs={{0,30},{1,31},{2,0},{3,1},{4,2},{5,3},{6,4},{7,5},{8,6},{9,7},{10,... | collective-permute-start | bytes 307208 | tf_op jit(solution)/shard_map/ppermute | solution.py:168
  127.0 4.6 %collective-permute-start.11 = (bf16[400,128]{0,1:T(8,128)(2,1)S(1)}, bf16[400,128]{0,1:T(8,128)(2,1)S(1)}, u32[]{:S(2)}, u32[]{:S(2)}) collective-permute-start(bf16[400,128]{0,1:T(8,128)(2,1)S(1)} %collective-permute-done.10), channel_id=1, source_target_pairs={{0,30},{1,31},{2,0},{3,1},{4,2},{5,3},{6,4},{7,5},{8,6},{9,7},{10,... | collective-permute-start | bytes 307208 | tf_op jit(solution)/shard_map/ppermute | solution.py:168
  133.9 4.6 %collective-permute-start.12 = (bf16[400,128]{0,1:T(8,128)(2,1)S(1)}, bf16[400,128]{0,1:T(8,128)(2,1)}, u32[]{:S(2)}, u32[]{:S(2)}) collective-permute-start(bf16[400,128]{0,1:T(8,128)(2,1)S(1)} %collective-permute-done.11), channel_id=1, source_target_pairs={{0,30},{1,31},{2,0},{3,1},{4,2},{5,3},{6,4},{7,5},{8,6},{9,7},{10,... | collective-permute-start | bytes 307208 | tf_op jit(solution)/shard_map/ppermute | solution.py:168
  140.8 4.7 %collective-permute-start.13 = (bf16[400,128]{0,1:T(8,128)(2,1)}, bf16[400,128]{0,1:T(8,128)(2,1)}, u32[]{:S(2)}, u32[]{:S(2)}) collective-permute-start(bf16[400,128]{0,1:T(8,128)(2,1)} %collective-permute-done.12), channel_id=1, source_target_pairs={{0,30},{1,31},{2,0},{3,1},{4,2},{5,3},{6,4},{7,5},{8,6},{9,7},{10,... | collective-permute-start | bytes 307208 | tf_op jit(solution)/shard_map/ppermute | solution.py:168
  149.4 7.0 %collective-permute-start.24 = (bf16[128,2048]{1,0:T(8,128)(2,1)}, bf16[128,2048]{1,0:T(8,128)(2,1)}, u32[]{:S(2)}, u32[]{:S(2)}) collective-permute-start(bf16[128,2048]{1,0:T(8,128)(2,1)} %fusion.29), channel_id=1, source_target_pairs={{0,1},{1,0},{2,3},{3,2},{4,5},{5,4},{6,7},{7,6},{8,9},{9,8},{10,11... | collective-permute-start | bytes 1572872 | tf_op jit(solution)/shard_map/ppermute | solution.py:43
  158.2 4.4 %collective-permute-start.25 = (bf16[128,2048]{1,0:T(8,128)(2,1)}, bf16[128,2048]{1,0:T(8,128)(2,1)}, u32[]{:S(2)}, u32[]{:S(2)}) collective-permute-start(bf16[128,2048]{1,0:T(8,128)(2,1)} %fusion.28), channel_id=1, source_target_pairs={{0,32},{1,33},{2,34},{3,35},{4,36},{5,37},{6,38},{7,39},{8,40},{9,... | collective-permute-start | bytes 1572872 | tf_op jit(solution)/shard_map/ppermute | solution.py:43
  162.6 4.9 %collective-permute-start.14 = (bf16[400,128]{0,1:T(8,128)(2,1)}, bf16[400,128]{0,1:T(8,128)(2,1)}, u32[]{:S(2)}, u32[]{:S(2)}) collective-permute-start(bf16[400,128]{0,1:T(8,128)(2,1)} %collective-permute-done.13), channel_id=1, source_target_pairs={{0,30},{1,31},{2,0},{3,1},{4,2},{5,3},{6,4},{7,5},{8,6},{9,7},{10,... | collective-permute-start | bytes 307208 | tf_op jit(solution)/shard_map/ppermute | solution.py:168
  175.6 4.2 %collective-permute-done.7 = bf16[400,128]{0,1:T(8,128)(2,1)S(1)} collective-permute-done((bf16[400,128]{0,1:T(8,128)(2,1)}, bf16[400,128]{0,1:T(8,128)(2,1)S(1)}, u32[]{:S(2)}, u32[]{:S(2)}) %collective-permute-start.7) | collective-permute-done | bytes 102432 | tf_op jit(solution)/shard_map/ppermute | solution.py:166
  197.5 4.6 %collective-permute-start.20 = (bf16[592,128]{0,1:T(8,128)(2,1)S(1)}, bf16[592,128]{0,1:T(8,128)(2,1)S(1)}, u32[]{:S(2)}, u32[]{:S(2)}) collective-permute-start(bf16[592,128]{0,1:T(8,128)(2,1)S(1)} %concatenate.171), channel_id=1, source_target_pairs={{0,33},{1,32},{2,35},{3,34},{4,37},{5,36},{6,39},{7,38},{8,41},{9,... | collective-permute-start | bytes 454664 | tf_op jit(solution)/shard_map/ppermute | solution.py:43
  209.1 3.6 %all-to-all-start = ((bf16[8,64,128]{2,1,0:T(8,128)(2,1)}), bf16[8,64,128]{2,1,0:T(8,128)(2,1)S(1)}, u32[]{:S(2)}, u32[]{:S(2)}) async-start(bf16[8,64,128]{2,1,0:T(8,128)(2,1)} %broadcast_in_dim.20), calls=%async_computation | async-start | bytes 262144 | tf_op jit(solution)/shard_map/all_to_all | solution.py:116
  213.8 4.7 %all-to-all-done = bf16[8,64,128]{2,1,0:T(8,128)(2,1)S(1)} async-done(((bf16[8,64,128]{2,1,0:T(8,128)(2,1)}), bf16[8,64,128]{2,1,0:T(8,128)(2,1)S(1)}, u32[]{:S(2)}, u32[]{:S(2)}) %all-to-all-start) | async-done | bytes 131104 | tf_op jit(solution)/shard_map/all_to_all | solution.py:116
  224.9 3.7 %collective-permute-start.28 = (bf16[256,128]{0,1:T(8,128)(2,1)S(1)}, bf16[256,128]{0,1:T(8,128)(2,1)S(1)}, u32[]{:S(2)}, u32[]{:S(2)}) collective-permute-start(bf16[256,128]{0,1:T(8,128)(2,1)S(1)} %get-tuple-element.49), channel_id=1, source_target_pairs={{0,32},{1,33},{2,34},{3,35},{4,36},{5,37},{6,38},{7,39},{8,40},{9,... | collective-permute-start | bytes 196616 | tf_op jit(solution)/shard_map/ppermute | solution.py:43
  232.0 4.0 %collective-permute-done.29 = bf16[256,128]{0,1:T(8,128)(2,1)S(1)} collective-permute-done((bf16[256,128]{0,1:T(8,128)(2,1)S(1)}, bf16[256,128]{0,1:T(8,128)(2,1)S(1)}, u32[]{:S(2)}, u32[]{:S(2)}) %collective-permute-start.29) | collective-permute-done | bytes 65568 | tf_op jit(solution)/shard_map/ppermute | solution.py:43
  238.2 8.3 %all_to_all.25 = bf16[8,40,128]{2,1,0:T(8,128)(2,1)S(1)} all-to-all(bf16[8,40,128]{2,1,0:T(8,128)(2,1)S(1)} %pad_maximum_fusion.3), channel_id=1, replica_groups={{0,1,2,3,4,5,6,7},{8,9,10,11,12,13,14,15},{16,17,18,19,20,21,22,23},{24..., dimensions={0} | all-to-all | bytes 163840 | tf_op jit(solution)/shard_map/all_to_all | solution.py:116
  246.6 22.9 %all_to_all.26 = bf16[8,32,128]{2,1,0:T(8,128)(2,1)S(1)} all-to-all(bf16[8,32,128]{2,1,0:T(8,128)(2,1)S(1)} %broadcast_in_dim.22), channel_id=1, replica_groups={{0,8,16,24,32,40,48,56},{1,9,17,25,33,41,49,57},{2,10,18,26,34,42,50,58..., dimensions={0} | all-to-all | bytes 131072 | tf_op jit(solution)/shard_map/all_to_all | solution.py:116
  270.2 5.4 %all-to-all-start.3 = ((bf16[8,32,128]{2,1,0:T(8,128)(2,1)}), bf16[8,32,128]{2,1,0:T(8,128)(2,1)S(1)}, u32[]{:S(2)}, u32[]{:S(2)}) async-start(bf16[8,32,128]{2,1,0:T(8,128)(2,1)} %broadcast_in_dim.23), calls=%async_computation.3 | async-start | bytes 131072 | tf_op jit(solution)/shard_map/all_to_all | solution.py:116
  275.7 5.0 %all-to-all-done.3 = bf16[8,32,128]{2,1,0:T(8,128)(2,1)S(1)} async-done(((bf16[8,32,128]{2,1,0:T(8,128)(2,1)}), bf16[8,32,128]{2,1,0:T(8,128)(2,1)S(1)}, u32[]{:S(2)}, u32[]{:S(2)}) %all-to-all-start.3) | async-done | bytes 65568 | tf_op jit(solution)/shard_map/all_to_all | solution.py:116
  280.9 12.6 %all_to_all.27 = bf16[8,200,128]{2,1,0:T(8,128)(2,1)S(1)} all-to-all(bf16[8,200,128]{2,1,0:T(8,128)(2,1)S(1)} %broadcast_in_dim.24), channel_id=1, replica_groups=mesh['dp'=8,'fsdp'=64] {'dp'}, dimensions={0} | all-to-all | bytes 819200 | tf_op jit(solution)/shard_map/all_to_all | solution.py:116
  (344 shorter events, 132.5 us)
Async XLA Ops:
  7.2 212.5 %all-gather.2.cloned.1.call-start = ((), (), s32[]{:S(2)}) async-start(), calls=%async_computation.5 | async-start | bytes 1114112 | tf_op jit(solution)/shard_map/all_gather | solution.py:162
  12.2 96.2 %collective-permute-start = (bf16[400,128]{0,1:T(8,128)(2,1)}, bf16[400,128]{0,1:T(8,128)(2,1)}, u32[]{:S(2)}, u32[]{:S(2)}) collective-permute-start(bf16[400,128]{0,1:T(8,128)(2,1)} %concatenate.149), channel_id=1, source_target_pairs={{0,2},{1,3},{2,4},{3,5},{4,6},{5,7},{6,8},{7,9},{8,10},{9,11},{10,... | collective-permute-start | bytes 307208 | tf_op jit(solution)/shard_map/ppermute | solution.py:166
  16.6 94.7 %collective-permute-start.8 = (bf16[400,128]{0,1:T(8,128)(2,1)}, bf16[400,128]{0,1:T(8,128)(2,1)}, u32[]{:S(2)}, u32[]{:S(2)}) collective-permute-start(bf16[400,128]{0,1:T(8,128)(2,1)} %concatenate.149), channel_id=1, source_target_pairs={{0,30},{1,31},{2,0},{3,1},{4,2},{5,3},{6,4},{7,5},{8,6},{9,7},{10,... | collective-permute-start | bytes 307208 | tf_op jit(solution)/shard_map/ppermute | solution.py:168
  48.3 101.1 %collective-permute-start.15 = (bf16[2560,128]{1,0:T(8,128)(2,1)}, bf16[2560,128]{1,0:T(8,128)(2,1)}, u32[]{:S(2)}, u32[]{:S(2)}) collective-permute-start(bf16[2560,128]{1,0:T(8,128)(2,1)} %pad_maximum_fusion), channel_id=1, source_target_pairs={{0,1},{1,0},{2,3},{3,2},{4,5},{5,4},{6,7},{7,6},{8,9},{9,8},{10,11... | collective-permute-start | bytes 1966088 | tf_op jit(solution)/shard_map/ppermute | solution.py:43
  55.9 106.6 %collective-permute-start.16 = (bf16[2560,128]{1,0:T(8,128)(2,1)}, bf16[2560,128]{1,0:T(8,128)(2,1)}, u32[]{:S(2)}, u32[]{:S(2)}) collective-permute-start(bf16[2560,128]{1,0:T(8,128)(2,1)} %pad_maximum_fusion.1), channel_id=1, source_target_pairs={{0,32},{1,33},{2,34},{3,35},{4,36},{5,37},{6,38},{7,39},{8,40},{9,... | collective-permute-start | bytes 1966088 | tf_op jit(solution)/shard_map/ppermute | solution.py:43
  60.6 32.7 %collective-permute-start.21 = (bf16[64,16]{0,1:T(8,128)(2,1)}, bf16[64,16]{0,1:T(8,128)(2,1)}, u32[]{:S(2)}, u32[]{:S(2)}) collective-permute-start(bf16[64,16]{0,1:T(8,128)(2,1)} %param.27), channel_id=1, source_target_pairs={{0,1},{1,0},{2,3},{3,2},{4,5},{5,4},{6,7},{7,6},{8,9},{9,8},{10,11... | collective-permute-start | bytes 6152 | tf_op jit(solution)/shard_map/ppermute | solution.py:43
  104.4 64.7 %collective-permute-start.17 = (bf16[2560,128]{1,0:T(8,128)(2,1)S(1)}, bf16[2560,128]{1,0:T(8,128)(2,1)S(1)}, u32[]{:S(2)}, u32[]{:S(2)}) collective-permute-start(bf16[2560,128]{1,0:T(8,128)(2,1)S(1)} %pad_maximum_fusion.2), channel_id=1, source_target_pairs={{0,33},{1,32},{2,35},{3,34},{4,37},{5,36},{6,39},{7,38},{8,41},{9,... | collective-permute-start | bytes 1966088 | tf_op jit(solution)/shard_map/ppermute | solution.py:43
  108.5 9.2 %collective-permute-start.1 = (bf16[400,128]{0,1:T(8,128)(2,1)}, bf16[400,128]{0,1:T(8,128)(2,1)S(1)}, u32[]{:S(2)}, u32[]{:S(2)}) collective-permute-start(bf16[400,128]{0,1:T(8,128)(2,1)} %collective-permute-done), channel_id=1, source_target_pairs={{0,2},{1,3},{2,4},{3,5},{4,6},{5,7},{6,8},{7,9},{8,10},{9,11},{10,... | collective-permute-start | bytes 307208 | tf_op jit(solution)/shard_map/ppermute | solution.py:166
  111.2 8.3 %collective-permute-start.9 = (bf16[400,128]{0,1:T(8,128)(2,1)}, bf16[400,128]{0,1:T(8,128)(2,1)S(1)}, u32[]{:S(2)}, u32[]{:S(2)}) collective-permute-start(bf16[400,128]{0,1:T(8,128)(2,1)} %collective-permute-done.8), channel_id=1, source_target_pairs={{0,30},{1,31},{2,0},{3,1},{4,2},{5,3},{6,4},{7,5},{8,6},{9,7},{10,... | collective-permute-start | bytes 307208 | tf_op jit(solution)/shard_map/ppermute | solution.py:168
  117.7 7.4 %collective-permute-start.2 = (bf16[400,128]{0,1:T(8,128)(2,1)S(1)}, bf16[400,128]{0,1:T(8,128)(2,1)S(1)}, u32[]{:S(2)}, u32[]{:S(2)}) collective-permute-start(bf16[400,128]{0,1:T(8,128)(2,1)S(1)} %collective-permute-done.1), channel_id=1, source_target_pairs={{0,2},{1,3},{2,4},{3,5},{4,6},{5,7},{6,8},{7,9},{8,10},{9,11},{10,... | collective-permute-start | bytes 307208 | tf_op jit(solution)/shard_map/ppermute | solution.py:166
  140.8 17.3 %collective-permute-start.13 = (bf16[400,128]{0,1:T(8,128)(2,1)}, bf16[400,128]{0,1:T(8,128)(2,1)}, u32[]{:S(2)}, u32[]{:S(2)}) collective-permute-start(bf16[400,128]{0,1:T(8,128)(2,1)} %collective-permute-done.12), channel_id=1, source_target_pairs={{0,30},{1,31},{2,0},{3,1},{4,2},{5,3},{6,4},{7,5},{8,6},{9,7},{10,... | collective-permute-start | bytes 307208 | tf_op jit(solution)/shard_map/ppermute | solution.py:168
  145.9 26.2 %collective-permute-start.6 = (bf16[400,128]{0,1:T(8,128)(2,1)}, bf16[400,128]{0,1:T(8,128)(2,1)}, u32[]{:S(2)}, u32[]{:S(2)}) collective-permute-start(bf16[400,128]{0,1:T(8,128)(2,1)} %collective-permute-done.5), channel_id=1, source_target_pairs={{0,2},{1,3},{2,4},{3,5},{4,6},{5,7},{6,8},{7,9},{8,10},{9,11},{10,... | collective-permute-start | bytes 307208 | tf_op jit(solution)/shard_map/ppermute | solution.py:166
  149.4 70.2 %collective-permute-start.24 = (bf16[128,2048]{1,0:T(8,128)(2,1)}, bf16[128,2048]{1,0:T(8,128)(2,1)}, u32[]{:S(2)}, u32[]{:S(2)}) collective-permute-start(bf16[128,2048]{1,0:T(8,128)(2,1)} %fusion.29), channel_id=1, source_target_pairs={{0,1},{1,0},{2,3},{3,2},{4,5},{5,4},{6,7},{7,6},{8,9},{9,8},{10,11... | collective-permute-start | bytes 1572872 | tf_op jit(solution)/shard_map/ppermute | solution.py:43
  158.2 61.5 %collective-permute-start.25 = (bf16[128,2048]{1,0:T(8,128)(2,1)}, bf16[128,2048]{1,0:T(8,128)(2,1)}, u32[]{:S(2)}, u32[]{:S(2)}) collective-permute-start(bf16[128,2048]{1,0:T(8,128)(2,1)} %fusion.28), channel_id=1, source_target_pairs={{0,32},{1,33},{2,34},{3,35},{4,36},{5,37},{6,38},{7,39},{8,40},{9,... | collective-permute-start | bytes 1572872 | tf_op jit(solution)/shard_map/ppermute | solution.py:43
  162.6 17.3 %collective-permute-start.14 = (bf16[400,128]{0,1:T(8,128)(2,1)}, bf16[400,128]{0,1:T(8,128)(2,1)}, u32[]{:S(2)}, u32[]{:S(2)}) collective-permute-start(bf16[400,128]{0,1:T(8,128)(2,1)} %collective-permute-done.13), channel_id=1, source_target_pairs={{0,30},{1,31},{2,0},{3,1},{4,2},{5,3},{6,4},{7,5},{8,6},{9,7},{10,... | collective-permute-start | bytes 307208 | tf_op jit(solution)/shard_map/ppermute | solution.py:168
  172.1 7.8 %collective-permute-start.7 = (bf16[400,128]{0,1:T(8,128)(2,1)}, bf16[400,128]{0,1:T(8,128)(2,1)S(1)}, u32[]{:S(2)}, u32[]{:S(2)}) collective-permute-start(bf16[400,128]{0,1:T(8,128)(2,1)} %collective-permute-done.6), channel_id=1, source_target_pairs={{0,2},{1,3},{2,4},{3,5},{4,6},{5,7},{6,8},{7,9},{8,10},{9,11},{10,... | collective-permute-start | bytes 307208 | tf_op jit(solution)/shard_map/ppermute | solution.py:166
  191.5 10.7 %collective-permute-start.18 = (bf16[592,128]{0,1:T(8,128)(2,1)S(1)}, bf16[592,128]{0,1:T(8,128)(2,1)S(1)}, u32[]{:S(2)}, u32[]{:S(2)}) collective-permute-start(bf16[592,128]{0,1:T(8,128)(2,1)S(1)} %concatenate.167), channel_id=1, source_target_pairs={{0,1},{1,0},{2,3},{3,2},{4,5},{5,4},{6,7},{7,6},{8,9},{9,8},{10,11... | collective-permute-start | bytes 454664 | tf_op jit(solution)/shard_map/ppermute | solution.py:43
  194.9 9.7 %collective-permute-start.19 = (bf16[592,128]{0,1:T(8,128)(2,1)S(1)}, bf16[592,128]{0,1:T(8,128)(2,1)S(1)}, u32[]{:S(2)}, u32[]{:S(2)}) collective-permute-start(bf16[592,128]{0,1:T(8,128)(2,1)S(1)} %concatenate.169), channel_id=1, source_target_pairs={{0,32},{1,33},{2,34},{3,35},{4,36},{5,37},{6,38},{7,39},{8,40},{9,... | collective-permute-start | bytes 454664 | tf_op jit(solution)/shard_map/ppermute | solution.py:43
  197.5 10.3 %collective-permute-start.20 = (bf16[592,128]{0,1:T(8,128)(2,1)S(1)}, bf16[592,128]{0,1:T(8,128)(2,1)S(1)}, u32[]{:S(2)}, u32[]{:S(2)}) collective-permute-start(bf16[592,128]{0,1:T(8,128)(2,1)S(1)} %concatenate.171), channel_id=1, source_target_pairs={{0,33},{1,32},{2,35},{3,34},{4,37},{5,36},{6,39},{7,38},{8,41},{9,... | collective-permute-start | bytes 454664 | tf_op jit(solution)/shard_map/ppermute | solution.py:43
  202.2 17.5 %collective-permute-start.26 = (bf16[128,2048]{1,0:T(8,128)(2,1)S(1)}, bf16[128,2048]{1,0:T(8,128)(2,1)S(1)}, u32[]{:S(2)}, u32[]{:S(2)}) collective-permute-start(bf16[128,2048]{1,0:T(8,128)(2,1)S(1)} %copy-done.13), channel_id=1, source_target_pairs={{0,33},{1,32},{2,35},{3,34},{4,37},{5,36},{6,39},{7,38},{8,41},{9,... | collective-permute-start | bytes 1572872 | tf_op jit(solution)/shard_map/ppermute | solution.py:43
  209.1 9.4 %all-to-all-start = ((bf16[8,64,128]{2,1,0:T(8,128)(2,1)}), bf16[8,64,128]{2,1,0:T(8,128)(2,1)S(1)}, u32[]{:S(2)}, u32[]{:S(2)}) async-start(bf16[8,64,128]{2,1,0:T(8,128)(2,1)} %broadcast_in_dim.20), calls=%async_computation | async-start | bytes 262144 | tf_op jit(solution)/shard_map/all_to_all | solution.py:116
  222.0 9.9 %collective-permute-start.27 = (bf16[256,128]{0,1:T(8,128)(2,1)S(1)}, bf16[256,128]{0,1:T(8,128)(2,1)S(1)}, u32[]{:S(2)}, u32[]{:S(2)}) collective-permute-start(bf16[256,128]{0,1:T(8,128)(2,1)S(1)} %get-tuple-element.47), channel_id=1, source_target_pairs={{0,1},{1,0},{2,3},{3,2},{4,5},{5,4},{6,7},{7,6},{8,9},{9,8},{10,11... | collective-permute-start | bytes 196616 | tf_op jit(solution)/shard_map/ppermute | solution.py:43
  228.6 7.4 %collective-permute-start.29 = (bf16[256,128]{0,1:T(8,128)(2,1)S(1)}, bf16[256,128]{0,1:T(8,128)(2,1)S(1)}, u32[]{:S(2)}, u32[]{:S(2)}) collective-permute-start(bf16[256,128]{0,1:T(8,128)(2,1)S(1)} %get-tuple-element.48), channel_id=1, source_target_pairs={{0,33},{1,32},{2,35},{3,34},{4,37},{5,36},{6,39},{7,38},{8,41},{9,... | collective-permute-start | bytes 196616 | tf_op jit(solution)/shard_map/ppermute | solution.py:43
  270.2 10.5 %all-to-all-start.3 = ((bf16[8,32,128]{2,1,0:T(8,128)(2,1)}), bf16[8,32,128]{2,1,0:T(8,128)(2,1)S(1)}, u32[]{:S(2)}, u32[]{:S(2)}) async-start(bf16[8,32,128]{2,1,0:T(8,128)(2,1)} %broadcast_in_dim.23), calls=%async_computation.3 | async-start | bytes 131072 | tf_op jit(solution)/shard_map/all_to_all | solution.py:116
  (62 other events, 855.1 us)
Sparse Core Ops, SparseCore 0:
  63.1 58.9 all-gather.1

commit v2 on v0

v2 whole, which is shorter than its diff:
```python
import math

import jax
import jax.numpy as jnp
import numpy as np
from jax import lax
from jax.experimental import pallas as pl
from jax.experimental.pallas import tpu as pltpu
from jax.sharding import PartitionSpec as P

GROUP = 8
EPS = 1e-05
ADAPTER_SCALE = 0.5
ROPE_BASE = 500000.0
MASKED = -1e30

NX, NZ, NC = 2, 16, 2
LENGTH, HEAD, RANK, KV = 256, 128, 64, 32
FEATURES = NX * NZ * NC * HEAD
STEPS = NZ // 2
BLOCKS = 2 * STEPS
PACKET = LENGTH + 2 * RANK + 16
PER_HEAD = 2 * LENGTH + 2 * KV
SHARED = LENGTH + 16

F32, BF16 = jnp.float32, jnp.bfloat16
VMEM = pl.BlockSpec(memory_space=pltpu.VMEM)
SMEM = pl.BlockSpec(memory_space=pltpu.SMEM)


def place(a, z, c):
    return a * (NZ * NC) + z * NC + c


NEAR_GROUPS = [[GROUP * g + i for i in range(GROUP)] for g in range(8)]
FAR_GROUPS = [
    [place(a, z + 4 * k, c) for a in range(NX) for k in range(4)] for z in range(4) for c in range(NC)
]
RING = [
    (place(a, z, c), place(a, (z + (1 if c == 0 else -1)) % NZ, c))
    for a in range(NX)
    for z in range(NZ)
    for c in range(NC)
]
LAST = [pair for pair in RING if pair[0] % NC == 1]
TO_MEMBER = [(GROUP * g + 2 * q + q % 2, GROUP * g + 4 + q) for g in range(8) for q in range(4)]


def swap(value, mask):
    return lax.ppermute(value, "fsdp", [(i, i ^ mask) for i in range(NX * NZ * NC)])


def exchange(value, axis, groups=None):
    return lax.all_to_all(value, axis, 0, 0, axis_index_groups=groups)


def after(value, *others):
    return lax.optimization_barrier((value, *others))[0]


def rope_tables():
    positions = np.arange(LENGTH, dtype=np.float32)[:, None]
    steps = np.arange(HEAD // 2, dtype=np.float32)
    frequency = np.exp(steps * np.float32(-2.0 * math.log(ROPE_BASE) / HEAD)).astype(np.float32)
    angles = positions * frequency[None, :]
    return np.cos(angles).astype(np.float32), np.sin(angles).astype(np.float32)


def contract(left_arr, right_arr, left_dim, right_dim):
    return lax.dot_general(
        left_arr,
        right_arr,
        (((left_dim,), (right_dim,)), ((), ())),
        preferred_element_type=F32,
    )


def two_terms(value):
    high = value.astype(BF16)
    return high, (value - high.astype(F32)).astype(BF16)


def call(body, outs, *operands, scratch=(), megabytes=32):
    specs = [SMEM if o.dtype == jnp.int32 and o.ndim == 1 else VMEM for o in operands]
    many = isinstance(outs, (list, tuple))
    return pl.pallas_call(
        body,
        out_shape=outs,
        in_specs=specs,
        out_specs=[VMEM] * len(outs) if many else VMEM,
        scratch_shapes=list(scratch),
        compiler_params=pltpu.CompilerParams(vmem_limit_bytes=megabytes << 20),
    )(*operands)


def shape(*dims, dtype=BF16):
    return jax.ShapeDtypeStruct(dims, dtype)


def diagonal(size):
    return lax.broadcasted_iota(jnp.int32, (size, size), 0) == lax.broadcasted_iota(
        jnp.int32, (size, size), 1
    )


def to_row(column):
    return jnp.sum(jnp.where(diagonal(128), column, 0.0), axis=0, keepdims=True)


def to_column(row):
    return jnp.sum(jnp.where(diagonal(128), row, 0.0), axis=1, keepdims=True)


def pack_kernel(hidden, gain, a_query, a_value, value_up, packet):
    values = hidden[...].astype(F32)
    packet[:LENGTH] = (values * gain[...].astype(F32)).astype(BF16)
    packet[LENGTH : LENGTH + RANK] = a_query[...]
    packet[LENGTH + RANK : LENGTH + 2 * RANK] = a_value[...]
    squares = jnp.sum(values * values, axis=1, keepdims=True)
    rows = jnp.concatenate([to_row(squares[:128]), to_row(squares[128:])], axis=0)
    high, low = two_terms(rows)
    base = LENGTH + 2 * RANK
    packet[base : base + 16] = jnp.concatenate([high, low, jnp.zeros((12, 128), BF16)], axis=0)
    columns = value_up[...].astype(F32).T
    columns = jnp.concatenate([columns, jnp.zeros((16, 128 - RANK), F32)], axis=1)
    packet[base + 16 : base + 32] = columns.astype(BF16)


def source_block(place_ref, slot, j):
    peer_x = place_ref[0] ^ (slot >> 1)
    peer_c = place_ref[2] ^ (slot & 1)
    hops = jnp.where(j < STEPS - 1, j + 1, peer_c * STEPS)
    z = (place_ref[1] + jnp.where(peer_c == 0, NZ - hops, hops)) % NZ
    return peer_x * (NZ * NC) + z * NC, peer_c


def projection_kernel(place_ref, wq, wq_scales, wkv, wkv_scales, *rest):
    outs, (q_levels, kv_levels) = rest[:4], rest[4:]
    q_levels[...] = wq_scales[...].astype(F32)
    kv_levels[...] = wkv_scales[...].astype(F32)
    for slot in range(4):
        out = outs[slot]

        def step(j, carry, slot=slot, out=out):
            chip, peer_c = source_block(place_ref, slot, j)
            q_both = q_levels[pl.ds(pl.multiple_of(chip * 4, 8), 8), :]
            kv_both = kv_levels[pl.ds(pl.multiple_of(chip * 4, 8), 8), :]
            for e in range(2):
                c = peer_c ^ e
                rows = pl.ds(pl.multiple_of((chip + c) * 128, 128), 128)
                level = jnp.where(c == 0, q_both[:4], q_both[4:])
                block = wq[rows, :].astype(F32).reshape(4, 32, 128) * level[:, None, :]
                to = pl.multiple_of((2 * j + e) * 128, 128)
                out[pl.ds(to, 128), :] = block.reshape(128, 128).astype(BF16)
                level = jnp.where(c == 0, kv_both[:4], kv_both[4:])
                block = wkv[rows, :].astype(F32).reshape(4, 32, KV) * level[:, None, :]
                to = pl.multiple_of(BLOCKS * 128 + (2 * j + e) * KV, KV)
                out[pl.ds(to, KV), :] = block.reshape(128, KV).T.astype(BF16)
            return carry

        lax.fori_loop(0, STEPS, step, 0)


def output_kernel(place_ref, wo, wo_scales, *outs):
    for slot in range(4):
        out = outs[slot]

        def step(j, carry, slot=slot, out=out):
            chip, peer_c = source_block(place_ref, slot, j)
            for e in range(2):
                columns = pl.ds(pl.multiple_of((chip + (peer_c ^ e)) * 128, 128), 128)
                level = wo_scales[:, columns].astype(F32)
                block = wo[:, columns].astype(F32).reshape(4, 32, 128) * level[:, None, :]
                to = pl.multiple_of((2 * j + e) * 128, 128)
                out[pl.ds(to, 128), :] = block.reshape(128, 128).astype(BF16)
            return carry

        lax.fori_loop(0, STEPS, step, 0)


def product_kernel(place_ref, *refs):
    pieces, grads = refs[: STEPS + 1], refs[STEPS + 1 : 2 * STEPS + 2]
    refs = refs[2 * STEPS + 2 :]
    projections, outputs, (kept, sent) = refs[:4], refs[4:8], refs[8:]
    first = place_ref[2] == 0
    base = LENGTH + 2 * RANK

    def pick(refs, start, rows):
        blocks = []
        for j in range(STEPS):
            for e in range(2):
                at = slice(e * refs[0].shape[0] // 2 + start, e * refs[0].shape[0] // 2 + start + rows)
                if j < STEPS - 1:
                    blocks.append(refs[j + 1][at])
                else:
                    blocks.append(jnp.where(first, refs[0][at], refs[STEPS][at]))
        return blocks

    inputs = jnp.concatenate(pick(pieces, 0, LENGTH), axis=1)
    downs = jnp.concatenate(pick(pieces, LENGTH, 2 * RANK), axis=1)
    squares = sum(
        b[0:2].astype(F32) + b[2:4].astype(F32) for b in pick(pieces, base, 16)
    )
    gradients = jnp.concatenate(pick(grads, 0, LENGTH), axis=1)
    low = contract(inputs, downs, 1, 1)
    kv_weights = jnp.concatenate(
        [
            jnp.concatenate(
                [p[BLOCKS * 128 + b * KV : BLOCKS * 128 + (b + 1) * KV, :] for b in range(BLOCKS)], axis=1
            )
            for p in projections
        ],
        axis=0,
    )
    kv = contract(kv_weights, inputs, 1, 1)
    for place_at, (out, cast) in enumerate(((kept, F32), (sent, BF16))):
        slots = (place_at, 2 + place_at)
        q_weights = jnp.concatenate([projections[s][: BLOCKS * 128, :] for s in slots], axis=1)
        q = contract(inputs, q_weights, 1, 0)
        o_weights = jnp.concatenate(
            [
                jnp.concatenate([outputs[s][b * 128 : (b + 1) * 128, :] for b in range(BLOCKS)], axis=1)
                for s in slots
            ],
            axis=0,
        )
        ctx = contract(gradients, o_weights, 1, 1)
        for i, s in enumerate(slots):
            at = i * PER_HEAD
            out[at : at + LENGTH] = q[:, i * 128 : (i + 1) * 128].astype(cast)
            out[at + LENGTH : at + 2 * LENGTH] = ctx[:, i * 128 : (i + 1) * 128].astype(cast)
            own = kv[s * KV : (s + 1) * KV]
            out[at + 2 * LENGTH : at + 2 * LENGTH + KV] = own[:, :128].astype(cast)
            out[at + 2 * LENGTH + KV : at + PER_HEAD] = own[:, 128:].astype(cast)
        at = 2 * PER_HEAD
        out[at : at + LENGTH] = low.astype(cast)
        high, rest = two_terms(squares)
        pad = jnp.zeros((12, 128), F32)
        out[at + LENGTH : at + SHARED] = jnp.concatenate(
            [high.astype(F32), rest.astype(F32), pad], axis=0
        ).astype(cast)


def middle_kernel(kept, got, keep, send):
    head, shared = kept[:PER_HEAD] + got[:PER_HEAD].astype(F32), 2 * PER_HEAD
    keep[:PER_HEAD] = head
    send[:PER_HEAD] = (kept[PER_HEAD:shared] + got[PER_HEAD:shared].astype(F32)).astype(BF16)
    low = kept[shared : shared + LENGTH] + got[shared : shared + LENGTH].astype(F32)
    keep[PER_HEAD : PER_HEAD + LENGTH] = low
    send[PER_HEAD : PER_HEAD + LENGTH] = low.astype(BF16)
    rows = kept[shared + LENGTH :] + got[shared + LENGTH :].astype(F32)
    squares = rows[0:2] + rows[2:4]
    high, rest = two_terms(squares)
    pad = jnp.zeros((12, 128), F32)
    rows = jnp.concatenate([high.astype(F32), rest.astype(F32), pad], axis=0)
    keep[PER_HEAD + LENGTH :] = rows
    send[PER_HEAD + LENGTH :] = rows.astype(BF16)


def turn(values, cosine, sine, axis):
    half = HEAD // 2
    if axis == 1:
        front, back = values[:, :half], values[:, half:]
    else:
        front, back = values[:half], values[half:]
    return jnp.concatenate([front * cosine - back * sine, back * cosine + front * sine], axis=axis)


def head_kernel(
    kept, got, hidden, gain, columns, own_columns, query_up, cosine, sine, queries, ctx, lows, normed, parcel
):
    total = kept[...] + got[...].astype(F32)
    q, grads = total[:LENGTH], total[LENGTH : 2 * LENGTH]
    kv = total[2 * LENGTH : PER_HEAD]
    low = total[PER_HEAD : PER_HEAD + LENGTH]
    squares = total[PER_HEAD + LENGTH : PER_HEAD + LENGTH + 2]
    squares = squares + total[PER_HEAD + LENGTH + 2 : PER_HEAD + LENGTH + 4]
    inverse = lax.rsqrt(squares * (1.0 / FEATURES) + EPS)
    column = jnp.concatenate([to_column(inverse[0:1]), to_column(inverse[1:2])], axis=0)
    normed[...] = (hidden[...].astype(F32) * column * gain[...].astype(F32)).astype(BF16)
    both = (low * column).astype(BF16)
    lows[...] = both
    ctx[...] = grads.astype(BF16)
    linear = q * column + ADAPTER_SCALE * contract(both[:, :RANK], query_up[...], 1, 0)
    queries[...] = turn(linear, cosine[...], sine[...], 1).astype(BF16)
    adapter = ADAPTER_SCALE * contract(columns[:, :RANK], both[:, RANK:], 1, 1)
    first = (kv[:KV] * inverse[0:1] + adapter[:, :128]).astype(BF16)
    second = (kv[KV:] * inverse[1:2] + adapter[:, 128:]).astype(BF16)
    mine = jnp.concatenate([first, second, own_columns[...]], axis=0)
    for i in range(GROUP):
        parcel[i] = mine


def attention_kernel(
    group, queries, ctx, lows, query_up, cosine, sine, cosine_t, sine_t, snapshot_row, snapshot_column, out, up
):
    def side(start):
        return jnp.concatenate(
            [
                jnp.concatenate([group[p, :KV, :], group[p, KV : 2 * KV, :]], axis=1)
                for p in range(start, start + 4)
            ],
            axis=0,
        )

    keys = turn(side(0).astype(F32), cosine_t[...], sine_t[...], 0).astype(BF16)
    values = side(4)
    value_up = jnp.concatenate([group[p, 2 * KV :, :] for p in range(GROUP)], axis=0)[:, :RANK]
    scale = HEAD ** (-0.5)
    scores = contract(queries[...], keys, 1, 0) * scale
    row = lax.broadcasted_iota(jnp.int32, (LENGTH, LENGTH), 0)
    column = lax.broadcasted_iota(jnp.int32, (LENGTH, LENGTH), 1)
    allowed = jnp.logical_and(column <= row, snapshot_column[...] == snapshot_row[...])
    scores = jnp.where(allowed, scores, MASKED)
    weights = jnp.exp(scores - jnp.max(scores, axis=1, keepdims=True))
    prob = weights / jnp.sum(weights, axis=1, keepdims=True)
    grads = ctx[...]
    grad_prob = contract(grads, values, 1, 0)
    grad_value = contract(prob.astype(BF16), grads, 0, 0).astype(BF16)
    inner = jnp.sum(prob * grad_prob, axis=1, keepdims=True)
    grad_score = (prob * (grad_prob - inner)).astype(BF16)
    grad_query = contract(grad_score, keys, 1, 1) * scale
    grad_linear = turn(grad_query, cosine[...], -sine[...], 1).astype(BF16)
    low_q, low_v = lows[:, :RANK], lows[:, RANK:]
    up[...] = ADAPTER_SCALE * contract(low_q, grad_linear, 0, 0)
    slices = ADAPTER_SCALE * contract(grad_value, low_v, 0, 0)
    slices = jnp.concatenate([slices, jnp.zeros((HEAD, 128 - RANK), F32)], axis=1).astype(BF16)
    grad_low = jnp.concatenate(
        [
            ADAPTER_SCALE * contract(grad_linear, query_up[...], 1, 1),
            ADAPTER_SCALE * contract(grad_value, value_up, 1, 0),
        ],
        axis=1,
    ).astype(BF16)
    rows = LENGTH // GROUP
    for i in range(GROUP):
        out[i, :rows, :] = grad_low[i * rows : (i + 1) * rows]
        out[i, rows:, :] = slices[16 * i : 16 * i + 16]


def near_kernel(parts, low, value):
    total = jnp.sum(parts[...].astype(F32), axis=0)
    rows = LENGTH // GROUP
    value[...] = total[rows:]
    for i in range(8):
        low[i] = total[:rows].astype(BF16)


def far_kernel(parts, low):
    total = jnp.sum(parts[...].astype(F32), axis=0).astype(BF16)
    for i in range(GROUP):
        low[i] = total


def rows_kernel(normed, low, up, value, out):
    whole = jnp.concatenate([low[i] for i in range(GROUP)], axis=0)
    rows = contract(normed[...], whole, 0, 0).astype(BF16)
    last = jnp.concatenate([up[...], value[...]], axis=0).astype(BF16)
    for i in range(8):
        out[i, :HEAD, :] = rows
        out[i, HEAD:, :] = last


def total_kernel(parts, grad_a_query, query_up, grad_a_value, value):
    total = jnp.sum(parts[...].astype(F32), axis=0)
    grad_a_query[...] = total[:HEAD, :RANK]
    grad_a_value[...] = total[:HEAD, RANK:]
    query_up[...] = total[HEAD : HEAD + RANK]
    value[...] = total[HEAD + RANK :, :RANK].T


def local(
    hidden_in,
    out_grad,
    snapshot_ids,
    norm_gain,
    wq_codes,
    wq_scales,
    wkv_codes,
    wkv_scales,
    wo_codes,
    wo_scales,
    a_query,
    query_up_weight,
    a_value,
    value_up_weight,
):
    head_index = lax.axis_index("fsdp")
    core = head_index % NC
    spot = jnp.stack([head_index // (NZ * NC), head_index // NC % NZ, core]).astype(jnp.int32)
    gain = norm_gain[None, :]

    packet = call(pack_kernel, shape(PACKET + 16, 128), hidden_in, gain, a_query, a_value, value_up_weight)
    other = swap(packet, 1)
    other_grad = swap(out_grad, 1)
    pieces = [jnp.concatenate([packet[:PACKET], other[:PACKET]], axis=0)]
    grads = [jnp.concatenate([out_grad, other_grad], axis=0)]
    for step in range(STEPS):
        pairs = RING if step < STEPS - 1 else LAST
        pieces.append(lax.ppermute(pieces[-1], "fsdp", pairs))
        grads.append(lax.ppermute(grads[-1], "fsdp", pairs))

    own_columns, other_columns = packet[PACKET:], other[PACKET:]
    chip_columns = jnp.where(
        core == 0,
        jnp.concatenate([own_columns, other_columns], axis=0),
        jnp.concatenate([other_columns, own_columns], axis=0),
    )
    columns = lax.ppermute(after(chip_columns, pieces[5]), "fsdp", TO_MEMBER)

    rows = BLOCKS * (128 + KV)
    projections = call(
        projection_kernel,
        [shape(rows, 128)] * 4,
        spot,
        after(wq_codes, packet),
        wq_scales,
        wkv_codes,
        wkv_scales,
        scratch=[pltpu.VMEM((256, 128), F32), pltpu.VMEM((256, KV), F32)],
    )
    outputs = call(
        output_kernel, [shape(BLOCKS * 128, 128)] * 4, spot, after(wo_codes, pieces[1]), wo_scales
    )
    masks = (1, NZ * NC, NZ * NC + 1)
    projections = [projections[0]] + [
        swap(after(projections[s], pieces[w]), masks[s - 1]) for s, w in ((1, 2), (2, 0), (3, 1))
    ]
    outputs = [outputs[0]] + [
        swap(after(outputs[s], pieces[w]), masks[s - 1]) for s, w in ((1, 5), (2, 3), (3, 4))
    ]

    rows = 2 * PER_HEAD + SHARED
    kept, sent = call(
        product_kernel,
        [shape(rows, 128, dtype=F32), shape(rows, 128)],
        spot,
        *pieces,
        *grads,
        *projections,
        *outputs,
        megabytes=48,
    )
    rows = PER_HEAD + SHARED
    kept, sent = call(middle_kernel, [shape(rows, 128, dtype=F32), shape(rows, 128)], kept, swap(sent, 1))
    got = swap(sent, NZ * NC)

    cosine, sine = rope_tables()
    square = shape(LENGTH, 128)
    queries, ctx, lows, normed, parcel = call(
        head_kernel,
        [square, square, square, square, shape(GROUP, 2 * KV + 16, 128)],
        kept,
        got,
        hidden_in,
        gain,
        columns,
        own_columns,
        query_up_weight,
        jnp.asarray(cosine),
        jnp.asarray(sine),
    )
    group = exchange(parcel, "fsdp", NEAR_GROUPS)
    slices, up = call(
        attention_kernel,
        [shape(GROUP, LENGTH // GROUP + 16, 128), shape(RANK, HEAD, dtype=F32)],
        group,
        queries,
        ctx,
        lows,
        query_up_weight,
        jnp.asarray(cosine),
        jnp.asarray(sine),
        jnp.asarray(cosine.T.copy()),
        jnp.asarray(sine.T.copy()),
        snapshot_ids,
        snapshot_ids.reshape(LENGTH, 1),
    )

    low, value = call(
        near_kernel,
        [shape(8, LENGTH // GROUP, 128), shape(16, 128, dtype=F32)],
        exchange(slices, "fsdp", NEAR_GROUPS),
    )
    low = call(far_kernel, shape(GROUP, LENGTH // GROUP, 128), exchange(low, "fsdp", FAR_GROUPS))
    mine = call(
        rows_kernel,
        shape(8, HEAD + RANK + 16, 128),
        normed,
        exchange(low, "fsdp", NEAR_GROUPS),
        up,
        value,
    )
    return tuple(
        call(
            total_kernel,
            [
                shape(HEAD, RANK, dtype=F32),
                shape(RANK, HEAD, dtype=F32),
                shape(HEAD, RANK, dtype=F32),
                shape(RANK, 16, dtype=F32),
            ],
            exchange(mine, "dp"),
        )
    )


def solution(mesh):
    in_specs = (
        P("dp", "fsdp"),
        P("dp", "fsdp"),
        P("dp", None),
        P("fsdp"),
        P(None, "fsdp"),
        P(None, "fsdp"),
        P(None, "fsdp"),
        P(None, "fsdp"),
        P("fsdp", None),
        P("fsdp", None),
        P(None, "fsdp"),
        P(None, "fsdp"),
        P(None, "fsdp"),
        P(None, "fsdp"),
    )
    out_specs = (P("fsdp", None), P(None, "fsdp"), P("fsdp", None), P(None, "fsdp"))
    return jax.shard_map(local, mesh=mesh, in_specs=in_specs, out_specs=out_specs, check_vma=False)
```

time: 841 us -> 210 us (0.25)
  the two profiles are of different devices: /device:TPU:32 before, /device:TPU:1 now
where the time goes in v2:
time: 210 us; the launch traced here: 209 us
  starting transfers between devices  99.2 us (47%)
  blocking collectives  53.6 us (26%)
  waiting for transfers between devices  28.4 us (14%)
  local copies, waits for them, and re-layouts  13 us (6%)
  Pallas kernels  13 us (6%)
    all_to_all x4, blocking collectives, exchange(): return lax.all_to_all(value, axis, 0, 0, axis_index_groups=groups)  53.6 us
    ppermute x10, starting transfers between devices, swap(): lax.ppermute(value, 'fsdp', [(i, i ^ mask) for i in range(NX * NZ * NC)])  35.7 us
    ppermute x8, starting transfers between devices, local(): pieces.append(lax.ppermute(pieces[-1], 'fsdp', pairs))  30.2 us
    ppermute x8, starting transfers between devices, local(): grads.append(lax.ppermute(grads[-1], 'fsdp', pairs))  26.7 us
    ppermute x10, waiting for transfers between devices, swap(): lax.ppermute(value, 'fsdp', [(i, i ^ mask) for i in range(NX * NZ * NC)])  15 us
    pallas_call x11, Pallas kernels, call(): pl.pallas_call(body, out_shape=outs, in_specs=specs, out_specs=[VMEM] * l...  13 us
    unnamed x46, local copies, waits for them, and re-layouts  10.7 us
    all_to_all x1, starting transfers between devices, exchange(): return lax.all_to_all(value, axis, 0, 0, axis_index_groups=groups)  5.85 us
  transfers between devices with their start and end apart: 28, of which 7 were waited for; matrix products, arithmetic and copies ran while one was open for 2% of the time, Pallas kernels for 3%

profile of v2, /device:TPU:1, one launch (start us, length us, event | category | flops | bytes accessed | tf_op | source)
XLA Modules:
  0.0 208.6 jit_solution(13992964205807630034)
XLA Ops:
  4.5 8.8 %collective-permute-start = (bf16[416,128]{1,0:T(8,128)(2,1)S(1)}, bf16[416,128]{1,0:T(8,128)(2,1)S(1)}, u32[]{:S(2)}, u32[]{:S(2)}) collective-permute-start(bf16[416,128]{1,0:T(8,128)(2,1)S(1)} %shard_map.201), channel_id=1, source_target_pairs={{0,1},{1,0},{2,3},{3,2},{4,5},{5,4},{6,7},{7,6},{8,9},{9,8},{10,11... | collective-permute-start | bytes 319496 | tf_op jit(solution)/shard_map/ppermute | solution.py:50
  15.9 5.7 %collective-permute-start.1 = (bf16[800,128]{1,0:T(8,128)(2,1)S(1)}, bf16[800,128]{1,0:T(8,128)(2,1)S(1)}, u32[]{:S(2)}, u32[]{:S(2)}) collective-permute-start(bf16[800,128]{1,0:T(8,128)(2,1)S(1)} %pad_maximum_fusion.refs_0_), channel_id=1, source_target_pairs={{0,2},{1,31},{2,4},{3,1},{4,6},{5,3},{6,8},{7,5},{8,10},{9,7},{10,... | collective-permute-start | bytes 614408 | tf_op jit(solution)/shard_map/ppermute | solution.py:400
  25.2 4.2 %collective-permute-start.2 = (bf16[800,128]{1,0:T(8,128)(2,1)S(1)}, bf16[800,128]{1,0:T(8,128)(2,1)S(1)}, u32[]{:S(2)}, u32[]{:S(2)}) collective-permute-start(bf16[800,128]{1,0:T(8,128)(2,1)S(1)} %collective-permute-done.1.refs_1_), channel_id=1, source_target_pairs={{0,2},{1,31},{2,4},{3,1},{4,6},{5,3},{6,8},{7,5},{8,10},{9,7},{10,... | collective-permute-start | bytes 614408 | tf_op jit(solution)/shard_map/ppermute | solution.py:400
  35.4 3.6 %collective-permute-start.12 = (bf16[512,128]{1,0:T(8,128)(2,1)S(1)}, bf16[512,128]{1,0:T(8,128)(2,1)}, u32[]{:S(2)}, u32[]{:S(2)}) collective-permute-start(bf16[512,128]{1,0:T(8,128)(2,1)S(1)} %collective-permute-done.11.refs_11_), channel_id=1, source_target_pairs={{0,2},{1,31},{2,4},{3,1},{4,6},{5,3},{6,8},{7,5},{8,10},{9,7},{10,... | collective-permute-start | bytes 393224 | tf_op jit(solution)/shard_map/ppermute | solution.py:401
  45.4 3.7 %shard_map.202 = (bf16[2560,128]{1,0:T(8,128)(2,1)S(1)}, bf16[2560,128]{1,0:T(8,128)(2,1)S(1)}, bf16[2560,128]{1,0:T(8,128)(2,1)S(1)}, bf16[2560,128]{1,0:T(8,128)(2,1)S(1)}) custom-call(s32[3]{0:T(128)S(1)} %pad_add_fusion.place_ref, bf16[8192,128]{1,0:T(8,128)(2,1)S(1)} %copy-done.1, bf16[256,128]{1,0:T(8,128)(2,1)S(1)} %copy-done.7, ...), custom_call_target="tpu_custom_call" | custom-call | tf_op jit(solution)/shard_map/pallas_call | solution.py:86
  49.2 4.7 %collective-permute-start.19 = (bf16[2560,128]{1,0:T(8,128)(2,1)S(1)}, bf16[2560,128]{1,0:T(8,128)(2,1)S(1)}, u32[]{:S(2)}, u32[]{:S(2)}) collective-permute-start(bf16[2560,128]{1,0:T(8,128)(2,1)S(1)} %get-tuple-element.39), channel_id=1, source_target_pairs={{0,32},{1,33},{2,34},{3,35},{4,36},{5,37},{6,38},{7,39},{8,40},{9,... | collective-permute-start | bytes 1966088 | tf_op jit(solution)/shard_map/ppermute | solution.py:50
  60.0 3.3 %collective-permute-start.14 = (bf16[512,128]{1,0:T(8,128)(2,1)S(1)}, bf16[512,128]{1,0:T(8,128)(2,1)S(1)}, u32[]{:S(2)}, u32[]{:S(2)}) collective-permute-start(bf16[512,128]{1,0:T(8,128)(2,1)S(1)} %collective-permute-done.13.refs_13_), channel_id=1, source_target_pairs={{0,2},{1,31},{2,4},{3,1},{4,6},{5,3},{6,8},{7,5},{8,10},{9,7},{10,... | collective-permute-start | bytes 393224 | tf_op jit(solution)/shard_map/ppermute | solution.py:401
  66.3 4.3 %collective-permute-start.15 = (bf16[512,128]{1,0:T(8,128)(2,1)S(1)}, bf16[512,128]{1,0:T(8,128)(2,1)S(1)}, u32[]{:S(2)}, u32[]{:S(2)}) collective-permute-start(bf16[512,128]{1,0:T(8,128)(2,1)S(1)} %collective-permute-done.14.refs_14_), channel_id=1, source_target_pairs={{0,2},{1,31},{2,4},{3,1},{4,6},{5,3},{6,8},{7,5},{8,10},{9,7},{10,... | collective-permute-start | bytes 393224 | tf_op jit(solution)/shard_map/ppermute | solution.py:401
  70.6 3.7 %collective-permute-start.5 = (bf16[800,128]{1,0:T(8,128)(2,1)S(1)}, bf16[800,128]{1,0:T(8,128)(2,1)S(1)}, u32[]{:S(2)}, u32[]{:S(2)}) collective-permute-start(bf16[800,128]{1,0:T(8,128)(2,1)S(1)} %collective-permute-done.4.refs_4_), channel_id=1, source_target_pairs={{0,2},{1,31},{2,4},{3,1},{4,6},{5,3},{6,8},{7,5},{8,10},{9,7},{10,... | collective-permute-start | bytes 614408 | tf_op jit(solution)/shard_map/ppermute | solution.py:400
  74.3 3.5 %collective-permute-start.16 = (bf16[512,128]{1,0:T(8,128)(2,1)S(1)}, bf16[512,128]{1,0:T(8,128)(2,1)S(1)}, u32[]{:S(2)}, u32[]{:S(2)}) collective-permute-start(bf16[512,128]{1,0:T(8,128)(2,1)S(1)} %collective-permute-done.15.refs_15_), channel_id=1, source_target_pairs={{0,2},{1,31},{2,4},{3,1},{4,6},{5,3},{6,8},{7,5},{8,10},{9,7},{10,... | collective-permute-start | bytes 393224 | tf_op jit(solution)/shard_map/ppermute | solution.py:401
  77.8 4.3 %collective-permute-start.18 = (bf16[2560,128]{1,0:T(8,128)(2,1)S(1)}, bf16[2560,128]{1,0:T(8,128)(2,1)S(1)}, u32[]{:S(2)}, u32[]{:S(2)}) collective-permute-start(bf16[2560,128]{1,0:T(8,128)(2,1)S(1)} %get-tuple-element.37), channel_id=1, source_target_pairs={{0,1},{1,0},{2,3},{3,2},{4,5},{5,4},{6,7},{7,6},{8,9},{9,8},{10,11... | collective-permute-start | bytes 1966088 | tf_op jit(solution)/shard_map/ppermute | solution.py:50
  82.1 4.4 %collective-permute-start.17 = (bf16[512,128]{1,0:T(8,128)(2,1)S(1)}, bf16[512,128]{1,0:T(8,128)(2,1)S(1)}, u32[]{:S(2)}, u32[]{:S(2)}) collective-permute-start(bf16[512,128]{1,0:T(8,128)(2,1)S(1)} %collective-permute-done.16.refs_16_), channel_id=1, source_target_pairs={{1,31},{3,1},{5,3},{7,5},{9,7},{11,9},{13,11},{15,13},{17,15},{19,... | collective-permute-start | bytes 393224 | tf_op jit(solution)/shard_map/ppermute | solution.py:401
  92.5 4.8 %collective-permute-start.23 = (bf16[2048,128]{1,0:T(8,128)(2,1)S(1)}, bf16[2048,128]{1,0:T(8,128)(2,1)S(1)}, u32[]{:S(2)}, u32[]{:S(2)}) collective-permute-start(bf16[2048,128]{1,0:T(8,128)(2,1)S(1)} %get-tuple-element.49), channel_id=1, source_target_pairs={{0,33},{1,32},{2,35},{3,34},{4,37},{5,36},{6,39},{7,38},{8,41},{9,... | collective-permute-start | bytes 1572872 | tf_op jit(solution)/shard_map/ppermute | solution.py:50
  99.5 4.7 %collective-permute-start.7 = (bf16[800,128]{1,0:T(8,128)(2,1)S(1)}, bf16[800,128]{1,0:T(8,128)(2,1)S(1)}, u32[]{:S(2)}, u32[]{:S(2)}) collective-permute-start(bf16[800,128]{1,0:T(8,128)(2,1)S(1)} %collective-permute-done.6.refs_6_), channel_id=1, source_target_pairs={{0,2},{1,31},{2,4},{3,1},{4,6},{5,3},{6,8},{7,5},{8,10},{9,7},{10,... | collective-permute-start | bytes 614408 | tf_op jit(solution)/shard_map/ppermute | solution.py:400
  106.8 5.3 %collective-permute-start.8 = (bf16[800,128]{1,0:T(8,128)(2,1)S(1)}, bf16[800,128]{1,0:T(8,128)(2,1)S(1)}, u32[]{:S(2)}, u32[]{:S(2)}) collective-permute-start(bf16[800,128]{1,0:T(8,128)(2,1)S(1)} %collective-permute-done.7.refs_7_), channel_id=1, source_target_pairs={{1,31},{3,1},{5,3},{7,5},{9,7},{11,9},{13,11},{15,13},{17,15},{19,... | collective-permute-start | bytes 614408 | tf_op jit(solution)/shard_map/ppermute | solution.py:400
  112.1 6.4 %collective-permute-done.23.refs_25_ = bf16[2048,128]{1,0:T(8,128)(2,1)S(1)} collective-permute-done((bf16[2048,128]{1,0:T(8,128)(2,1)S(1)}, bf16[2048,128]{1,0:T(8,128)(2,1)S(1)}, u32[]{:S(2)}, u32[]{:S(2)}) %collective-permute-start.23) | collective-permute-done | bytes 524320 | tf_op jit(solution)/shard_map/ppermute | solution.py:50
  118.7 4.3 %shard_map.204 = (f32[1424,128]{1,0:T(8,128)}, bf16[1424,128]{1,0:T(8,128)(2,1)S(1)}) custom-call(s32[3]{0:T(128)S(1)} %pad_add_fusion.place_ref, bf16[800,128]{1,0:T(8,128)(2,1)S(1)} %pad_maximum_fusion.refs_0_, bf16[800,128]{1,0:T(8,128)(2,1)S(1)} %collective-permute-done.1.refs_1_, bf16[800,128]{1,0:T(8,128)(2,1)S(1)} %collective-permute-done.2.refs_2_, ...), custom_call_target="tpu_custom_call" | custom-call | tf_op jit(solution)/shard_map/pallas_call | solution.py:86
  130.8 7.2 %collective-permute-done.25.got = bf16[848,128]{1,0:T(8,128)(2,1)S(1)} collective-permute-done((bf16[848,128]{1,0:T(8,128)(2,1)S(1)}, bf16[848,128]{1,0:T(8,128)(2,1)S(1)}, u32[]{:S(2)}, u32[]{:S(2)}) %collective-permute-start.25) | collective-permute-done | bytes 217120 | tf_op jit(solution)/shard_map/ppermute | solution.py:50
  139.1 5.8 %all-to-all-start = ((bf16[8,80,128]{2,1,0:T(8,128)(2,1)}), bf16[8,80,128]{2,1,0:T(8,128)(2,1)S(1)}, u32[]{:S(2)}, u32[]{:S(2)}) async-start(bf16[8,80,128]{2,1,0:T(8,128)(2,1)} %get-tuple-element.56), calls=%async_computation | async-start | bytes 327680 | tf_op jit(solution)/shard_map/all_to_all | solution.py:54
  145.1 5.8 %all-to-all-done.group = bf16[8,80,128]{2,1,0:T(8,128)(2,1)S(1)} async-done(((bf16[8,80,128]{2,1,0:T(8,128)(2,1)}), bf16[8,80,128]{2,1,0:T(8,128)(2,1)S(1)}, u32[]{:S(2)}, u32[]{:S(2)}) %all-to-all-start) | async-done | bytes 163872 | tf_op jit(solution)/shard_map/all_to_all | solution.py:54
  152.0 9.5 %all_to_all.25.parts = bf16[8,48,128]{2,1,0:T(8,128)(2,1)S(1)} all-to-all(bf16[8,48,128]{2,1,0:T(8,128)(2,1)S(1)} %get-tuple-element.60), channel_id=1, replica_groups={{0,1,2,3,4,5,6,7},{8,9,10,11,12,13,14,15},{16,17,18,19,20,21,22,23},{24..., dimensions={0} | all-to-all | bytes 196608 | tf_op jit(solution)/shard_map/all_to_all | solution.py:54
  161.5 21.8 %all_to_all.26.parts = bf16[8,32,128]{2,1,0:T(8,128)(2,1)S(1)} all-to-all(bf16[8,32,128]{2,1,0:T(8,128)(2,1)S(1)} %get-tuple-element.61), channel_id=1, replica_groups={{0,8,16,24,32,40,48,56},{1,9,17,25,33,41,49,57},{2,10,18,26,34,42,50,58..., dimensions={0} | all-to-all | bytes 131072 | tf_op jit(solution)/shard_map/all_to_all | solution.py:54
  183.2 9.6 %all_to_all.27.low = bf16[8,32,128]{2,1,0:T(8,128)(2,1)S(1)} all-to-all(bf16[8,32,128]{2,1,0:T(8,128)(2,1)S(1)} %shard_map.209), channel_id=1, replica_groups={{0,1,2,3,4,5,6,7},{8,9,10,11,12,13,14,15},{16,17,18,19,20,21,22,23},{24..., dimensions={0} | all-to-all | bytes 131072 | tf_op jit(solution)/shard_map/all_to_all | solution.py:54
  193.1 12.8 %all_to_all.28.parts = bf16[8,208,128]{2,1,0:T(8,128)(2,1)S(1)} all-to-all(bf16[8,208,128]{2,1,0:T(8,128)(2,1)S(1)} %shard_map.210), channel_id=1, replica_groups=mesh['dp'=8,'fsdp'=64] {'dp'}, dimensions={0} | all-to-all | bytes 851968 | tf_op jit(solution)/shard_map/all_to_all | solution.py:54
  (106 shorter events, 55.0 us)
Async XLA Ops:
  4.5 10.7 %collective-permute-start = (bf16[416,128]{1,0:T(8,128)(2,1)S(1)}, bf16[416,128]{1,0:T(8,128)(2,1)S(1)}, u32[]{:S(2)}, u32[]{:S(2)}) collective-permute-start(bf16[416,128]{1,0:T(8,128)(2,1)S(1)} %shard_map.201), channel_id=1, source_target_pairs={{0,1},{1,0},{2,3},{3,2},{4,5},{5,4},{6,7},{7,6},{8,9},{9,8},{10,11... | collective-permute-start | bytes 319496 | tf_op jit(solution)/shard_map/ppermute | solution.py:50
  13.3 9.2 %collective-permute-start.9 = (bf16[256,128]{1,0:T(8,128)(2,1)}, bf16[256,128]{1,0:T(8,128)(2,1)S(1)}, u32[]{:S(2)}, u32[]{:S(2)}) collective-permute-start(bf16[256,128]{1,0:T(8,128)(2,1)} %param.19), channel_id=1, source_target_pairs={{0,1},{1,0},{2,3},{3,2},{4,5},{5,4},{6,7},{7,6},{8,9},{9,8},{10,11... | collective-permute-start | bytes 196616 | tf_op jit(solution)/shard_map/ppermute | solution.py:50
  15.9 9.3 %collective-permute-start.1 = (bf16[800,128]{1,0:T(8,128)(2,1)S(1)}, bf16[800,128]{1,0:T(8,128)(2,1)S(1)}, u32[]{:S(2)}, u32[]{:S(2)}) collective-permute-start(bf16[800,128]{1,0:T(8,128)(2,1)S(1)} %pad_maximum_fusion.refs_0_), channel_id=1, source_target_pairs={{0,2},{1,31},{2,4},{3,1},{4,6},{5,3},{6,8},{7,5},{8,10},{9,7},{10,... | collective-permute-start | bytes 614408 | tf_op jit(solution)/shard_map/ppermute | solution.py:400
  22.5 6.8 %collective-permute-start.10 = (bf16[512,128]{1,0:T(8,128)(2,1)S(1)}, bf16[512,128]{1,0:T(8,128)(2,1)S(1)}, u32[]{:S(2)}, u32[]{:S(2)}) collective-permute-start(bf16[512,128]{1,0:T(8,128)(2,1)S(1)} %constant_dynamic-update-slice_fusion.refs_9_), channel_id=1, source_target_pairs={{0,2},{1,31},{2,4},{3,1},{4,6},{5,3},{6,8},{7,5},{8,10},{9,7},{10,... | collective-permute-start | bytes 393224 | tf_op jit(solution)/shard_map/ppermute | solution.py:401
  25.2 13.9 %collective-permute-start.2 = (bf16[800,128]{1,0:T(8,128)(2,1)S(1)}, bf16[800,128]{1,0:T(8,128)(2,1)S(1)}, u32[]{:S(2)}, u32[]{:S(2)}) collective-permute-start(bf16[800,128]{1,0:T(8,128)(2,1)S(1)} %collective-permute-done.1.refs_1_), channel_id=1, source_target_pairs={{0,2},{1,31},{2,4},{3,1},{4,6},{5,3},{6,8},{7,5},{8,10},{9,7},{10,... | collective-permute-start | bytes 614408 | tf_op jit(solution)/shard_map/ppermute | solution.py:400
  35.4 18.4 %collective-permute-start.12 = (bf16[512,128]{1,0:T(8,128)(2,1)S(1)}, bf16[512,128]{1,0:T(8,128)(2,1)}, u32[]{:S(2)}, u32[]{:S(2)}) collective-permute-start(bf16[512,128]{1,0:T(8,128)(2,1)S(1)} %collective-permute-done.11.refs_11_), channel_id=1, source_target_pairs={{0,2},{1,31},{2,4},{3,1},{4,6},{5,3},{6,8},{7,5},{8,10},{9,7},{10,... | collective-permute-start | bytes 393224 | tf_op jit(solution)/shard_map/ppermute | solution.py:401
  39.0 24.4 %collective-permute-start.3 = (bf16[800,128]{1,0:T(8,128)(2,1)S(1)}, bf16[800,128]{1,0:T(8,128)(2,1)S(1)}, u32[]{:S(2)}, u32[]{:S(2)}) collective-permute-start(bf16[800,128]{1,0:T(8,128)(2,1)S(1)} %collective-permute-done.2.refs_2_), channel_id=1, source_target_pairs={{0,2},{1,31},{2,4},{3,1},{4,6},{5,3},{6,8},{7,5},{8,10},{9,7},{10,... | collective-permute-start | bytes 614408 | tf_op jit(solution)/shard_map/ppermute | solution.py:400
  49.2 41.1 %collective-permute-start.19 = (bf16[2560,128]{1,0:T(8,128)(2,1)S(1)}, bf16[2560,128]{1,0:T(8,128)(2,1)S(1)}, u32[]{:S(2)}, u32[]{:S(2)}) collective-permute-start(bf16[2560,128]{1,0:T(8,128)(2,1)S(1)} %get-tuple-element.39), channel_id=1, source_target_pairs={{0,32},{1,33},{2,34},{3,35},{4,36},{5,37},{6,38},{7,39},{8,40},{9,... | collective-permute-start | bytes 1966088 | tf_op jit(solution)/shard_map/ppermute | solution.py:50
  56.0 36.5 %collective-permute-start.20 = (bf16[2560,128]{1,0:T(8,128)(2,1)S(1)}, bf16[2560,128]{1,0:T(8,128)(2,1)S(1)}, u32[]{:S(2)}, u32[]{:S(2)}) collective-permute-start(bf16[2560,128]{1,0:T(8,128)(2,1)S(1)} %get-tuple-element.41), channel_id=1, source_target_pairs={{0,33},{1,32},{2,35},{3,34},{4,37},{5,36},{6,39},{7,38},{8,41},{9,... | collective-permute-start | bytes 1966088 | tf_op jit(solution)/shard_map/ppermute | solution.py:50
  60.0 6.2 %collective-permute-start.14 = (bf16[512,128]{1,0:T(8,128)(2,1)S(1)}, bf16[512,128]{1,0:T(8,128)(2,1)S(1)}, u32[]{:S(2)}, u32[]{:S(2)}) collective-permute-start(bf16[512,128]{1,0:T(8,128)(2,1)S(1)} %collective-permute-done.13.refs_13_), channel_id=1, source_target_pairs={{0,2},{1,31},{2,4},{3,1},{4,6},{5,3},{6,8},{7,5},{8,10},{9,7},{10,... | collective-permute-start | bytes 393224 | tf_op jit(solution)/shard_map/ppermute | solution.py:401
  63.4 7.2 %collective-permute-start.4 = (bf16[800,128]{1,0:T(8,128)(2,1)S(1)}, bf16[800,128]{1,0:T(8,128)(2,1)S(1)}, u32[]{:S(2)}, u32[]{:S(2)}) collective-permute-start(bf16[800,128]{1,0:T(8,128)(2,1)S(1)} %collective-permute-done.3.refs_3_), channel_id=1, source_target_pairs={{0,2},{1,31},{2,4},{3,1},{4,6},{5,3},{6,8},{7,5},{8,10},{9,7},{10,... | collective-permute-start | bytes 614408 | tf_op jit(solution)/shard_map/ppermute | solution.py:400
  66.3 8.0 %collective-permute-start.15 = (bf16[512,128]{1,0:T(8,128)(2,1)S(1)}, bf16[512,128]{1,0:T(8,128)(2,1)S(1)}, u32[]{:S(2)}, u32[]{:S(2)}) collective-permute-start(bf16[512,128]{1,0:T(8,128)(2,1)S(1)} %collective-permute-done.14.refs_14_), channel_id=1, source_target_pairs={{0,2},{1,31},{2,4},{3,1},{4,6},{5,3},{6,8},{7,5},{8,10},{9,7},{10,... | collective-permute-start | bytes 393224 | tf_op jit(solution)/shard_map/ppermute | solution.py:401
  70.6 15.9 %collective-permute-start.5 = (bf16[800,128]{1,0:T(8,128)(2,1)S(1)}, bf16[800,128]{1,0:T(8,128)(2,1)S(1)}, u32[]{:S(2)}, u32[]{:S(2)}) collective-permute-start(bf16[800,128]{1,0:T(8,128)(2,1)S(1)} %collective-permute-done.4.refs_4_), channel_id=1, source_target_pairs={{0,2},{1,31},{2,4},{3,1},{4,6},{5,3},{6,8},{7,5},{8,10},{9,7},{10,... | collective-permute-start | bytes 614408 | tf_op jit(solution)/shard_map/ppermute | solution.py:400
  74.3 7.8 %collective-permute-start.16 = (bf16[512,128]{1,0:T(8,128)(2,1)S(1)}, bf16[512,128]{1,0:T(8,128)(2,1)S(1)}, u32[]{:S(2)}, u32[]{:S(2)}) collective-permute-start(bf16[512,128]{1,0:T(8,128)(2,1)S(1)} %collective-permute-done.15.refs_15_), channel_id=1, source_target_pairs={{0,2},{1,31},{2,4},{3,1},{4,6},{5,3},{6,8},{7,5},{8,10},{9,7},{10,... | collective-permute-start | bytes 393224 | tf_op jit(solution)/shard_map/ppermute | solution.py:401
  77.8 34.3 %collective-permute-start.18 = (bf16[2560,128]{1,0:T(8,128)(2,1)S(1)}, bf16[2560,128]{1,0:T(8,128)(2,1)S(1)}, u32[]{:S(2)}, u32[]{:S(2)}) collective-permute-start(bf16[2560,128]{1,0:T(8,128)(2,1)S(1)} %get-tuple-element.37), channel_id=1, source_target_pairs={{0,1},{1,0},{2,3},{3,2},{4,5},{5,4},{6,7},{7,6},{8,9},{9,8},{10,11... | collective-permute-start | bytes 1966088 | tf_op jit(solution)/shard_map/ppermute | solution.py:50
  82.1 15.2 %collective-permute-start.17 = (bf16[512,128]{1,0:T(8,128)(2,1)S(1)}, bf16[512,128]{1,0:T(8,128)(2,1)S(1)}, u32[]{:S(2)}, u32[]{:S(2)}) collective-permute-start(bf16[512,128]{1,0:T(8,128)(2,1)S(1)} %collective-permute-done.16.refs_16_), channel_id=1, source_target_pairs={{1,31},{3,1},{5,3},{7,5},{9,7},{11,9},{13,11},{15,13},{17,15},{19,... | collective-permute-start | bytes 393224 | tf_op jit(solution)/shard_map/ppermute | solution.py:401
  86.6 12.9 %collective-permute-start.6 = (bf16[800,128]{1,0:T(8,128)(2,1)S(1)}, bf16[800,128]{1,0:T(8,128)(2,1)S(1)}, u32[]{:S(2)}, u32[]{:S(2)}) collective-permute-start(bf16[800,128]{1,0:T(8,128)(2,1)S(1)} %collective-permute-done.5.refs_5_), channel_id=1, source_target_pairs={{0,2},{1,31},{2,4},{3,1},{4,6},{5,3},{6,8},{7,5},{8,10},{9,7},{10,... | collective-permute-start | bytes 614408 | tf_op jit(solution)/shard_map/ppermute | solution.py:400
  90.3 21.8 %collective-permute-start.22 = (bf16[2048,128]{1,0:T(8,128)(2,1)S(1)}, bf16[2048,128]{1,0:T(8,128)(2,1)S(1)}, u32[]{:S(2)}, u32[]{:S(2)}) collective-permute-start(bf16[2048,128]{1,0:T(8,128)(2,1)S(1)} %get-tuple-element.47), channel_id=1, source_target_pairs={{0,32},{1,33},{2,34},{3,35},{4,36},{5,37},{6,38},{7,39},{8,40},{9,... | collective-permute-start | bytes 1572872 | tf_op jit(solution)/shard_map/ppermute | solution.py:50
  92.5 26.1 %collective-permute-start.23 = (bf16[2048,128]{1,0:T(8,128)(2,1)S(1)}, bf16[2048,128]{1,0:T(8,128)(2,1)S(1)}, u32[]{:S(2)}, u32[]{:S(2)}) collective-permute-start(bf16[2048,128]{1,0:T(8,128)(2,1)S(1)} %get-tuple-element.49), channel_id=1, source_target_pairs={{0,33},{1,32},{2,35},{3,34},{4,37},{5,36},{6,39},{7,38},{8,41},{9,... | collective-permute-start | bytes 1572872 | tf_op jit(solution)/shard_map/ppermute | solution.py:50
  97.3 21.3 %collective-permute-start.21 = (bf16[2048,128]{1,0:T(8,128)(2,1)S(1)}, bf16[2048,128]{1,0:T(8,128)(2,1)S(1)}, u32[]{:S(2)}, u32[]{:S(2)}) collective-permute-start(bf16[2048,128]{1,0:T(8,128)(2,1)S(1)} %get-tuple-element.45), channel_id=1, source_target_pairs={{0,1},{1,0},{2,3},{3,2},{4,5},{5,4},{6,7},{7,6},{8,9},{9,8},{10,11... | collective-permute-start | bytes 1572872 | tf_op jit(solution)/shard_map/ppermute | solution.py:50
  99.5 7.3 %collective-permute-start.7 = (bf16[800,128]{1,0:T(8,128)(2,1)S(1)}, bf16[800,128]{1,0:T(8,128)(2,1)S(1)}, u32[]{:S(2)}, u32[]{:S(2)}) collective-permute-start(bf16[800,128]{1,0:T(8,128)(2,1)S(1)} %collective-permute-done.6.refs_6_), channel_id=1, source_target_pairs={{0,2},{1,31},{2,4},{3,1},{4,6},{5,3},{6,8},{7,5},{8,10},{9,7},{10,... | collective-permute-start | bytes 614408 | tf_op jit(solution)/shard_map/ppermute | solution.py:400
  106.8 11.8 %collective-permute-start.8 = (bf16[800,128]{1,0:T(8,128)(2,1)S(1)}, bf16[800,128]{1,0:T(8,128)(2,1)S(1)}, u32[]{:S(2)}, u32[]{:S(2)}) collective-permute-start(bf16[800,128]{1,0:T(8,128)(2,1)S(1)} %collective-permute-done.7.refs_7_), channel_id=1, source_target_pairs={{1,31},{3,1},{5,3},{7,5},{9,7},{11,9},{13,11},{15,13},{17,15},{19,... | collective-permute-start | bytes 614408 | tf_op jit(solution)/shard_map/ppermute | solution.py:400
  127.9 10.0 %collective-permute-start.25 = (bf16[848,128]{1,0:T(8,128)(2,1)S(1)}, bf16[848,128]{1,0:T(8,128)(2,1)S(1)}, u32[]{:S(2)}, u32[]{:S(2)}) collective-permute-start(bf16[848,128]{1,0:T(8,128)(2,1)S(1)} %get-tuple-element.53), channel_id=1, source_target_pairs={{0,32},{1,33},{2,34},{3,35},{4,36},{5,37},{6,38},{7,39},{8,40},{9,... | collective-permute-start | bytes 651272 | tf_op jit(solution)/shard_map/ppermute | solution.py:50
  139.1 11.8 %all-to-all-start = ((bf16[8,80,128]{2,1,0:T(8,128)(2,1)}), bf16[8,80,128]{2,1,0:T(8,128)(2,1)S(1)}, u32[]{:S(2)}, u32[]{:S(2)}) async-start(bf16[8,80,128]{2,1,0:T(8,128)(2,1)} %get-tuple-element.56), calls=%async_computation | async-start | bytes 327680 | tf_op jit(solution)/shard_map/all_to_all | solution.py:54
  (26 other events, 404.1 us)

commit v3 on v2

v3 whole, which is shorter than its diff:
```python
import math

import jax
import jax.numpy as jnp
import numpy as np
from jax import lax
from jax.experimental import pallas as pl
from jax.experimental.pallas import tpu as pltpu
from jax.sharding import PartitionSpec as P

GROUP = 8
EPS = 1e-05
ADAPTER_SCALE = 0.5
ROPE_BASE = 500000.0
MASKED = -1e30

NX, NZ, NC = 2, 16, 2
LENGTH, HEAD, RANK, KV = 256, 128, 64, 32
FEATURES = NX * NZ * NC * HEAD
BLOCKS = NZ
DOWNS_AT = LENGTH
SQUARES_AT = DOWNS_AT + 2 * RANK
COLUMNS_AT = SQUARES_AT + 16
GRADS_AT = COLUMNS_AT + 16
PACKET = GRADS_AT + LENGTH
PER_HEAD = 2 * LENGTH
SHARED = LENGTH + 16

F32, BF16 = jnp.float32, jnp.bfloat16
VMEM = pl.BlockSpec(memory_space=pltpu.VMEM)
SMEM = pl.BlockSpec(memory_space=pltpu.SMEM)


def place(a, z, c):
    return a * (NZ * NC) + z * NC + c


Z_GROUPS = [[place(a, z, c) for z in range(NZ)] for a in range(NX) for c in range(NC)]
BOX_GROUPS = [
    [place(a, 4 * b + i, c) for a in range(NX) for i in range(4) for c in range(NC)] for b in range(4)
]
NEAR_GROUPS = [[GROUP * g + i for i in range(GROUP)] for g in range(8)]
FAR_GROUPS = [
    [place(a, z + 4 * k, c) for a in range(NX) for k in range(4)] for z in range(4) for c in range(NC)
]


def swap(value, mask):
    return lax.ppermute(value, "fsdp", [(i, i ^ mask) for i in range(NX * NZ * NC)])


def swap_weights(value, mask):
    if mask < NZ * NC:
        return swap(value, mask)
    size = NX * NZ * NC
    rows = lax.axis_size("dp")
    pairs = [(d * size + i, (d ^ 1) * size + (i ^ mask)) for d in range(rows) for i in range(size)]
    return lax.ppermute(value, ("dp", "fsdp"), pairs)


def exchange(value, axis, groups=None):
    return lax.all_to_all(value, axis, 0, 0, axis_index_groups=groups)


def after(value, *others):
    return lax.optimization_barrier((value, *others))[0]


def rope_tables():
    positions = np.arange(LENGTH, dtype=np.float32)[:, None]
    steps = np.arange(HEAD // 2, dtype=np.float32)
    frequency = np.exp(steps * np.float32(-2.0 * math.log(ROPE_BASE) / HEAD)).astype(np.float32)
    angles = positions * frequency[None, :]
    return np.cos(angles).astype(np.float32), np.sin(angles).astype(np.float32)


def contract(left_arr, right_arr, left_dim, right_dim):
    return lax.dot_general(
        left_arr,
        right_arr,
        (((left_dim,), (right_dim,)), ((), ())),
        preferred_element_type=F32,
    )


def two_terms(value):
    high = value.astype(BF16)
    return high, (value - high.astype(F32)).astype(BF16)


def call(body, outs, *operands, scratch=(), megabytes=32, held=False):
    specs = [SMEM if o.dtype == jnp.int32 and o.ndim == 1 else VMEM for o in operands]
    if held:
        specs = [spec if spec is SMEM else pl.BlockSpec(memory_space=pl.ANY) for spec in specs]
    many = isinstance(outs, (list, tuple))
    return pl.pallas_call(
        body,
        out_shape=outs,
        in_specs=specs,
        out_specs=[VMEM] * len(outs) if many else VMEM,
        scratch_shapes=list(scratch),
        compiler_params=pltpu.CompilerParams(vmem_limit_bytes=megabytes << 20),
    )(*operands)


def shape(*dims, dtype=BF16):
    return jax.ShapeDtypeStruct(dims, dtype)


def diagonal(size):
    return lax.broadcasted_iota(jnp.int32, (size, size), 0) == lax.broadcasted_iota(
        jnp.int32, (size, size), 1
    )


def to_row(column):
    return jnp.sum(jnp.where(diagonal(128), column, 0.0), axis=0, keepdims=True)


def to_column(row):
    return jnp.sum(jnp.where(diagonal(128), row, 0.0), axis=1, keepdims=True)


def fetch(sources, targets, sems):
    copies = [pltpu.make_async_copy(a, b, sems.at[i]) for i, (a, b) in enumerate(zip(sources, targets))]
    for copy in copies:
        copy.start()
    for copy in copies:
        copy.wait()


def pack_kernel(
    hidden_at, gain_at, a_query_at, a_value_at, value_up_at, grad_at, packet, hidden, gain, value_up, sems
):
    fetch(
        (hidden_at, gain_at, value_up_at, a_query_at, a_value_at, grad_at),
        (
            hidden,
            gain,
            value_up,
            packet.at[pl.ds(DOWNS_AT, RANK)],
            packet.at[pl.ds(DOWNS_AT + RANK, RANK)],
            packet.at[pl.ds(GRADS_AT, LENGTH)],
        ),
        sems,
    )
    values = hidden[...].astype(F32)
    packet[:LENGTH] = (values * gain[...].astype(F32)).astype(BF16)
    squares = jnp.sum(values * values, axis=1, keepdims=True)
    rows = jnp.concatenate([to_row(squares[:128]), to_row(squares[128:])], axis=0)
    high, low = two_terms(rows)
    packet[SQUARES_AT:COLUMNS_AT] = jnp.concatenate([high, low, jnp.zeros((12, 128), BF16)], axis=0)
    packet[COLUMNS_AT:GRADS_AT] = jnp.concatenate(
        [value_up[...], jnp.zeros((16, 128 - RANK), BF16)], axis=1
    )


def peer_block(place_ref, slot, j):
    peer_x = place_ref[0] ^ (slot >> 1)
    peer_c = place_ref[2] ^ (slot & 1)
    return peer_x * (NZ * NC) + j * NC + peer_c, peer_c


def projection_kernel(place_ref, *rest):
    sources, outs, held = rest[:4], rest[4:8], rest[8:12]
    q_levels, kv_levels, sems = rest[12:]
    fetch(sources, held, sems)
    wq, wq_scales, wkv, wkv_scales = held
    q_levels[...] = wq_scales[...].astype(F32)
    widen = lax.broadcasted_iota(jnp.int32, (32, 1024), 1) // 32 == lax.broadcasted_iota(
        jnp.int32, (32, 1024), 0
    )
    widen = jnp.where(widen, 1.0, 0.0).astype(BF16)
    for i in range(8):
        level = contract(wkv_scales[:, 32 * i : 32 * i + 32], widen, 1, 0)
        kv_levels[:, 1024 * i : 1024 * i + 1024] = level
    for slot in range(4):
        out = outs[slot]

        def step(j, carry, slot=slot, out=out):
            block, peer_c = peer_block(place_ref, slot, j)
            rows = pl.ds(pl.multiple_of(block * 128, 128), 128)
            both = q_levels[pl.ds(pl.multiple_of((block - peer_c) * 4, 8), 8), :]
            level = jnp.where(peer_c == 0, both[:4], both[4:])
            codes = wq[rows, :].astype(F32).reshape(4, 32, 128) * level[:, None, :]
            to = pl.multiple_of(j * 128, 128)
            out[pl.ds(to, 128), :] = codes.reshape(128, 128).astype(BF16)
            codes = wkv[:, rows].astype(F32) * kv_levels[:, rows]
            to = pl.multiple_of(BLOCKS * 128 + j * KV, KV)
            out[pl.ds(to, KV), :] = codes.astype(BF16)
            return carry

        lax.fori_loop(0, BLOCKS, step, 0, unroll=2)


def output_kernel(place_ref, *rest):
    sources, outs, (wo, wo_scales, sems) = rest[:2], rest[2:6], rest[6:]
    fetch(sources, (wo, wo_scales), sems)
    for slot in range(4):
        out = outs[slot]

        def step(j, carry, slot=slot, out=out):
            block, _ = peer_block(place_ref, slot, j)
            columns = pl.ds(pl.multiple_of(block * 128, 128), 128)
            level = wo_scales[:, columns].astype(F32)
            codes = wo[:, columns].astype(F32).reshape(4, 32, 128) * level[:, None, :]
            to = pl.multiple_of(j * 128, 128)
            out[pl.ds(to, 128), :] = codes.reshape(128, 128).astype(BF16)
            return carry

        lax.fori_loop(0, BLOCKS, step, 0, unroll=2)


def product_kernel(place_ref, gathered, *refs):
    weights, outputs, (kept, sent, box) = refs[:4], refs[4:8], refs[8:]
    inputs = gathered[:LENGTH]
    low = contract(inputs, gathered[DOWNS_AT:SQUARES_AT], 1, 1)
    squares = sum(
        gathered[SQUARES_AT : SQUARES_AT + 16, b * 128 : (b + 1) * 128].astype(F32) for b in range(BLOCKS)
    )
    squares = squares[0:2] + squares[2:4]
    kv_weights = jnp.concatenate(
        [
            jnp.concatenate(
                [w[BLOCKS * 128 + b * KV : BLOCKS * 128 + (b + 1) * KV, :] for b in range(BLOCKS)], axis=1
            )
            for w in weights
        ],
        axis=0,
    )
    kv = contract(kv_weights, inputs, 1, 1).astype(BF16)
    at_zero, first = place_ref[0] == 0, place_ref[2] == 0
    for a in range(NX):
        mine = at_zero if a == 0 else jnp.logical_not(at_zero)
        near = jnp.where(mine, kv[: 2 * KV], kv[2 * KV :])
        low_core = jnp.where(first, near[:KV], near[KV:])
        high_core = jnp.where(first, near[KV:], near[:KV])
        whole = jnp.concatenate(
            [low_core[:, :128], low_core[:, 128:], high_core[:, :128], high_core[:, 128:]], axis=0
        )
        for i in range(GROUP):
            box[GROUP * a + i] = whole
    block_start = pl.multiple_of(place_ref[1] // 4 * 512, 512)
    columns = gathered[COLUMNS_AT:GRADS_AT, pl.ds(block_start, 512)]
    columns = jnp.concatenate([columns[:, 128 * i : 128 * i + 128] for i in range(4)], axis=0)
    gradients = gathered[GRADS_AT:]
    for place_at, (out, cast) in enumerate(((kept, F32), (sent, BF16))):
        slots = (place_at, 2 + place_at)
        q_weights = jnp.concatenate([weights[s][: BLOCKS * 128, :] for s in slots], axis=1)
        q = contract(inputs, q_weights, 1, 0)
        o_weights = jnp.concatenate(
            [
                jnp.concatenate([outputs[s][b * 128 : (b + 1) * 128, :] for b in range(BLOCKS)], axis=1)
                for s in slots
            ],
            axis=0,
        )
        ctx = contract(gradients, o_weights, 1, 1)
        for i in range(2):
            at = i * PER_HEAD
            out[at : at + LENGTH] = q[:, i * 128 : (i + 1) * 128].astype(cast)
            out[at + LENGTH : at + PER_HEAD] = ctx[:, i * 128 : (i + 1) * 128].astype(cast)
        at = 2 * PER_HEAD
        out[at : at + LENGTH] = low.astype(cast)
        high, rest = two_terms(squares)
        pad = jnp.zeros((12, 128), F32)
        out[at + LENGTH : at + SHARED] = jnp.concatenate(
            [high.astype(F32), rest.astype(F32), pad], axis=0
        ).astype(cast)
        out[at + SHARED :] = columns.astype(cast)


def middle_kernel(place_ref, kept, got, keep, send, value_up):
    shared = 2 * PER_HEAD
    keep[:PER_HEAD] = kept[:PER_HEAD] + got[:PER_HEAD].astype(F32)
    send[:PER_HEAD] = (kept[PER_HEAD:shared] + got[PER_HEAD:shared].astype(F32)).astype(BF16)
    low = kept[shared : shared + LENGTH] + got[shared : shared + LENGTH].astype(F32)
    keep[PER_HEAD : PER_HEAD + LENGTH] = low
    send[PER_HEAD : PER_HEAD + LENGTH] = low.astype(BF16)
    rows = kept[shared + LENGTH : shared + SHARED] + got[shared + LENGTH : shared + SHARED].astype(F32)
    squares = rows[0:2] + rows[2:4]
    high, rest = two_terms(squares)
    pad = jnp.zeros((12, 128), F32)
    rows = jnp.concatenate([high.astype(F32), rest.astype(F32), pad], axis=0)
    keep[PER_HEAD + LENGTH :] = rows
    send[PER_HEAD + LENGTH :] = rows.astype(BF16)
    mine, other = kept[shared + SHARED :].astype(BF16), got[shared + SHARED :]
    first = place_ref[2] == 0
    for i in range(4):
        own, its = mine[16 * i : 16 * i + 16], other[16 * i : 16 * i + 16]
        value_up[32 * i : 32 * i + 16] = jnp.where(first, own, its)
        value_up[32 * i + 16 : 32 * i + 32] = jnp.where(first, its, own)


def turn(values, cosine, sine, axis):
    half = HEAD // 2
    if axis == 1:
        front, back = values[:, :half], values[:, half:]
    else:
        front, back = values[:half], values[half:]
    return jnp.concatenate([front * cosine - back * sine, back * cosine + front * sine], axis=axis)


def attention_kernel(
    kept,
    got,
    box,
    value_up_ref,
    hidden,
    gain,
    query_up,
    cosine,
    sine,
    cosine_t,
    sine_t,
    snapshot,
    out,
    up,
    normed,
):
    total = kept[...] + got[...].astype(F32)
    low = total[PER_HEAD : PER_HEAD + LENGTH]
    squares = total[PER_HEAD + LENGTH : PER_HEAD + LENGTH + 2]
    squares = squares + total[PER_HEAD + LENGTH + 2 : PER_HEAD + LENGTH + 4]
    inverse = lax.rsqrt(squares * (1.0 / FEATURES) + EPS)
    column = jnp.concatenate([to_column(inverse[0:1]), to_column(inverse[1:2])], axis=0)
    normed[...] = (hidden[...].astype(F32) * column * gain[...].astype(F32)).astype(BF16)
    lows = (low * column).astype(BF16)
    linear = total[:LENGTH] * column + ADAPTER_SCALE * contract(lows[:, :RANK], query_up[...], 1, 0)
    queries = turn(linear, cosine[...], sine[...], 1).astype(BF16)
    grads = total[LENGTH:PER_HEAD].astype(BF16)
    row_inverse = jnp.concatenate([inverse[0:1], inverse[1:2]], axis=1)
    value_up = value_up_ref[:, :RANK]

    def side(start):
        rows = []
        for i in (start, start + 1):
            part = sum(box[GROUP * a + 2 * i + c].astype(F32) for a in range(NX) for c in range(NC))
            for c in range(NC):
                at = 2 * KV * c
                rows.append(jnp.concatenate([part[at : at + KV], part[at + KV : at + 2 * KV]], axis=1))
        return jnp.concatenate(rows, axis=0) * row_inverse

    keys = side(0).astype(BF16).astype(F32)
    keys = turn(keys, cosine_t[...], sine_t[...], 0).astype(BF16)
    values = (side(2) + ADAPTER_SCALE * contract(value_up, lows[:, RANK:], 1, 1)).astype(BF16)
    scale = HEAD ** (-0.5)
    scores = contract(queries, keys, 1, 0) * scale
    row = lax.broadcasted_iota(jnp.int32, (LENGTH, LENGTH), 0)
    column = lax.broadcasted_iota(jnp.int32, (LENGTH, LENGTH), 1)
    segment = snapshot[...].astype(F32)
    own = jnp.concatenate([to_column(segment[:, :128]), to_column(segment[:, 128:])], axis=0)
    allowed = jnp.logical_and(column <= row, own == segment)
    scores = jnp.where(allowed, scores, MASKED)
    weights = jnp.exp(scores - jnp.max(scores, axis=1, keepdims=True))
    prob = weights / jnp.sum(weights, axis=1, keepdims=True)
    grad_prob = contract(grads, values, 1, 0)
    grad_value = contract(prob.astype(BF16), grads, 0, 0).astype(BF16)
    inner = jnp.sum(prob * grad_prob, axis=1, keepdims=True)
    grad_score = (prob * (grad_prob - inner)).astype(BF16)
    grad_query = contract(grad_score, keys, 1, 1) * scale
    grad_linear = turn(grad_query, cosine[...], -sine[...], 1).astype(BF16)
    low_q, low_v = lows[:, :RANK], lows[:, RANK:]
    up[...] = ADAPTER_SCALE * contract(low_q, grad_linear, 0, 0)
    slices = ADAPTER_SCALE * contract(grad_value, low_v, 0, 0)
    slices = jnp.concatenate([slices, jnp.zeros((HEAD, 128 - RANK), F32)], axis=1).astype(BF16)
    grad_low = jnp.concatenate(
        [
            ADAPTER_SCALE * contract(grad_linear, query_up[...], 1, 1),
            ADAPTER_SCALE * contract(grad_value, value_up, 1, 0),
        ],
        axis=1,
    ).astype(BF16)
    rows = LENGTH // GROUP
    for i in range(GROUP):
        out[i, :rows, :] = grad_low[i * rows : (i + 1) * rows]
        out[i, rows:, :] = slices[16 * i : 16 * i + 16]


def near_kernel(parts, low, value):
    total = jnp.sum(parts[...].astype(F32), axis=0)
    rows = LENGTH // GROUP
    value[...] = total[rows:]
    for i in range(8):
        low[i] = total[:rows].astype(BF16)


def far_kernel(parts, low):
    total = jnp.sum(parts[...].astype(F32), axis=0).astype(BF16)
    for i in range(GROUP):
        low[i] = total


def rows_kernel(normed, low, up, value, out):
    whole = jnp.concatenate([low[i] for i in range(GROUP)], axis=0)
    rows = contract(normed[...], whole, 0, 0).astype(BF16)
    last = jnp.concatenate([up[...], value[...]], axis=0).astype(BF16)
    for i in range(8):
        out[i, :HEAD, :] = rows
        out[i, HEAD:, :] = last


def total_kernel(parts, grad_a_query, query_up, grad_a_value, value):
    total = jnp.sum(parts[...].astype(F32), axis=0)
    rows = total[:HEAD].T
    grad_a_query[...] = rows[:RANK]
    grad_a_value[...] = rows[RANK:]
    query_up[...] = total[HEAD : HEAD + RANK]
    value[...] = total[HEAD + RANK :, :RANK]


def local(
    hidden_in,
    out_grad,
    snapshot_ids,
    norm_gain,
    wq_codes,
    wq_scales,
    wkv_codes,
    wkv_scales,
    wo_codes,
    wo_scales,
    a_query,
    query_up_weight,
    a_value,
    value_up_weight,
):
    head_index = lax.axis_index("fsdp")
    spot = jnp.stack([head_index // (NZ * NC), head_index // NC % NZ, head_index % NC]).astype(jnp.int32)
    gain = norm_gain[None, :]
    masks = (1, NZ * NC, NZ * NC + 1)

    packet = call(
        pack_kernel,
        shape(PACKET, 128),
        hidden_in,
        gain,
        a_query,
        a_value,
        value_up_weight.T,
        out_grad,
        scratch=[
            pltpu.VMEM((LENGTH, 128), BF16),
            pltpu.VMEM((1, 128), BF16),
            pltpu.VMEM((16, RANK), BF16),
            pltpu.SemaphoreType.DMA((6,)),
        ],
        megabytes=56,
        held=True,
    )
    gathered = lax.all_gather(packet, "fsdp", axis=1, tiled=True, axis_index_groups=Z_GROUPS)

    spot = after(spot, packet)
    projections = call(
        projection_kernel,
        [shape(BLOCKS * (128 + KV), 128)] * 4,
        spot,
        wq_codes,
        wq_scales,
        wkv_codes.T,
        wkv_scales.T,
        scratch=[
            pltpu.VMEM((FEATURES, 128), BF16),
            pltpu.VMEM((256, 128), BF16),
            pltpu.VMEM((KV, FEATURES), BF16),
            pltpu.VMEM((KV, 256), BF16),
            pltpu.VMEM((256, 128), F32),
            pltpu.VMEM((KV, FEATURES), F32),
            pltpu.SemaphoreType.DMA((4,)),
        ],
        megabytes=56,
        held=True,
    )
    outputs = call(
        output_kernel,
        [shape(BLOCKS * 128, 128)] * 4,
        after(spot, *projections),
        wo_codes,
        wo_scales,
        scratch=[
            pltpu.VMEM((128, FEATURES), BF16),
            pltpu.VMEM((4, FEATURES), BF16),
            pltpu.SemaphoreType.DMA((2,)),
        ],
        megabytes=56,
        held=True,
    )
    projections = [projections[0]] + [swap_weights(p, mask) for p, mask in zip(projections[1:], masks)]
    outputs = [outputs[0]] + [swap_weights(p, mask) for p, mask in zip(outputs[1:], masks)]

    rows = 2 * PER_HEAD + SHARED + 64
    kept, sent, box = call(
        product_kernel,
        [shape(rows, 128, dtype=F32), shape(rows, 128), shape(2 * GROUP, 128, 128)],
        spot,
        gathered,
        *projections,
        *outputs,
        megabytes=56,
    )
    box = exchange(box, "fsdp", BOX_GROUPS)
    rows = PER_HEAD + SHARED
    kept, sent, value_up = call(
        middle_kernel,
        [shape(rows, 128, dtype=F32), shape(rows, 128), shape(128, 128)],
        spot,
        kept,
        swap(sent, 1),
    )
    got = swap(sent, NZ * NC)

    cosine, sine = rope_tables()
    slices, up, normed = call(
        attention_kernel,
        [shape(GROUP, LENGTH // GROUP + 16, 128), shape(RANK, HEAD, dtype=F32), shape(LENGTH, 128)],
        kept,
        got,
        box,
        value_up,
        hidden_in,
        gain,
        query_up_weight,
        jnp.asarray(cosine),
        jnp.asarray(sine),
        jnp.asarray(cosine.T.copy()),
        jnp.asarray(sine.T.copy()),
        snapshot_ids,
    )

    low, value = call(
        near_kernel,
        [shape(8, LENGTH // GROUP, 128), shape(16, 128, dtype=F32)],
        exchange(slices, "fsdp", NEAR_GROUPS),
    )
    low = call(far_kernel, shape(GROUP, LENGTH // GROUP, 128), exchange(low, "fsdp", FAR_GROUPS))
    mine = call(
        rows_kernel,
        shape(8, HEAD + RANK + 16, 128),
        normed,
        exchange(low, "fsdp", NEAR_GROUPS),
        up,
        value,
    )
    grad_a_query, query_up, grad_a_value, value = call(
        total_kernel,
        [
            shape(RANK, HEAD, dtype=F32),
            shape(RANK, HEAD, dtype=F32),
            shape(RANK, HEAD, dtype=F32),
            shape(16, RANK, dtype=F32),
        ],
        exchange(mine, "dp"),
    )
    return grad_a_query.T, query_up, grad_a_value.T, value.T


def solution(mesh):
    in_specs = (
        P("dp", "fsdp"),
        P("dp", "fsdp"),
        P("dp", None),
        P("fsdp"),
        P(None, "fsdp"),
        P(None, "fsdp"),
        P(None, "fsdp"),
        P(None, "fsdp"),
        P("fsdp", None),
        P("fsdp", None),
        P(None, "fsdp"),
        P(None, "fsdp"),
        P(None, "fsdp"),
        P(None, "fsdp"),
    )
    out_specs = (P("fsdp", None), P(None, "fsdp"), P("fsdp", None), P(None, "fsdp"))
    return jax.shard_map(local, mesh=mesh, in_specs=in_specs, out_specs=out_specs, check_vma=False)
```

time: 210 us -> 194 us (0.924)
  starting transfers between devices: 99.2 us -> 45.7 us
  waiting for transfers between devices: 28.4 us -> 55 us
  between operations: 1.31 us -> 14.4 us
  local copies, waits for them, and re-layouts: 13 us -> 2.02 us
  Pallas kernels: 13 us -> 20.9 us
    ppermute x17 -> x4, starting transfers between devices: 57.6 us -> 13.5 us  [swap_weights(): return lax.ppermute(value, ('dp', 'fsdp'), pairs)]
    ppermute x17 -> x4, waiting for transfers between devices: 7.56 us -> 42.5 us  [swap_weights(): return lax.ppermute(value, ('dp', 'fsdp'), pairs)]
    ppermute x10 -> x4, starting transfers between devices: 35.7 us -> 17.5 us  [swap(): lax.ppermute(value, 'fsdp', [(i, i ^ mask) for i in range(NX * NZ * NC)])]
    all_to_all x1, starting transfers between devices: 5.85 us -> 14.6 us  [exchange(): return lax.all_to_all(value, axis, 0, 0, axis_index_groups=groups)]
    unnamed x46 -> x38, local copies, waits for them, and re-layouts: 10.7 us -> 2.02 us
    pallas_call x11 -> x10, Pallas kernels: 13 us -> 20.9 us  [call(): pl.pallas_call(body, out_shape=outs, in_specs=specs, out_specs=[VMEM] * l...]
    ppermute x10 -> x4, waiting for transfers between devices: 15 us -> 8.45 us  [swap(): lax.ppermute(value, 'fsdp', [(i, i ^ mask) for i in range(NX * NZ * NC)])]
    all_to_all x1, waiting for transfers between devices: 5.84 us -> 0.01 us  [exchange(): return lax.all_to_all(value, axis, 0, 0, axis_index_groups=groups)]
  transfers between devices with their start and end apart: 28 -> 10, of which waited for: 7 -> 5; matrix products, arithmetic and copies ran while one was open for 2% -> 0% of each run, Pallas kernels for 3% -> 5%
where the time goes in v3:
time: 194 us; the launch traced here: 193 us
  waiting for transfers between devices  55 us (28%)
  blocking collectives  54.3 us (28%)
  starting transfers between devices  45.7 us (24%)
  Pallas kernels  20.9 us (11%)
  between operations  14.4 us (7%)
  local copies, waits for them, and re-layouts  2.02 us (1%)
    all_to_all x4, blocking collectives, exchange(): return lax.all_to_all(value, axis, 0, 0, axis_index_groups=groups)  54.3 us
    ppermute x4, waiting for transfers between devices, swap_weights(): return lax.ppermute(value, ('dp', 'fsdp'), pairs)  42.5 us
    pallas_call x10, Pallas kernels, call(): pl.pallas_call(body, out_shape=outs, in_specs=specs, out_specs=[VMEM] * l...  20.9 us
    ppermute x4, starting transfers between devices, swap(): lax.ppermute(value, 'fsdp', [(i, i ^ mask) for i in range(NX * NZ * NC)])  17.5 us
    all_to_all x1, starting transfers between devices, exchange(): return lax.all_to_all(value, axis, 0, 0, axis_index_groups=groups)  14.6 us
    ppermute x4, starting transfers between devices, swap_weights(): return lax.ppermute(value, ('dp', 'fsdp'), pairs)  13.5 us
    ppermute x4, waiting for transfers between devices, swap(): lax.ppermute(value, 'fsdp', [(i, i ^ mask) for i in range(NX * NZ * NC)])  8.45 us
    all_gather x1, waiting for transfers between devices, local(): lax.all_gather(packet, 'fsdp', axis=1, tiled=True, axis_index_groups=Z_GR...  4.07 us
  transfers between devices with their start and end apart: 10, of which 5 were waited for; matrix products, arithmetic and copies ran while one was open for 0% of the time, Pallas kernels for 5%

profile of v3, /device:TPU:1, one launch (start us, length us, event | category | flops | bytes accessed | tf_op | source)
XLA Modules:
  0.0 193.0 jit_solution(16300350829487712967)
XLA Ops:
  7.2 1.8 shard_map.201
  9.7 5.1 %shard_map.202 = (bf16[2560,128]{1,0:T(8,128)(2,1)}, bf16[2560,128]{1,0:T(8,128)(2,1)}, bf16[2560,128]{1,0:T(8,128)(2,1)}, bf16[2560,128]{1,0:T(8,128)(2,1)}) custom-call(s32[3]{0:T(128)} %pad_add_fusion.place_ref, bf16[8192,128]{1,0:T(8,128)(2,1)} %rest_0_.2, bf16[256,128]{1,0:T(8,128)(2,1)} %rest_1_.2, bf16[32,8192]{1,0:T(8,128)(2,1)} %bitcast.12, ...), custom_call_target="tpu_custom_call" | custom-call | tf_op jit(solution)/shard_map/pallas_call | solution.py:96
  14.8 4.7 %shard_map.203 = (bf16[2048,128]{1,0:T(8,128)(2,1)}, bf16[2048,128]{1,0:T(8,128)(2,1)}, bf16[2048,128]{1,0:T(8,128)(2,1)}, bf16[2048,128]{1,0:T(8,128)(2,1)}) custom-call(s32[3]{0:T(128)} %pad_add_fusion.place_ref, bf16[128,8192]{1,0:T(8,128)(2,1)} %rest_0_.3, bf16[4,8192]{1,0:T(4,128)(2,1)} %rest_1_.3), custom_call_target="tpu_custom_call" | custom-call | tf_op jit(solution)/shard_map/pallas_call | solution.py:96
  19.5 8.8 %collective-permute-start.3 = (bf16[2048,128]{1,0:T(8,128)(2,1)}, bf16[2048,128]{1,0:T(8,128)(2,1)S(1)}, u32[]{:S(2)}, u32[]{:S(2)}) collective-permute-start(bf16[2048,128]{1,0:T(8,128)(2,1)} %get-tuple-element.36), channel_id=1, source_target_pairs={{0,1},{1,0},{2,3},{3,2},{4,5},{5,4},{6,7},{7,6},{8,9},{9,8},{10,11... | collective-permute-start | bytes 1572872 | tf_op jit(solution)/shard_map/ppermute | solution.py:49
  28.3 1.9 collective-permute-start
  30.3 1.9 collective-permute-start.1
  32.2 5.2 %collective-permute-start.2 = (bf16[2560,128]{1,0:T(8,128)(2,1)S(1)}, bf16[2560,128]{1,0:T(8,128)(2,1)S(1)}, u32[]{:S(2)}, u32[]{:S(2)}) collective-permute-start(bf16[2560,128]{1,0:T(8,128)(2,1)S(1)} %copy-done.16), channel_id=1, source_target_pairs={{0,97},{1,96},{2,99},{3,98},{4,101},{5,100},{6,103},{7,102},{8,105... | collective-permute-start | bytes 1966088 | tf_op jit(solution)/shard_map/ppermute | solution.py:58
  37.5 1.9 collective-permute-start.4
  39.4 4.5 %collective-permute-start.5 = (bf16[2048,128]{1,0:T(8,128)(2,1)}, bf16[2048,128]{1,0:T(8,128)(2,1)S(1)}, u32[]{:S(2)}, u32[]{:S(2)}) collective-permute-start(bf16[2048,128]{1,0:T(8,128)(2,1)} %get-tuple-element.38), channel_id=1, source_target_pairs={{0,97},{1,96},{2,99},{3,98},{4,101},{5,100},{6,103},{7,102},{8,105... | collective-permute-start | bytes 1572872 | tf_op jit(solution)/shard_map/ppermute | solution.py:58
  43.9 30.6 %collective-permute-done.4.refs_6_ = bf16[2048,128]{1,0:T(8,128)(2,1)S(1)} collective-permute-done((bf16[2048,128]{1,0:T(8,128)(2,1)}, bf16[2048,128]{1,0:T(8,128)(2,1)S(1)}, u32[]{:S(2)}, u32[]{:S(2)}) %collective-permute-start.4) | collective-permute-done | bytes 524320 | tf_op jit(solution)/shard_map/ppermute | solution.py:58
  74.5 11.9 %collective-permute-done.5.refs_7_ = bf16[2048,128]{1,0:T(8,128)(2,1)S(1)} collective-permute-done((bf16[2048,128]{1,0:T(8,128)(2,1)}, bf16[2048,128]{1,0:T(8,128)(2,1)S(1)}, u32[]{:S(2)}, u32[]{:S(2)}) %collective-permute-start.5) | collective-permute-done | bytes 524320 | tf_op jit(solution)/shard_map/ppermute | solution.py:58
  87.2 4.1 %all-gather.2.cloned.1.call-done.gathered = bf16[672,2048]{1,0:T(8,128)(2,1)} async-done(((bf16[672,128]{1,0:T(8,128)(2,1)}), bf16[672,2048]{1,0:T(8,128)(2,1)}) %all-gather.2.cloned.1.call-update) | async-done | bytes 2752528 | tf_op jit(solution)/shard_map/all_gather | solution.py:451
  91.3 6.2 %shard_map.204 = (f32[1360,128]{1,0:T(8,128)}, bf16[1360,128]{1,0:T(8,128)(2,1)}, bf16[16,128,128]{2,1,0:T(8,128)(2,1)}) custom-call(s32[3]{0:T(128)} %pad_add_fusion.place_ref, bf16[672,2048]{1,0:T(8,128)(2,1)} %all-gather.2.cloned.1.call-done.gathered, bf16[2560,128]{1,0:T(8,128)(2,1)} %get-tuple-element.30.refs_0_, bf16[2560,128]{1,0:T(8,128)(2,1)} %copy-done.10, ...), custom_call_target="tpu_custom_call" | custom-call | tf_op jit(solution)/shard_map/pallas_call | solution.py:96
  97.6 14.6 %all-to-all-start = ((bf16[16,128,128]{2,1,0:T(8,128)(2,1)}), bf16[16,128,128]{2,1,0:T(8,128)(2,1)S(1)}, u32[]{:S(2)}, u32[]{:S(2)}) async-start(bf16[16,128,128]{2,1,0:T(8,128)(2,1)} %get-tuple-element.43), calls=%async_computation | async-start | bytes 1048576 | tf_op jit(solution)/shard_map/all_to_all | solution.py:62
  112.2 2.0 %collective-permute-start.6 = (bf16[1360,128]{1,0:T(8,128)(2,1)}, bf16[1360,128]{1,0:T(8,128)(2,1)S(1)}, u32[]{:S(2)}, u32[]{:S(2)}) collective-permute-start(bf16[1360,128]{1,0:T(8,128)(2,1)} %get-tuple-element.40), channel_id=1, source_target_pairs={{0,1},{1,0},{2,3},{3,2},{4,5},{5,4},{6,7},{7,6},{8,9},{9,8},{10,11... | collective-permute-start | bytes 1044488 | tf_op jit(solution)/shard_map/ppermute | solution.py:49
  114.2 1.7 collective-permute-done.6.got
  115.9 1.1 copy-done
  117.7 4.8 %collective-permute-start.7 = (bf16[784,128]{1,0:T(8,128)(2,1)S(1)}, bf16[784,128]{1,0:T(8,128)(2,1)S(1)}, u32[]{:S(2)}, u32[]{:S(2)}) collective-permute-start(bf16[784,128]{1,0:T(8,128)(2,1)S(1)} %get-tuple-element.42), channel_id=1, source_target_pairs={{0,32},{1,33},{2,34},{3,35},{4,36},{5,37},{6,38},{7,39},{8,40},{9,... | collective-permute-start | bytes 602120 | tf_op jit(solution)/shard_map/ppermute | solution.py:49
  122.5 6.7 %collective-permute-done.7.got = bf16[784,128]{1,0:T(8,128)(2,1)S(1)} collective-permute-done((bf16[784,128]{1,0:T(8,128)(2,1)S(1)}, bf16[784,128]{1,0:T(8,128)(2,1)S(1)}, u32[]{:S(2)}, u32[]{:S(2)}) %collective-permute-start.7) | collective-permute-done | bytes 200736 | tf_op jit(solution)/shard_map/ppermute | solution.py:49
  129.2 1.5 shard_map.206
  130.8 10.3 %all_to_all.25.parts = bf16[8,48,128]{2,1,0:T(8,128)(2,1)S(1)} all-to-all(bf16[8,48,128]{2,1,0:T(8,128)(2,1)S(1)} %get-tuple-element.46), channel_id=1, replica_groups={{0,1,2,3,4,5,6,7},{8,9,10,11,12,13,14,15},{16,17,18,19,20,21,22,23},{24..., dimensions={0} | all-to-all | bytes 196608 | tf_op jit(solution)/shard_map/all_to_all | solution.py:62
  141.2 22.1 %all_to_all.26.parts = bf16[8,32,128]{2,1,0:T(8,128)(2,1)S(1)} all-to-all(bf16[8,32,128]{2,1,0:T(8,128)(2,1)S(1)} %get-tuple-element.47), channel_id=1, replica_groups={{0,8,16,24,32,40,48,56},{1,9,17,25,33,41,49,57},{2,10,18,26,34,42,50,58..., dimensions={0} | all-to-all | bytes 131072 | tf_op jit(solution)/shard_map/all_to_all | solution.py:62
  163.3 9.6 %all_to_all.27.low = bf16[8,32,128]{2,1,0:T(8,128)(2,1)S(1)} all-to-all(bf16[8,32,128]{2,1,0:T(8,128)(2,1)S(1)} %shard_map.208), channel_id=1, replica_groups={{0,1,2,3,4,5,6,7},{8,9,10,11,12,13,14,15},{16,17,18,19,20,21,22,23},{24..., dimensions={0} | all-to-all | bytes 131072 | tf_op jit(solution)/shard_map/all_to_all | solution.py:62
  173.2 12.2 %all_to_all.28.parts = bf16[8,208,128]{2,1,0:T(8,128)(2,1)S(1)} all-to-all(bf16[8,208,128]{2,1,0:T(8,128)(2,1)S(1)} %shard_map.209), channel_id=1, replica_groups=mesh['dp'=8,'fsdp'=64] {'dp'}, dimensions={0} | all-to-all | bytes 851968 | tf_op jit(solution)/shard_map/all_to_all | solution.py:62
  (50 shorter events, 3.2 us)
Async XLA Ops:
  7.2 84.1 %all-gather.2.cloned.1.call-start = ((), (), s32[]{:S(2)}) async-start(), calls=%async_computation.5 | async-start | bytes 2924544 | tf_op jit(solution)/shard_map/all_gather | solution.py:451
  14.8 13.5 %copy-start.18 = (bf16[2560,128]{1,0:T(8,128)(2,1)S(1)}, bf16[2560,128]{1,0:T(8,128)(2,1)}, u32[]{:S(2)}) copy-start(bf16[2560,128]{1,0:T(8,128)(2,1)} %get-tuple-element.31) | copy-start | bytes 1966084
  14.8 15.4 %copy-start.17 = (bf16[2560,128]{1,0:T(8,128)(2,1)S(1)}, bf16[2560,128]{1,0:T(8,128)(2,1)}, u32[]{:S(2)}) copy-start(bf16[2560,128]{1,0:T(8,128)(2,1)} %get-tuple-element.32) | copy-start | bytes 1966084
  14.8 17.4 %copy-start.16 = (bf16[2560,128]{1,0:T(8,128)(2,1)S(1)}, bf16[2560,128]{1,0:T(8,128)(2,1)}, u32[]{:S(2)}) copy-start(bf16[2560,128]{1,0:T(8,128)(2,1)} %get-tuple-element.33) | copy-start | bytes 1966084
  19.5 19.9 %collective-permute-start.3 = (bf16[2048,128]{1,0:T(8,128)(2,1)}, bf16[2048,128]{1,0:T(8,128)(2,1)S(1)}, u32[]{:S(2)}, u32[]{:S(2)}) collective-permute-start(bf16[2048,128]{1,0:T(8,128)(2,1)} %get-tuple-element.36), channel_id=1, source_target_pairs={{0,1},{1,0},{2,3},{3,2},{4,5},{5,4},{6,7},{7,6},{8,9},{9,8},{10,11... | collective-permute-start | bytes 1572872 | tf_op jit(solution)/shard_map/ppermute | solution.py:49
  28.3 58.0 %collective-permute-start = (bf16[2560,128]{1,0:T(8,128)(2,1)S(1)}, bf16[2560,128]{1,0:T(8,128)(2,1)S(1)}, u32[]{:S(2)}, u32[]{:S(2)}) collective-permute-start(bf16[2560,128]{1,0:T(8,128)(2,1)S(1)} %copy-done.18), channel_id=1, source_target_pairs={{0,1},{1,0},{2,3},{3,2},{4,5},{5,4},{6,7},{7,6},{8,9},{9,8},{10,11... | collective-permute-start | bytes 1966088 | tf_op jit(solution)/shard_map/ppermute | solution.py:49
  30.3 56.1 %collective-permute-start.1 = (bf16[2560,128]{1,0:T(8,128)(2,1)S(1)}, bf16[2560,128]{1,0:T(8,128)(2,1)S(1)}, u32[]{:S(2)}, u32[]{:S(2)}) collective-permute-start(bf16[2560,128]{1,0:T(8,128)(2,1)S(1)} %copy-done.17), channel_id=1, source_target_pairs={{0,96},{1,97},{2,98},{3,99},{4,100},{5,101},{6,102},{7,103},{8,104... | collective-permute-start | bytes 1966088 | tf_op jit(solution)/shard_map/ppermute | solution.py:58
  32.2 55.0 %collective-permute-start.2 = (bf16[2560,128]{1,0:T(8,128)(2,1)S(1)}, bf16[2560,128]{1,0:T(8,128)(2,1)S(1)}, u32[]{:S(2)}, u32[]{:S(2)}) collective-permute-start(bf16[2560,128]{1,0:T(8,128)(2,1)S(1)} %copy-done.16), channel_id=1, source_target_pairs={{0,97},{1,96},{2,99},{3,98},{4,101},{5,100},{6,103},{7,102},{8,105... | collective-permute-start | bytes 1966088 | tf_op jit(solution)/shard_map/ppermute | solution.py:58
  37.5 37.0 %collective-permute-start.4 = (bf16[2048,128]{1,0:T(8,128)(2,1)}, bf16[2048,128]{1,0:T(8,128)(2,1)S(1)}, u32[]{:S(2)}, u32[]{:S(2)}) collective-permute-start(bf16[2048,128]{1,0:T(8,128)(2,1)} %get-tuple-element.37), channel_id=1, source_target_pairs={{0,96},{1,97},{2,98},{3,99},{4,100},{5,101},{6,102},{7,103},{8,104... | collective-permute-start | bytes 1572872 | tf_op jit(solution)/shard_map/ppermute | solution.py:58
  39.4 51.9 %copy-start.13 = (bf16[2048,128]{1,0:T(8,128)(2,1)}, bf16[2048,128]{1,0:T(8,128)(2,1)S(1)}, u32[]{:S(2)}) copy-start(bf16[2048,128]{1,0:T(8,128)(2,1)S(1)} %collective-permute-done.3.refs_5_) | copy-start | bytes 1572868
  39.4 46.9 %collective-permute-start.5 = (bf16[2048,128]{1,0:T(8,128)(2,1)}, bf16[2048,128]{1,0:T(8,128)(2,1)S(1)}, u32[]{:S(2)}, u32[]{:S(2)}) collective-permute-start(bf16[2048,128]{1,0:T(8,128)(2,1)} %get-tuple-element.38), channel_id=1, source_target_pairs={{0,97},{1,96},{2,99},{3,98},{4,101},{5,100},{6,103},{7,102},{8,105... | collective-permute-start | bytes 1572872 | tf_op jit(solution)/shard_map/ppermute | solution.py:58
  74.5 16.8 %copy-start.14 = (bf16[2048,128]{1,0:T(8,128)(2,1)}, bf16[2048,128]{1,0:T(8,128)(2,1)S(1)}, u32[]{:S(2)}) copy-start(bf16[2048,128]{1,0:T(8,128)(2,1)S(1)} %collective-permute-done.4.refs_6_) | copy-start | bytes 1572868
  91.3 24.6 %copy-start.7 = (s32[3]{0:T(128)S(1)}, s32[3]{0:T(128)}, u32[]{:S(2)}) copy-start(s32[3]{0:T(128)} %pad_add_fusion.place_ref) | copy-start | bytes 40
  97.5 31.7 %copy-start.1 = (bf16[256,128]{1,0:T(8,128)(2,1)S(1)}, bf16[256,128]{1,0:T(8,128)(2,1)}, u32[]{:S(2)}) copy-start(bf16[256,128]{1,0:T(8,128)(2,1)} %hidden.1) | copy-start | bytes 196612
  97.5 31.7 %copy-start.2 = (f32[256,64]{1,0:T(8,128)S(1)}, f32[256,64]{1,0:T(8,128)}, u32[]{:S(2)}) copy-start(f32[256,64]{1,0:T(8,128)} %constant.58.clone.sine) | copy-start | bytes 196612
  97.5 31.7 %copy-start.3 = (f32[256,64]{1,0:T(8,128)S(1)}, f32[256,64]{1,0:T(8,128)}, u32[]{:S(2)}) copy-start(f32[256,64]{1,0:T(8,128)} %constant.57.clone.cosine) | copy-start | bytes 196612
  97.5 31.7 %copy-start.4 = (f32[64,256]{1,0:T(8,128)S(1)}, f32[64,256]{1,0:T(8,128)}, u32[]{:S(2)}) copy-start(f32[64,256]{1,0:T(8,128)} %constant.60.clone.sine_t) | copy-start | bytes 196612
  97.5 31.7 %copy-start.5 = (f32[64,256]{1,0:T(8,128)S(1)}, f32[64,256]{1,0:T(8,128)}, u32[]{:S(2)}) copy-start(f32[64,256]{1,0:T(8,128)} %constant.59.clone.cosine_t) | copy-start | bytes 196612
  97.5 31.7 %copy-start.6 = (bf16[64,128]{1,0:T(8,128)(2,1)S(1)}, bf16[64,128]{1,0:T(8,128)(2,1)}, u32[]{:S(2)}) copy-start(bf16[64,128]{1,0:T(8,128)(2,1)} %query_up.1) | copy-start | bytes 49156
  97.6 31.7 %copy-start.8 = (bf16[128]{0:T(256)(128)(2,1)S(1)}, bf16[128]{0:T(256)(128)(2,1)}, u32[]{:S(2)}) copy-start(bf16[128]{0:T(256)(128)(2,1)} %param.21) | copy-start | bytes 772
  97.6 31.7 %copy-start.9 = (s32[1,256]{1,0:T(1,128)S(1)}, s32[1,256]{1,0:T(1,128)}, u32[]{:S(2)}) copy-start(s32[1,256]{1,0:T(1,128)} %snapshot.1) | copy-start | bytes 3076
  97.6 31.6 %all-to-all-start = ((bf16[16,128,128]{2,1,0:T(8,128)(2,1)}), bf16[16,128,128]{2,1,0:T(8,128)(2,1)S(1)}, u32[]{:S(2)}, u32[]{:S(2)}) async-start(bf16[16,128,128]{2,1,0:T(8,128)(2,1)} %get-tuple-element.43), calls=%async_computation | async-start | bytes 1048576 | tf_op jit(solution)/shard_map/all_to_all | solution.py:62
  112.2 3.8 %collective-permute-start.6 = (bf16[1360,128]{1,0:T(8,128)(2,1)}, bf16[1360,128]{1,0:T(8,128)(2,1)S(1)}, u32[]{:S(2)}, u32[]{:S(2)}) collective-permute-start(bf16[1360,128]{1,0:T(8,128)(2,1)} %get-tuple-element.40), channel_id=1, source_target_pairs={{0,1},{1,0},{2,3},{3,2},{4,5},{5,4},{6,7},{7,6},{8,9},{9,8},{10,11... | collective-permute-start | bytes 1044488 | tf_op jit(solution)/shard_map/ppermute | solution.py:49
  117.7 11.5 %collective-permute-start.7 = (bf16[784,128]{1,0:T(8,128)(2,1)S(1)}, bf16[784,128]{1,0:T(8,128)(2,1)S(1)}, u32[]{:S(2)}, u32[]{:S(2)}) collective-permute-start(bf16[784,128]{1,0:T(8,128)(2,1)S(1)} %get-tuple-element.42), channel_id=1, source_target_pairs={{0,32},{1,33},{2,34},{3,35},{4,36},{5,37},{6,38},{7,39},{8,40},{9,... | collective-permute-start | bytes 602120 | tf_op jit(solution)/shard_map/ppermute | solution.py:49
  (5 other events, 15.1 us)
Sparse Core Ops, SparseCore 0:
  10.0 81.2 all-gather.1

commit v4 on v3

--- a/solution.py
+++ b/solution.py
@@ -17,7 +17,8 @@
 NX, NZ, NC = 2, 16, 2
 LENGTH, HEAD, RANK, KV = 256, 128, 64, 32
 FEATURES = NX * NZ * NC * HEAD
-BLOCKS = NZ
+HALF = FEATURES // NX
+BLOCKS = NZ * NC
 DOWNS_AT = LENGTH
 SQUARES_AT = DOWNS_AT + 2 * RANK
 COLUMNS_AT = SQUARES_AT + 16
@@ -35,7 +36,7 @@
     return a * (NZ * NC) + z * NC + c
 
 
-Z_GROUPS = [[place(a, z, c) for z in range(NZ)] for a in range(NX) for c in range(NC)]
+HALF_GROUPS = [[place(a, z, c) for z in range(NZ) for c in range(NC)] for a in range(NX)]
 BOX_GROUPS = [
     [place(a, 4 * b + i, c) for a in range(NX) for i in range(4) for c in range(NC)] for b in range(4)
 ]
@@ -155,15 +156,17 @@
     )
 
 
-def peer_block(place_ref, slot, j):
-    peer_x = place_ref[0] ^ (slot >> 1)
-    peer_c = place_ref[2] ^ (slot & 1)
-    return peer_x * (NZ * NC) + j * NC + peer_c, peer_c
-
-
 def projection_kernel(place_ref, *rest):
-    sources, outs, held = rest[:4], rest[4:8], rest[8:12]
-    q_levels, kv_levels, sems = rest[12:]
+    sources, out, held = rest[:4], rest[4], rest[5:9]
+    q_levels, kv_levels, sems = rest[9:]
+    half = pl.multiple_of(place_ref[0] * HALF, HALF)
+    scales = pl.multiple_of(place_ref[0] * 128, 128)
+    sources = (
+        sources[0].at[pl.ds(half, HALF), :],
+        sources[1].at[pl.ds(scales, 128), :],
+        sources[2].at[:, pl.ds(half, HALF)],
+        sources[3].at[:, pl.ds(scales, 128)],
+    )
     fetch(sources, held, sems)
     wq, wq_scales, wkv, wkv_scales = held
     q_levels[...] = wq_scales[...].astype(F32)
@@ -171,125 +174,93 @@
         jnp.int32, (32, 1024), 0
     )
     widen = jnp.where(widen, 1.0, 0.0).astype(BF16)
-    for i in range(8):
+    for i in range(4):
         level = contract(wkv_scales[:, 32 * i : 32 * i + 32], widen, 1, 0)
         kv_levels[:, 1024 * i : 1024 * i + 1024] = level
-    for slot in range(4):
-        out = outs[slot]
-
-        def step(j, carry, slot=slot, out=out):
-            block, peer_c = peer_block(place_ref, slot, j)
-            rows = pl.ds(pl.multiple_of(block * 128, 128), 128)
-            both = q_levels[pl.ds(pl.multiple_of((block - peer_c) * 4, 8), 8), :]
-            level = jnp.where(peer_c == 0, both[:4], both[4:])
-            codes = wq[rows, :].astype(F32).reshape(4, 32, 128) * level[:, None, :]
-            to = pl.multiple_of(j * 128, 128)
-            out[pl.ds(to, 128), :] = codes.reshape(128, 128).astype(BF16)
+
+    def step(j, carry):
+        levels = q_levels[pl.ds(pl.multiple_of(j * 8, 8), 8), :]
+        for e in range(2):
+            rows = pl.ds(pl.multiple_of((2 * j + e) * 128, 128), 128)
+            codes = wq[rows, :].astype(F32).reshape(4, 32, 128) * levels[4 * e : 4 * e + 4][:, None, :]
+            out[rows, :] = codes.reshape(128, 128).astype(BF16)
             codes = wkv[:, rows].astype(F32) * kv_levels[:, rows]
-            to = pl.multiple_of(BLOCKS * 128 + j * KV, KV)
+            to = pl.multiple_of(HALF + (2 * j + e) * KV, KV)
             out[pl.ds(to, KV), :] = codes.astype(BF16)
-            return carry
-
-        lax.fori_loop(0, BLOCKS, step, 0, unroll=2)
+        return carry
+
+    lax.fori_loop(0, BLOCKS // 2, step, 0, unroll=2)
 
 
 def output_kernel(place_ref, *rest):
-    sources, outs, (wo, wo_scales, sems) = rest[:2], rest[2:6], rest[6:]
-    fetch(sources, (wo, wo_scales), sems)
-    for slot in range(4):
-        out = outs[slot]
-
-        def step(j, carry, slot=slot, out=out):
-            block, _ = peer_block(place_ref, slot, j)
-            columns = pl.ds(pl.multiple_of(block * 128, 128), 128)
-            level = wo_scales[:, columns].astype(F32)
-            codes = wo[:, columns].astype(F32).reshape(4, 32, 128) * level[:, None, :]
-            to = pl.multiple_of(j * 128, 128)
-            out[pl.ds(to, 128), :] = codes.reshape(128, 128).astype(BF16)
-            return carry
-
-        lax.fori_loop(0, BLOCKS, step, 0, unroll=2)
-
-
-def product_kernel(place_ref, gathered, *refs):
-    weights, outputs, (kept, sent, box) = refs[:4], refs[4:8], refs[8:]
-    inputs = gathered[:LENGTH]
-    low = contract(inputs, gathered[DOWNS_AT:SQUARES_AT], 1, 1)
-    squares = sum(
-        gathered[SQUARES_AT : SQUARES_AT + 16, b * 128 : (b + 1) * 128].astype(F32) for b in range(BLOCKS)
-    )
+    sources, out, (wo, wo_scales, sems) = rest[:2], rest[2], rest[3:]
+    half = pl.ds(pl.multiple_of(place_ref[0] * HALF, HALF), HALF)
+    fetch((sources[0].at[:, half], sources[1].at[:, half]), (wo, wo_scales), sems)
+
+    def step(j, carry):
+        block = pl.ds(pl.multiple_of(j * 128, 128), 128)
+        level = wo_scales[:, block].astype(F32)
+        codes = wo[:, block].astype(F32).reshape(4, 32, 128) * level[:, None, :]
+        out[block, :] = codes.reshape(128, 128).astype(BF16)
+        return carry
+
+    lax.fori_loop(0, BLOCKS, step, 0, unroll=4)
+
+
+def product_kernel(place_ref, *refs):
+    sources, (kept, sent, box, value_up), held, sems = refs[:5], refs[5:9], refs[9:14], refs[14]
+    copies = [pltpu.make_async_copy(a, b, sems.at[i]) for i, (a, b) in enumerate(zip(sources, held))]
+    for copy in copies:
+        copy.start()
+    gathered, weights, outputs = held[0], held[1:3], held[3:5]
+
+    def rows(start, number):
+        return [gathered[b * PACKET + start : b * PACKET + start + number, :] for b in range(BLOCKS)]
+
+    copies[0].wait()
+    inputs = jnp.concatenate(rows(0, LENGTH), axis=1)
+    low = contract(inputs, jnp.concatenate(rows(DOWNS_AT, 2 * RANK), axis=1), 1, 1)
+    squares = sum(r.astype(F32) for r in rows(SQUARES_AT, 16))
     squares = squares[0:2] + squares[2:4]
+    group = place_ref[1] // 4 * GROUP
+    for i in range(GROUP):
+        at = pl.multiple_of((group + i) * PACKET + COLUMNS_AT, 16)
+        value_up[16 * i : 16 * i + 16, :] = gathered[pl.ds(at, 16), :]
+    copies[1].wait()
+    copies[2].wait()
+    q = contract(inputs, jnp.concatenate([w[:HALF, :] for w in weights], axis=1), 1, 0)
     kv_weights = jnp.concatenate(
         [
-            jnp.concatenate(
-                [w[BLOCKS * 128 + b * KV : BLOCKS * 128 + (b + 1) * KV, :] for b in range(BLOCKS)], axis=1
-            )
+            jnp.concatenate([w[HALF + b * KV : HALF + (b + 1) * KV, :] for b in range(BLOCKS)], axis=1)
             for w in weights
         ],
         axis=0,
     )
     kv = contract(kv_weights, inputs, 1, 1).astype(BF16)
-    at_zero, first = place_ref[0] == 0, place_ref[2] == 0
+    at_zero = place_ref[0] == 0
     for a in range(NX):
         mine = at_zero if a == 0 else jnp.logical_not(at_zero)
-        near = jnp.where(mine, kv[: 2 * KV], kv[2 * KV :])
-        low_core = jnp.where(first, near[:KV], near[KV:])
-        high_core = jnp.where(first, near[KV:], near[:KV])
-        whole = jnp.concatenate(
-            [low_core[:, :128], low_core[:, 128:], high_core[:, :128], high_core[:, 128:]], axis=0
-        )
+        whole = jnp.where(mine, kv[:KV], kv[KV:])
+        whole = jnp.concatenate([whole[:, :128], whole[:, 128:]], axis=0)
         for i in range(GROUP):
             box[GROUP * a + i] = whole
-    block_start = pl.multiple_of(place_ref[1] // 4 * 512, 512)
-    columns = gathered[COLUMNS_AT:GRADS_AT, pl.ds(block_start, 512)]
-    columns = jnp.concatenate([columns[:, 128 * i : 128 * i + 128] for i in range(4)], axis=0)
-    gradients = gathered[GRADS_AT:]
-    for place_at, (out, cast) in enumerate(((kept, F32), (sent, BF16))):
-        slots = (place_at, 2 + place_at)
-        q_weights = jnp.concatenate([weights[s][: BLOCKS * 128, :] for s in slots], axis=1)
-        q = contract(inputs, q_weights, 1, 0)
-        o_weights = jnp.concatenate(
-            [
-                jnp.concatenate([outputs[s][b * 128 : (b + 1) * 128, :] for b in range(BLOCKS)], axis=1)
-                for s in slots
-            ],
-            axis=0,
-        )
-        ctx = contract(gradients, o_weights, 1, 1)
-        for i in range(2):
-            at = i * PER_HEAD
-            out[at : at + LENGTH] = q[:, i * 128 : (i + 1) * 128].astype(cast)
-            out[at + LENGTH : at + PER_HEAD] = ctx[:, i * 128 : (i + 1) * 128].astype(cast)
-        at = 2 * PER_HEAD
-        out[at : at + LENGTH] = low.astype(cast)
-        high, rest = two_terms(squares)
-        pad = jnp.zeros((12, 128), F32)
-        out[at + LENGTH : at + SHARED] = jnp.concatenate(
-            [high.astype(F32), rest.astype(F32), pad], axis=0
-        ).astype(cast)
-        out[at + SHARED :] = columns.astype(cast)
-
-
-def middle_kernel(place_ref, kept, got, keep, send, value_up):
-    shared = 2 * PER_HEAD
-    keep[:PER_HEAD] = kept[:PER_HEAD] + got[:PER_HEAD].astype(F32)
-    send[:PER_HEAD] = (kept[PER_HEAD:shared] + got[PER_HEAD:shared].astype(F32)).astype(BF16)
-    low = kept[shared : shared + LENGTH] + got[shared : shared + LENGTH].astype(F32)
-    keep[PER_HEAD : PER_HEAD + LENGTH] = low
-    send[PER_HEAD : PER_HEAD + LENGTH] = low.astype(BF16)
-    rows = kept[shared + LENGTH : shared + SHARED] + got[shared + LENGTH : shared + SHARED].astype(F32)
-    squares = rows[0:2] + rows[2:4]
+    copies[3].wait()
+    copies[4].wait()
+    o_weights = jnp.concatenate(
+        [
+            jnp.concatenate([w[b * 128 : (b + 1) * 128, :] for b in range(BLOCKS)], axis=1)
+            for w in outputs
+        ],
+        axis=0,
+    )
+    ctx = contract(jnp.concatenate(rows(GRADS_AT, LENGTH), axis=1), o_weights, 1, 1)
     high, rest = two_terms(squares)
-    pad = jnp.zeros((12, 128), F32)
-    rows = jnp.concatenate([high.astype(F32), rest.astype(F32), pad], axis=0)
-    keep[PER_HEAD + LENGTH :] = rows
-    send[PER_HEAD + LENGTH :] = rows.astype(BF16)
-    mine, other = kept[shared + SHARED :].astype(BF16), got[shared + SHARED :]
-    first = place_ref[2] == 0
-    for i in range(4):
-        own, its = mine[16 * i : 16 * i + 16], other[16 * i : 16 * i + 16]
-        value_up[32 * i : 32 * i + 16] = jnp.where(first, own, its)
-        value_up[32 * i + 16 : 32 * i + 32] = jnp.where(first, its, own)
+    shared = jnp.concatenate([high.astype(F32), rest.astype(F32), jnp.zeros((12, 128), F32)], axis=0)
+    for i, (out, cast) in enumerate(((kept, F32), (sent, BF16))):
+        out[:LENGTH] = q[:, i * 128 : (i + 1) * 128].astype(cast)
+        out[LENGTH:PER_HEAD] = ctx[:, i * 128 : (i + 1) * 128].astype(cast)
+        out[PER_HEAD : PER_HEAD + LENGTH] = low.astype(cast)
+        out[PER_HEAD + LENGTH :] = shared.astype(cast)
 
 
 def turn(values, cosine, sine, axis):
@@ -334,16 +305,14 @@
 
     def side(start):
         rows = []
-        for i in (start, start + 1):
-            part = sum(box[GROUP * a + 2 * i + c].astype(F32) for a in range(NX) for c in range(NC))
-            for c in range(NC):
-                at = 2 * KV * c
-                rows.append(jnp.concatenate([part[at : at + KV], part[at + KV : at + 2 * KV]], axis=1))
+        for i in range(start, start + GROUP // 2):
+            part = sum(box[GROUP * a + i].astype(F32) for a in range(NX))
+            rows.append(jnp.concatenate([part[:KV], part[KV:]], axis=1))
         return jnp.concatenate(rows, axis=0) * row_inverse
 
     keys = side(0).astype(BF16).astype(F32)
     keys = turn(keys, cosine_t[...], sine_t[...], 0).astype(BF16)
-    values = (side(2) + ADAPTER_SCALE * contract(value_up, lows[:, RANK:], 1, 1)).astype(BF16)
+    values = (side(GROUP // 2) + ADAPTER_SCALE * contract(value_up, lows[:, RANK:], 1, 1)).astype(BF16)
     scale = HEAD ** (-0.5)
     scores = contract(queries, keys, 1, 0) * scale
     row = lax.broadcasted_iota(jnp.int32, (LENGTH, LENGTH), 0)
@@ -428,7 +397,6 @@
     head_index = lax.axis_index("fsdp")
     spot = jnp.stack([head_index // (NZ * NC), head_index // NC % NZ, head_index % NC]).astype(jnp.int32)
     gain = norm_gain[None, :]
-    masks = (1, NZ * NC, NZ * NC + 1)
 
     packet = call(
         pack_kernel,
@@ -448,66 +416,80 @@
         megabytes=56,
         held=True,
     )
-    gathered = lax.all_gather(packet, "fsdp", axis=1, tiled=True, axis_index_groups=Z_GROUPS)
-
-    spot = after(spot, packet)
-    projections = call(
-        projection_kernel,
-        [shape(BLOCKS * (128 + KV), 128)] * 4,
+    gathered = lax.all_gather(packet, "fsdp", axis=0, tiled=True, axis_index_groups=HALF_GROUPS)
+
+    def projection(spot):
+        return call(
+            projection_kernel,
+            shape(BLOCKS * (128 + KV), 128),
+            spot,
+            wq_codes,
+            wq_scales,
+            wkv_codes.T,
+            wkv_scales.T,
+            scratch=[
+                pltpu.VMEM((HALF, 128), BF16),
+                pltpu.VMEM((128, 128), BF16),
+                pltpu.VMEM((KV, HALF), BF16),
+                pltpu.VMEM((KV, 128), BF16),
+                pltpu.VMEM((128, 128), F32),
+                pltpu.VMEM((KV, HALF), F32),
+                pltpu.SemaphoreType.DMA((4,)),
+            ],
+            megabytes=56,
+            held=True,
+        )
+
+    def output(spot):
+        return call(
+            output_kernel,
+            shape(BLOCKS * 128, 128),
+            spot,
+            wo_codes,
+            wo_scales,
+            scratch=[
+                pltpu.VMEM((128, HALF), BF16),
+                pltpu.VMEM((4, HALF), BF16),
+                pltpu.SemaphoreType.DMA((2,)),
+            ],
+            megabytes=56,
+            held=True,
+        )
+
+    other = spot ^ jnp.array([1, 0, 0], jnp.int32)
+    sent_projection = projection(after(other, packet))
+    sent_output = output(after(other, sent_projection))
+    own_projection = projection(after(spot, sent_output))
+    own_output = output(after(spot, own_projection))
+    got_projection = swap_weights(sent_projection, NZ * NC)
+    got_output = swap_weights(sent_output, NZ * NC)
+
+    rows = PER_HEAD + SHARED
+    kept, sent, box, value_up = call(
+        product_kernel,
+        [
+            shape(rows, 128, dtype=F32),
+            shape(rows, 128),
+            shape(2 * GROUP, 2 * KV, 128),
+            shape(128, 128),
+        ],
         spot,
-        wq_codes,
-        wq_scales,
-        wkv_codes.T,
-        wkv_scales.T,
+        gathered,
+        own_projection,
+        got_projection,
+        own_output,
+        got_output,
         scratch=[
-            pltpu.VMEM((FEATURES, 128), BF16),
-            pltpu.VMEM((256, 128), BF16),
-            pltpu.VMEM((KV, FEATURES), BF16),
-            pltpu.VMEM((KV, 256), BF16),
-            pltpu.VMEM((256, 128), F32),
-            pltpu.VMEM((KV, FEATURES), F32),
-            pltpu.SemaphoreType.DMA((4,)),
+            pltpu.VMEM((BLOCKS * PACKET, 128), BF16),
+            *[pltpu.VMEM((BLOCKS * (128 + KV), 128), BF16)] * 2,
+            *[pltpu.VMEM((BLOCKS * 128, 128), BF16)] * 2,
+            pltpu.SemaphoreType.DMA((5,)),
         ],
         megabytes=56,
         held=True,
     )
-    outputs = call(
-        output_kernel,
-        [shape(BLOCKS * 128, 128)] * 4,
-        after(spot, *projections),
-        wo_codes,
-        wo_scales,
-        scratch=[
-            pltpu.VMEM((128, FEATURES), BF16),
-            pltpu.VMEM((4, FEATURES), BF16),
-            pltpu.SemaphoreType.DMA((2,)),
-        ],
-        megabytes=56,
-        held=True,
-    )
-    projections = [projections[0]] + [swap_weights(p, mask) for p, mask in zip(projections[1:], masks)]
-    outputs = [outputs[0]] + [swap_weights(p, mask) for p, mask in zip(outputs[1:], masks)]
-
-    rows = 2 * PER_HEAD + SHARED + 64
-    kept, sent, box = call(
-        product_kernel,
-        [shape(rows, 128, dtype=F32), shape(rows, 128), shape(2 * GROUP, 128, 128)],
-        spot,
-        gathered,
-        *projections,
-        *outputs,
-        megabytes=56,
-    )
+    got = swap(sent, NZ * NC)
     box = exchange(box, "fsdp", BOX_GROUPS)
-    rows = PER_HEAD + SHARED
-    kept, sent, value_up = call(
-        middle_kernel,
-        [shape(rows, 128, dtype=F32), shape(rows, 128), shape(128, 128)],
-        spot,
-        kept,
-        swap(sent, 1),
-    )
-    got = swap(sent, NZ * NC)
 
     cosine, sine = rope_tables()
     slices, up, normed = call(

time: 194 us -> 184 us (0.948)
  starting transfers between devices: 45.7 us -> 18 us
  waiting for transfers between devices: 55 us -> 67.7 us
  Pallas kernels: 20.9 us -> 26.2 us
    all_gather x1, waiting for transfers between devices: 4.07 us -> 25.3 us  [local(): lax.all_gather(packet, 'fsdp', axis=0, tiled=True, axis_index_groups=HALF...]
    ppermute x4 -> x1, starting transfers between devices: 17.5 us -> 4.79 us  [swap(): lax.ppermute(value, 'fsdp', [(i, i ^ mask) for i in range(NX * NZ * NC)])]
    all_to_all x1, starting transfers between devices: 14.6 us -> 6.03 us  [exchange(): return lax.all_to_all(value, axis, 0, 0, axis_index_groups=groups)]
    ppermute x4 -> x2, waiting for transfers between devices: 42.5 us -> 35.3 us  [swap_weights(): return lax.ppermute(value, ('dp', 'fsdp'), pairs)]
    ppermute x4 -> x2, starting transfers between devices: 13.5 us -> 7.15 us  [swap_weights(): return lax.ppermute(value, ('dp', 'fsdp'), pairs)]
    pallas_call x10 -> x11, Pallas kernels: 20.9 us -> 26.2 us  [call(): pl.pallas_call(body, out_shape=outs, in_specs=specs, out_specs=[VMEM] * l...]
    ppermute x4 -> x1, waiting for transfers between devices: 8.45 us -> 7.09 us  [swap(): lax.ppermute(value, 'fsdp', [(i, i ^ mask) for i in range(NX * NZ * NC)])]
  transfers between devices with their start and end apart: 10 -> 5, of which waited for: 5 -> 3; matrix products, arithmetic and copies ran while one was open for 0% -> 1% of each run, Pallas kernels for 5% -> 8%
where the time goes in v4:
time: 184 us; the launch traced here: 183 us
  waiting for transfers between devices  67.7 us (37%)
  blocking collectives  53.6 us (29%)
  Pallas kernels  26.2 us (14%)
  starting transfers between devices  18 us (10%)
  between operations  14.3 us (8%)
    all_to_all x4, blocking collectives, exchange(): return lax.all_to_all(value, axis, 0, 0, axis_index_groups=groups)  53.6 us
    ppermute x2, waiting for transfers between devices, swap_weights(): return lax.ppermute(value, ('dp', 'fsdp'), pairs)  35.3 us
    pallas_call x11, Pallas kernels, call(): pl.pallas_call(body, out_shape=outs, in_specs=specs, out_specs=[VMEM] * l...  26.2 us
    all_gather x1, waiting for transfers between devices, local(): lax.all_gather(packet, 'fsdp', axis=0, tiled=True, axis_index_groups=HALF...  25.3 us
    ppermute x2, starting transfers between devices, swap_weights(): return lax.ppermute(value, ('dp', 'fsdp'), pairs)  7.15 us
    ppermute x1, waiting for transfers between devices, swap(): lax.ppermute(value, 'fsdp', [(i, i ^ mask) for i in range(NX * NZ * NC)])  7.09 us
    all_to_all x1, starting transfers between devices, exchange(): return lax.all_to_all(value, axis, 0, 0, axis_index_groups=groups)  6.03 us
    ppermute x1, starting transfers between devices, swap(): lax.ppermute(value, 'fsdp', [(i, i ^ mask) for i in range(NX * NZ * NC)])  4.79 us
  transfers between devices with their start and end apart: 5, of which 3 were waited for; matrix products, arithmetic and copies ran while one was open for 1% of the time, Pallas kernels for 8%

profile of v4, /device:TPU:1, one launch (start us, length us, event | category | flops | bytes accessed | tf_op | source)
XLA Modules:
  0.0 182.8 jit_solution(10721350449929301391)
XLA Ops:
  7.2 0.0 all-gather.2.cloned.1.call-start
  7.2 1.8 shard_map.210
  9.1 1.2 fusion
  10.3 3.7 %shard_map.211 = bf16[5120,128]{1,0:T(8,128)(2,1)} custom-call(s32[3]{0:T(128)} %get-tuple-element.22.place_ref, bf16[8192,128]{1,0:T(8,128)(2,1)} %rest_0_.6, bf16[256,128]{1,0:T(8,128)(2,1)} %rest_1_.6, bf16[32,8192]{1,0:T(8,128)(2,1)} %bitcast.12, bf16[32,256]{1,0:T(8,128)(2,1)} %bitcast.14), custom_call_target="tpu_custom_call" | custom-call | tf_op jit(solution)/shard_map/pallas_call | solution.py:97
  14.0 5.2 %collective-permute-start = (bf16[5120,128]{1,0:T(8,128)(2,1)}, bf16[5120,128]{1,0:T(8,128)(2,1)S(1)}, u32[]{:S(2)}, u32[]{:S(2)}) collective-permute-start(bf16[5120,128]{1,0:T(8,128)(2,1)} %shard_map.211), channel_id=1, source_target_pairs={{0,96},{1,97},{2,98},{3,99},{4,100},{5,101},{6,102},{7,103},{8,104... | collective-permute-start | bytes 3932168 | tf_op jit(solution)/shard_map/ppermute | solution.py:59
  19.2 3.2 %shard_map.212 = bf16[4096,128]{1,0:T(8,128)(2,1)} custom-call(s32[3]{0:T(128)} %get-tuple-element.22.place_ref, bf16[128,8192]{1,0:T(8,128)(2,1)} %rest_0_.7, bf16[4,8192]{1,0:T(4,128)(2,1)} %rest_1_.7), custom_call_target="tpu_custom_call" | custom-call | tf_op jit(solution)/shard_map/pallas_call | solution.py:97
  22.5 1.9 %collective-permute-start.1 = (bf16[4096,128]{1,0:T(8,128)(2,1)}, bf16[4096,128]{1,0:T(8,128)(2,1)S(1)}, u32[]{:S(2)}, u32[]{:S(2)}) collective-permute-start(bf16[4096,128]{1,0:T(8,128)(2,1)} %shard_map.212), channel_id=1, source_target_pairs={{0,96},{1,97},{2,98},{3,99},{4,100},{5,101},{6,102},{7,103},{8,104... | collective-permute-start | bytes 3145736 | tf_op jit(solution)/shard_map/ppermute | solution.py:59
  24.4 3.7 %shard_map.213.refs_1_ = bf16[5120,128]{1,0:T(8,128)(2,1)} custom-call(s32[3]{0:T(128)} %get-tuple-element.24.place_ref, bf16[8192,128]{1,0:T(8,128)(2,1)} %rest_0_.6, bf16[256,128]{1,0:T(8,128)(2,1)} %rest_1_.6, bf16[32,8192]{1,0:T(8,128)(2,1)} %bitcast.13, bf16[32,256]{1,0:T(8,128)(2,1)} %bitcast.15), custom_call_target="tpu_custom_call" | custom-call | tf_op jit(solution)/shard_map/pallas_call | solution.py:97
  28.1 3.3 %shard_map.214.refs_3_ = bf16[4096,128]{1,0:T(8,128)(2,1)} custom-call(s32[3]{0:T(128)} %get-tuple-element.24.place_ref, bf16[128,8192]{1,0:T(8,128)(2,1)} %rest_0_.7, bf16[4,8192]{1,0:T(4,128)(2,1)} %rest_1_.7), custom_call_target="tpu_custom_call" | custom-call | tf_op jit(solution)/shard_map/pallas_call | solution.py:97
  31.5 35.2 %collective-permute-done.1.refs_4_ = bf16[4096,128]{1,0:T(8,128)(2,1)S(1)} collective-permute-done((bf16[4096,128]{1,0:T(8,128)(2,1)}, bf16[4096,128]{1,0:T(8,128)(2,1)S(1)}, u32[]{:S(2)}, u32[]{:S(2)}) %collective-permute-start.1) | collective-permute-done | bytes 1048608 | tf_op jit(solution)/shard_map/ppermute | solution.py:59
  66.8 25.3 %all-gather.2.cloned.1.call-done.refs_0_ = bf16[21504,128]{1,0:T(8,128)(2,1)} async-done(((bf16[672,128]{1,0:T(8,128)(2,1)}), bf16[21504,128]{1,0:T(8,128)(2,1)}) %all-gather.2.cloned.1.call-update) | async-done | bytes 5505040 | tf_op jit(solution)/shard_map/all_gather | solution.py:419
  92.1 8.0 %shard_map.215 = (f32[784,128]{1,0:T(8,128)}, bf16[784,128]{1,0:T(8,128)(2,1)}, bf16[16,64,128]{2,1,0:T(8,128)(2,1)}, bf16[128,128]{1,0:T(8,128)(2,1)}) custom-call(s32[3]{0:T(128)} %get-tuple-element.24.place_ref, bf16[21504,128]{1,0:T(8,128)(2,1)} %all-gather.2.cloned.1.call-done.refs_0_, bf16[5120,128]{1,0:T(8,128)(2,1)} %shard_map.213.refs_1_, ...), custom_call_target="tpu_custom_call" | custom-call | tf_op jit(solution)/shard_map/pallas_call | solution.py:97
  100.1 6.0 %all-to-all-start = ((bf16[16,64,128]{2,1,0:T(8,128)(2,1)}), bf16[16,64,128]{2,1,0:T(8,128)(2,1)S(1)}, u32[]{:S(2)}, u32[]{:S(2)}) async-start(bf16[16,64,128]{2,1,0:T(8,128)(2,1)} %get-tuple-element.27), calls=%async_computation | async-start | bytes 524288 | tf_op jit(solution)/shard_map/all_to_all | solution.py:63
  106.2 4.8 %collective-permute-start.2 = (bf16[784,128]{1,0:T(8,128)(2,1)}, bf16[784,128]{1,0:T(8,128)(2,1)S(1)}, u32[]{:S(2)}, u32[]{:S(2)}) collective-permute-start(bf16[784,128]{1,0:T(8,128)(2,1)} %get-tuple-element.26), channel_id=1, source_target_pairs={{0,32},{1,33},{2,34},{3,35},{4,36},{5,37},{6,38},{7,39},{8,40},{9,... | collective-permute-start | bytes 602120 | tf_op jit(solution)/shard_map/ppermute | solution.py:50
  111.0 7.1 %collective-permute-done.2.got = bf16[784,128]{1,0:T(8,128)(2,1)S(1)} collective-permute-done((bf16[784,128]{1,0:T(8,128)(2,1)}, bf16[784,128]{1,0:T(8,128)(2,1)S(1)}, u32[]{:S(2)}, u32[]{:S(2)}) %collective-permute-start.2) | collective-permute-done | bytes 200736 | tf_op jit(solution)/shard_map/ppermute | solution.py:50
  118.1 1.0 copy-done
  119.1 0.8 copy-done.6
  119.9 1.5 shard_map.216
  121.4 10.3 %all_to_all.25.parts = bf16[8,48,128]{2,1,0:T(8,128)(2,1)S(1)} all-to-all(bf16[8,48,128]{2,1,0:T(8,128)(2,1)S(1)} %get-tuple-element.30), channel_id=1, replica_groups={{0,1,2,3,4,5,6,7},{8,9,10,11,12,13,14,15},{16,17,18,19,20,21,22,23},{24..., dimensions={0} | all-to-all | bytes 196608 | tf_op jit(solution)/shard_map/all_to_all | solution.py:63
  131.8 21.8 %all_to_all.26.parts = bf16[8,32,128]{2,1,0:T(8,128)(2,1)S(1)} all-to-all(bf16[8,32,128]{2,1,0:T(8,128)(2,1)S(1)} %get-tuple-element.31), channel_id=1, replica_groups={{0,8,16,24,32,40,48,56},{1,9,17,25,33,41,49,57},{2,10,18,26,34,42,50,58..., dimensions={0} | all-to-all | bytes 131072 | tf_op jit(solution)/shard_map/all_to_all | solution.py:63
  153.6 9.6 %all_to_all.27.low = bf16[8,32,128]{2,1,0:T(8,128)(2,1)S(1)} all-to-all(bf16[8,32,128]{2,1,0:T(8,128)(2,1)S(1)} %shard_map.218), channel_id=1, replica_groups={{0,1,2,3,4,5,6,7},{8,9,10,11,12,13,14,15},{16,17,18,19,20,21,22,23},{24..., dimensions={0} | all-to-all | bytes 131072 | tf_op jit(solution)/shard_map/all_to_all | solution.py:63
  163.2 0.2 shard_map.219
  163.4 11.8 %all_to_all.28.parts = bf16[8,208,128]{2,1,0:T(8,128)(2,1)S(1)} all-to-all(bf16[8,208,128]{2,1,0:T(8,128)(2,1)S(1)} %shard_map.219), channel_id=1, replica_groups=mesh['dp'=8,'fsdp'=64] {'dp'}, dimensions={0} | all-to-all | bytes 851968 | tf_op jit(solution)/shard_map/all_to_all | solution.py:63
  175.2 0.7 shard_map.220
  (27 shorter events, 0.1 us)
Async XLA Ops:
  7.2 85.0 %all-gather.2.cloned.1.call-start = ((), (), s32[]{:S(2)}) async-start(), calls=%async_computation.5 | async-start | bytes 5677056 | tf_op jit(solution)/shard_map/all_gather | solution.py:419
  14.0 52.8 %collective-permute-start = (bf16[5120,128]{1,0:T(8,128)(2,1)}, bf16[5120,128]{1,0:T(8,128)(2,1)S(1)}, u32[]{:S(2)}, u32[]{:S(2)}) collective-permute-start(bf16[5120,128]{1,0:T(8,128)(2,1)} %shard_map.211), channel_id=1, source_target_pairs={{0,96},{1,97},{2,98},{3,99},{4,100},{5,101},{6,102},{7,103},{8,104... | collective-permute-start | bytes 3932168 | tf_op jit(solution)/shard_map/ppermute | solution.py:59
  22.5 44.3 %collective-permute-start.1 = (bf16[4096,128]{1,0:T(8,128)(2,1)}, bf16[4096,128]{1,0:T(8,128)(2,1)S(1)}, u32[]{:S(2)}, u32[]{:S(2)}) collective-permute-start(bf16[4096,128]{1,0:T(8,128)(2,1)} %shard_map.212), channel_id=1, source_target_pairs={{0,96},{1,97},{2,98},{3,99},{4,100},{5,101},{6,102},{7,103},{8,104... | collective-permute-start | bytes 3145736 | tf_op jit(solution)/shard_map/ppermute | solution.py:59
  31.4 86.6 %copy-start.1 = (bf16[256,128]{1,0:T(8,128)(2,1)S(1)}, bf16[256,128]{1,0:T(8,128)(2,1)}, u32[]{:S(2)}) copy-start(bf16[256,128]{1,0:T(8,128)(2,1)} %hidden.1) | copy-start | bytes 196612
  31.5 86.6 %copy-start.2 = (f32[256,64]{1,0:T(8,128)S(1)}, f32[256,64]{1,0:T(8,128)}, u32[]{:S(2)}) copy-start(f32[256,64]{1,0:T(8,128)} %constant.60.clone.cosine) | copy-start | bytes 196612
  31.5 86.6 %copy-start.3 = (f32[256,64]{1,0:T(8,128)S(1)}, f32[256,64]{1,0:T(8,128)}, u32[]{:S(2)}) copy-start(f32[256,64]{1,0:T(8,128)} %constant.61.clone.sine) | copy-start | bytes 196612
  31.5 86.6 %copy-start.4 = (f32[64,256]{1,0:T(8,128)S(1)}, f32[64,256]{1,0:T(8,128)}, u32[]{:S(2)}) copy-start(f32[64,256]{1,0:T(8,128)} %constant.62.clone.cosine_t) | copy-start | bytes 196612
  31.5 86.6 %copy-start.5 = (f32[64,256]{1,0:T(8,128)S(1)}, f32[64,256]{1,0:T(8,128)}, u32[]{:S(2)}) copy-start(f32[64,256]{1,0:T(8,128)} %constant.63.clone.sine_t) | copy-start | bytes 196612
  31.5 86.6 %copy-start.7 = (bf16[64,128]{1,0:T(8,128)(2,1)S(1)}, bf16[64,128]{1,0:T(8,128)(2,1)}, u32[]{:S(2)}) copy-start(bf16[64,128]{1,0:T(8,128)(2,1)} %query_up.1) | copy-start | bytes 49156
  31.5 86.6 %copy-start.8 = (bf16[128]{0:T(256)(128)(2,1)S(1)}, bf16[128]{0:T(256)(128)(2,1)}, u32[]{:S(2)}) copy-start(bf16[128]{0:T(256)(128)(2,1)} %param.22) | copy-start | bytes 772
  31.5 86.6 %copy-start.9 = (s32[1,256]{1,0:T(1,128)S(1)}, s32[1,256]{1,0:T(1,128)}, u32[]{:S(2)}) copy-start(s32[1,256]{1,0:T(1,128)} %snapshot.1) | copy-start | bytes 3076
  66.8 25.4 %copy-start.11 = (bf16[4096,128]{1,0:T(8,128)(2,1)}, bf16[4096,128]{1,0:T(8,128)(2,1)S(1)}, u32[]{:S(2)}) copy-start(bf16[4096,128]{1,0:T(8,128)(2,1)S(1)} %collective-permute-done.1.refs_4_) | copy-start | bytes 3145732
  66.8 25.3 %copy-start.10 = (bf16[5120,128]{1,0:T(8,128)(2,1)}, bf16[5120,128]{1,0:T(8,128)(2,1)S(1)}, u32[]{:S(2)}) copy-start(bf16[5120,128]{1,0:T(8,128)(2,1)S(1)} %collective-permute-done.refs_2_) | copy-start | bytes 3932164
  100.1 17.9 %all-to-all-start = ((bf16[16,64,128]{2,1,0:T(8,128)(2,1)}), bf16[16,64,128]{2,1,0:T(8,128)(2,1)S(1)}, u32[]{:S(2)}, u32[]{:S(2)}) async-start(bf16[16,64,128]{2,1,0:T(8,128)(2,1)} %get-tuple-element.27), calls=%async_computation | async-start | bytes 524288 | tf_op jit(solution)/shard_map/all_to_all | solution.py:63
  106.2 11.9 %collective-permute-start.2 = (bf16[784,128]{1,0:T(8,128)(2,1)}, bf16[784,128]{1,0:T(8,128)(2,1)S(1)}, u32[]{:S(2)}, u32[]{:S(2)}) collective-permute-start(bf16[784,128]{1,0:T(8,128)(2,1)} %get-tuple-element.26), channel_id=1, source_target_pairs={{0,32},{1,33},{2,34},{3,35},{4,36},{5,37},{6,38},{7,39},{8,40},{9,... | collective-permute-start | bytes 602120 | tf_op jit(solution)/shard_map/ppermute | solution.py:50
  118.1 1.0 copy-start
  119.1 0.8 copy-start.6
Sparse Core Ops, SparseCore 0:
  10.1 81.9 all-gather.1

commit v5 on v4

--- a/solution.py
+++ b/solution.py
@@ -40,9 +40,9 @@
 BOX_GROUPS = [
     [place(a, 4 * b + i, c) for a in range(NX) for i in range(4) for c in range(NC)] for b in range(4)
 ]
-NEAR_GROUPS = [[GROUP * g + i for i in range(GROUP)] for g in range(8)]
+NEAR_GROUPS = [[GROUP * g + i for i in range(GROUP)][::-1] for g in range(8)]
 FAR_GROUPS = [
-    [place(a, z + 4 * k, c) for a in range(NX) for k in range(4)] for z in range(4) for c in range(NC)
+    [place(a, z + 4 * k, c) for a in range(NX) for k in (2, 3, 0, 1)] for z in range(4) for c in range(NC)
 ]
 
 
@@ -91,8 +91,12 @@
 
 def call(body, outs, *operands, scratch=(), megabytes=32, held=False):
     specs = [SMEM if o.dtype == jnp.int32 and o.ndim == 1 else VMEM for o in operands]
-    if held:
-        specs = [spec if spec is SMEM else pl.BlockSpec(memory_space=pl.ANY) for spec in specs]
+    if held is not False:
+        here = range(len(operands)) if held is True else held
+        specs = [
+            pl.BlockSpec(memory_space=pl.ANY) if i in here and spec is not SMEM else spec
+            for i, spec in enumerate(specs)
+        ]
     many = isinstance(outs, (list, tuple))
     return pl.pallas_call(
         body,
@@ -207,36 +211,36 @@
     lax.fori_loop(0, BLOCKS, step, 0, unroll=4)
 
 
-def product_kernel(place_ref, *refs):
-    sources, (kept, sent, box, value_up), held, sems = refs[:5], refs[5:9], refs[9:14], refs[14]
-    copies = [pltpu.make_async_copy(a, b, sems.at[i]) for i, (a, b) in enumerate(zip(sources, held))]
-    for copy in copies:
+def product_kernel(place_ref, gathered_at, *refs):
+    weights, outputs, (kept, sent, box, value_up), gathered, sems = refs[:2], refs[2:4], refs[4:8], refs[8], refs[9]
+
+    def start(source, target, i):
+        copy = pltpu.make_async_copy(source, target, sems.at[i])
         copy.start()
-    gathered, weights, outputs = held[0], held[1:3], held[3:5]
-
-    def rows(start, number):
-        return [gathered[b * PACKET + start : b * PACKET + start + number, :] for b in range(BLOCKS)]
-
-    copies[0].wait()
+        return copy
+
+    def part(first, number):
+        return pl.ds(0, BLOCKS), pl.ds(first, number), slice(None)
+
+    x_copy = start(gathered_at.at[part(0, LENGTH)], gathered.at[part(0, LENGTH)], 0)
+    rest = part(LENGTH, GRADS_AT - LENGTH)
+    a_copy = start(gathered_at.at[rest], gathered.at[rest], 1)
+    g_copy = start(gathered_at.at[part(GRADS_AT, LENGTH)], gathered.at[part(GRADS_AT, LENGTH)], 2)
+
+    def rows(first, number):
+        return [gathered[b, first : first + number, :] for b in range(BLOCKS)]
+
+    x_copy.wait()
     inputs = jnp.concatenate(rows(0, LENGTH), axis=1)
-    low = contract(inputs, jnp.concatenate(rows(DOWNS_AT, 2 * RANK), axis=1), 1, 1)
-    squares = sum(r.astype(F32) for r in rows(SQUARES_AT, 16))
-    squares = squares[0:2] + squares[2:4]
-    group = place_ref[1] // 4 * GROUP
-    for i in range(GROUP):
-        at = pl.multiple_of((group + i) * PACKET + COLUMNS_AT, 16)
-        value_up[16 * i : 16 * i + 16, :] = gathered[pl.ds(at, 16), :]
-    copies[1].wait()
-    copies[2].wait()
     q = contract(inputs, jnp.concatenate([w[:HALF, :] for w in weights], axis=1), 1, 0)
-    kv_weights = jnp.concatenate(
-        [
+    a_copy.wait()
+    narrow = [jnp.concatenate(rows(DOWNS_AT, 2 * RANK), axis=1)]
+    for w in weights:
+        narrow.append(
             jnp.concatenate([w[HALF + b * KV : HALF + (b + 1) * KV, :] for b in range(BLOCKS)], axis=1)
-            for w in weights
-        ],
-        axis=0,
-    )
-    kv = contract(kv_weights, inputs, 1, 1).astype(BF16)
+        )
+    narrow = contract(inputs, jnp.concatenate(narrow, axis=0), 1, 1)
+    low, kv = narrow[:, : 2 * RANK], narrow[:, 2 * RANK :].T.astype(BF16)
     at_zero = place_ref[0] == 0
     for a in range(NX):
         mine = at_zero if a == 0 else jnp.logical_not(at_zero)
@@ -244,8 +248,12 @@
         whole = jnp.concatenate([whole[:, :128], whole[:, 128:]], axis=0)
         for i in range(GROUP):
             box[GROUP * a + i] = whole
-    copies[3].wait()
-    copies[4].wait()
+    squares = sum(r.astype(F32) for r in rows(SQUARES_AT, 16))
+    squares = squares[0:2] + squares[2:4]
+    group = place_ref[1] // 4 * GROUP
+    for i in range(GROUP):
+        value_up[16 * i : 16 * i + 16, :] = gathered[group + i, COLUMNS_AT:GRADS_AT, :]
+    g_copy.wait()
     o_weights = jnp.concatenate(
         [
             jnp.concatenate([w[b * 128 : (b + 1) * 128, :] for b in range(BLOCKS)], axis=1)
@@ -342,8 +350,8 @@
     ).astype(BF16)
     rows = LENGTH // GROUP
     for i in range(GROUP):
-        out[i, :rows, :] = grad_low[i * rows : (i + 1) * rows]
-        out[i, rows:, :] = slices[16 * i : 16 * i + 16]
+        out[GROUP - 1 - i, :rows, :] = grad_low[i * rows : (i + 1) * rows]
+        out[GROUP - 1 - i, rows:, :] = slices[16 * i : 16 * i + 16]
 
 
 def near_kernel(parts, low, value):
@@ -361,7 +369,7 @@
 
 
 def rows_kernel(normed, low, up, value, out):
-    whole = jnp.concatenate([low[i] for i in range(GROUP)], axis=0)
+    whole = jnp.concatenate([low[GROUP - 1 - i] for i in range(GROUP)], axis=0)
     rows = contract(normed[...], whole, 0, 0).astype(BF16)
     last = jnp.concatenate([up[...], value[...]], axis=0).astype(BF16)
     for i in range(8):
@@ -436,7 +444,7 @@
                 pltpu.VMEM((KV, HALF), F32),
                 pltpu.SemaphoreType.DMA((4,)),
             ],
-            megabytes=56,
+            megabytes=12,
             held=True,
         )
 
@@ -452,7 +460,7 @@
                 pltpu.VMEM((4, HALF), BF16),
                 pltpu.SemaphoreType.DMA((2,)),
             ],
-            megabytes=56,
+            megabytes=12,
             held=True,
         )
 
@@ -465,6 +473,7 @@
     got_output = swap_weights(sent_output, NZ * NC)
 
     rows = PER_HEAD + SHARED
+    gathered = gathered.reshape(BLOCKS, PACKET, 128)
     kept, sent, box, value_up = call(
         product_kernel,
         [
@@ -480,13 +489,11 @@
         own_output,
         got_output,
         scratch=[
-            pltpu.VMEM((BLOCKS * PACKET, 128), BF16),
-            *[pltpu.VMEM((BLOCKS * (128 + KV), 128), BF16)] * 2,
-            *[pltpu.VMEM((BLOCKS * 128, 128), BF16)] * 2,
-            pltpu.SemaphoreType.DMA((5,)),
+            pltpu.VMEM((BLOCKS, PACKET, 128), BF16),
+            pltpu.SemaphoreType.DMA((3,)),
         ],
-        megabytes=56,
-        held=True,
+        megabytes=50,
+        held=(1,),
     )
     got = swap(sent, NZ * NC)
     box = exchange(box, "fsdp", BOX_GROUPS)
@@ -531,7 +538,7 @@
             shape(RANK, HEAD, dtype=F32),
             shape(16, RANK, dtype=F32),
         ],
-        exchange(mine, "dp"),
+        exchange(mine, "dp", [list(range(7, -1, -1))]),
     )
     return grad_a_query.T, query_up, grad_a_value.T, value.T
 

time: 184 us -> 174 us (0.946)
  Pallas kernels: 26.2 us -> 16.2 us
  blocking collectives: 53.6 us -> 46.5 us
  waiting for transfers between devices: 67.7 us -> 71.7 us
  local copies, waits for them, and re-layouts: 1.81 us -> 5.35 us
    pallas_call x11, Pallas kernels: 26.2 us -> 16.2 us  [call(): pl.pallas_call(body, out_shape=outs, in_specs=specs, out_specs=[VMEM] * l...]
    all_to_all x4, blocking collectives: 53.6 us -> 46.5 us  [exchange(): return lax.all_to_all(value, axis, 0, 0, axis_index_groups=groups)]
    ppermute x2, waiting for transfers between devices: 35.3 us -> 40.7 us  [swap_weights(): return lax.ppermute(value, ('dp', 'fsdp'), pairs)]
    unnamed x24 -> x36, local copies, waits for them, and re-layouts: 1.81 us -> 5.35 us
  transfers between devices with their start and end apart: 5 -> 5, of which waited for: 3 -> 3; matrix products, arithmetic and copies ran while one was open for 1% -> 0% of each run, Pallas kernels for 8% -> 3%
where the time goes in v5:
time: 174 us; the launch traced here: 173 us
  waiting for transfers between devices  71.7 us (41%)
  blocking collectives  46.5 us (27%)
  starting transfers between devices  18.2 us (10%)
  Pallas kernels  16.2 us (9%)
  between operations  14.3 us (8%)
  local copies, waits for them, and re-layouts  5.35 us (3%)
    all_to_all x4, blocking collectives, exchange(): return lax.all_to_all(value, axis, 0, 0, axis_index_groups=groups)  46.5 us
    ppermute x2, waiting for transfers between devices, swap_weights(): return lax.ppermute(value, ('dp', 'fsdp'), pairs)  40.7 us
    all_gather x1, waiting for transfers between devices, local(): lax.all_gather(packet, 'fsdp', axis=0, tiled=True, axis_index_groups=HALF...  24.1 us
    pallas_call x11, Pallas kernels, call(): pl.pallas_call(body, out_shape=outs, in_specs=specs, out_specs=[VMEM] * l...  16.2 us
    ppermute x2, starting transfers between devices, swap_weights(): return lax.ppermute(value, ('dp', 'fsdp'), pairs)  7.27 us
    ppermute x1, waiting for transfers between devices, swap(): lax.ppermute(value, 'fsdp', [(i, i ^ mask) for i in range(NX * NZ * NC)])  6.86 us
    all_to_all x1, starting transfers between devices, exchange(): return lax.all_to_all(value, axis, 0, 0, axis_index_groups=groups)  6.11 us
    unnamed x36, local copies, waits for them, and re-layouts  5.35 us
  transfers between devices with their start and end apart: 5, of which 3 were waited for; matrix products, arithmetic and copies ran while one was open for 0% of the time, Pallas kernels for 3%

profile of v5, /device:TPU:1, one launch (start us, length us, event | category | flops | bytes accessed | tf_op | source)
XLA Modules:
  0.0 173.1 jit_solution(3659404146788257951)
XLA Ops:
  7.2 1.8 %shard_map.210 = bf16[672,128]{1,0:T(8,128)(2,1)} custom-call(bf16[256,128]{1,0:T(8,128)(2,1)} %hidden.1, bf16[1,128]{1,0:T(2,128)(2,1)} %bitcast.15, bf16[64,128]{1,0:T(8,128)(2,1)} %a_query_at.1, bf16[64,128]{1,0:T(8,128)(2,1)} %a_value_at.1, bf16[16,64]{1,0:T(8,128)(2,1)} %bitcast.18, bf16[256,128]{1,0:T(8,128)(2,1)} %grad_at.1), custom_call_target="tpu_custom_call" | custom-call | tf_op jit(solution)/shard_map/pallas_call | solution.py:101
  9.1 0.7 fusion
  9.8 1.6 copy-done
  11.4 1.0 copy-done.4
  12.5 0.8 copy-done.6
  14.0 1.3 shard_map.211
  15.4 5.3 %collective-permute-start = (bf16[5120,128]{1,0:T(8,128)(2,1)S(1)}, bf16[5120,128]{1,0:T(8,128)(2,1)}, u32[]{:S(2)}, u32[]{:S(2)}) collective-permute-start(bf16[5120,128]{1,0:T(8,128)(2,1)S(1)} %shard_map.211), channel_id=1, source_target_pairs={{0,96},{1,97},{2,98},{3,99},{4,100},{5,101},{6,102},{7,103},{8,104... | collective-permute-start | bytes 3932168 | tf_op jit(solution)/shard_map/ppermute | solution.py:59
  20.8 1.0 shard_map.212
  21.8 1.9 %collective-permute-start.1 = (bf16[4096,128]{1,0:T(8,128)(2,1)S(1)}, bf16[4096,128]{1,0:T(8,128)(2,1)S(1)}, u32[]{:S(2)}, u32[]{:S(2)}) collective-permute-start(bf16[4096,128]{1,0:T(8,128)(2,1)S(1)} %shard_map.212), channel_id=1, source_target_pairs={{0,96},{1,97},{2,98},{3,99},{4,100},{5,101},{6,102},{7,103},{8,104... | collective-permute-start | bytes 3145736 | tf_op jit(solution)/shard_map/ppermute | solution.py:59
  23.8 1.3 shard_map.213.refs_0_
  25.1 1.1 copy-done.3
  26.2 1.0 shard_map.214.refs_2_
  27.3 40.7 %collective-permute-done.1.refs_3_ = bf16[4096,128]{1,0:T(8,128)(2,1)S(1)} collective-permute-done((bf16[4096,128]{1,0:T(8,128)(2,1)S(1)}, bf16[4096,128]{1,0:T(8,128)(2,1)S(1)}, u32[]{:S(2)}, u32[]{:S(2)}) %collective-permute-start.1) | collective-permute-done | bytes 1048608 | tf_op jit(solution)/shard_map/ppermute | solution.py:59
  68.0 24.1 %all-gather.2.cloned.1.call-done = bf16[21504,128]{1,0:T(8,128)(2,1)} async-done(((bf16[672,128]{1,0:T(8,128)(2,1)}), bf16[21504,128]{1,0:T(8,128)(2,1)}) %all-gather.2.cloned.1.call-update) | async-done | bytes 5505040 | tf_op jit(solution)/shard_map/all_gather | solution.py:427
  92.1 7.2 %shard_map.215 = (f32[784,128]{1,0:T(8,128)S(1)}, bf16[784,128]{1,0:T(8,128)(2,1)S(1)}, bf16[16,64,128]{2,1,0:T(8,128)(2,1)}, bf16[128,128]{1,0:T(8,128)(2,1)S(1)}) custom-call(s32[3]{0:T(128)S(1)} %get-tuple-element.24.place_ref, bf16[32,672,128]{2,1,0:T(8,128)(2,1)} %bitcast.17, bf16[5120,128]{1,0:T(8,128)(2,1)} %copy-done.3, ...), custom_call_target="tpu_custom_call" | custom-call | tf_op jit(solution)/shard_map/pallas_call | solution.py:101
  99.3 6.1 %all-to-all-start = ((bf16[16,64,128]{2,1,0:T(8,128)(2,1)}), bf16[16,64,128]{2,1,0:T(8,128)(2,1)S(1)}, u32[]{:S(2)}, u32[]{:S(2)}) async-start(bf16[16,64,128]{2,1,0:T(8,128)(2,1)} %get-tuple-element.27), calls=%async_computation | async-start | bytes 524288 | tf_op jit(solution)/shard_map/all_to_all | solution.py:63
  105.4 4.8 %collective-permute-start.2 = (bf16[784,128]{1,0:T(8,128)(2,1)S(1)}, bf16[784,128]{1,0:T(8,128)(2,1)S(1)}, u32[]{:S(2)}, u32[]{:S(2)}) collective-permute-start(bf16[784,128]{1,0:T(8,128)(2,1)S(1)} %get-tuple-element.26), channel_id=1, source_target_pairs={{0,32},{1,33},{2,34},{3,35},{4,36},{5,37},{6,38},{7,39},{8,40},{9,... | collective-permute-start | bytes 602120 | tf_op jit(solution)/shard_map/ppermute | solution.py:50
  110.2 6.9 %collective-permute-done.2.got = bf16[784,128]{1,0:T(8,128)(2,1)S(1)} collective-permute-done((bf16[784,128]{1,0:T(8,128)(2,1)S(1)}, bf16[784,128]{1,0:T(8,128)(2,1)S(1)}, u32[]{:S(2)}, u32[]{:S(2)}) %collective-permute-start.2) | collective-permute-done | bytes 200736 | tf_op jit(solution)/shard_map/ppermute | solution.py:50
  117.2 1.5 shard_map.216
  118.7 8.5 %all_to_all.25.parts = bf16[8,48,128]{2,1,0:T(8,128)(2,1)S(1)} all-to-all(bf16[8,48,128]{2,1,0:T(8,128)(2,1)S(1)} %get-tuple-element.30), channel_id=1, replica_groups={{7,6,5,4,3,2,1,0},{15,14,13,12,11,10,9,8},{23,22,21,20,19,18,17,16},{31..., dimensions={0} | all-to-all | bytes 196608 | tf_op jit(solution)/shard_map/all_to_all | solution.py:63
  127.3 17.2 %all_to_all.26.parts = bf16[8,32,128]{2,1,0:T(8,128)(2,1)S(1)} all-to-all(bf16[8,32,128]{2,1,0:T(8,128)(2,1)S(1)} %get-tuple-element.31), channel_id=1, replica_groups={{16,24,0,8,48,56,32,40},{17,25,1,9,49,57,33,41},{18,26,2,10,50,58,34,42..., dimensions={0} | all-to-all | bytes 131072 | tf_op jit(solution)/shard_map/all_to_all | solution.py:63
  144.5 9.2 %all_to_all.27.low = bf16[8,32,128]{2,1,0:T(8,128)(2,1)S(1)} all-to-all(bf16[8,32,128]{2,1,0:T(8,128)(2,1)S(1)} %shard_map.218), channel_id=1, replica_groups={{7,6,5,4,3,2,1,0},{15,14,13,12,11,10,9,8},{23,22,21,20,19,18,17,16},{31..., dimensions={0} | all-to-all | bytes 131072 | tf_op jit(solution)/shard_map/all_to_all | solution.py:63
  153.8 11.7 %all_to_all.28.parts = bf16[8,208,128]{2,1,0:T(8,128)(2,1)S(1)} all-to-all(bf16[8,208,128]{2,1,0:T(8,128)(2,1)S(1)} %shard_map.219), channel_id=1, replica_groups={{448,384,320,256,192,128,64,0},{449,385,321,257,193,129,65,1},{450,386,..., dimensions={0} | all-to-all | bytes 851968 | tf_op jit(solution)/shard_map/all_to_all | solution.py:63
  165.5 0.7 shard_map.220
  (39 shorter events, 1.1 us)
Async XLA Ops:
  7.2 84.9 %all-gather.2.cloned.1.call-start = ((), (), s32[]{:S(2)}) async-start(), calls=%async_computation.5 | async-start | bytes 5677056 | tf_op jit(solution)/shard_map/all_gather | solution.py:427
  9.0 11.7 %copy-start.8 = (bf16[4,8192]{1,0:T(4,128)(2,1)S(1)}, bf16[4,8192]{1,0:T(4,128)(2,1)}, u32[]{:S(2)}) copy-start(bf16[4,8192]{1,0:T(4,128)(2,1)} %rest_1_.7) | copy-start | bytes 196612
  9.8 1.6 copy-start
  11.4 1.0 copy-start.4
  12.5 0.8 copy-start.6
  13.3 0.7 copy-start.12
  14.0 6.7 %copy-start.2 = (bf16[128,8192]{1,0:T(8,128)(2,1)S(1)}, bf16[128,8192]{1,0:T(8,128)(2,1)}, u32[]{:S(2)}) copy-start(bf16[128,8192]{1,0:T(8,128)(2,1)} %rest_0_.7) | copy-start | bytes 6291460
  15.4 8.4 %copy-start.1 = (bf16[8192,128]{1,0:T(8,128)(2,1)S(1)}, bf16[8192,128]{1,0:T(8,128)(2,1)}, u32[]{:S(2)}) copy-start(bf16[8192,128]{1,0:T(8,128)(2,1)} %rest_0_.6) | copy-start | bytes 6291460
  15.4 8.4 %copy-start.5 = (bf16[8192,32]{0,1:T(8,128)(2,1)S(1)}, bf16[8192,32]{0,1:T(8,128)(2,1)}, u32[]{:S(2)}) copy-start(bf16[8192,32]{0,1:T(8,128)(2,1)} %param.25) | copy-start | bytes 1572868
  15.4 8.4 %copy-start.7 = (bf16[256,128]{1,0:T(8,128)(2,1)S(1)}, bf16[256,128]{1,0:T(8,128)(2,1)}, u32[]{:S(2)}) copy-start(bf16[256,128]{1,0:T(8,128)(2,1)} %rest_1_.6) | copy-start | bytes 196612
  15.4 52.6 %collective-permute-start = (bf16[5120,128]{1,0:T(8,128)(2,1)S(1)}, bf16[5120,128]{1,0:T(8,128)(2,1)}, u32[]{:S(2)}, u32[]{:S(2)}) collective-permute-start(bf16[5120,128]{1,0:T(8,128)(2,1)S(1)} %shard_map.211), channel_id=1, source_target_pairs={{0,96},{1,97},{2,98},{3,99},{4,100},{5,101},{6,102},{7,103},{8,104... | collective-permute-start | bytes 3932168 | tf_op jit(solution)/shard_map/ppermute | solution.py:59
  21.8 46.1 %collective-permute-start.1 = (bf16[4096,128]{1,0:T(8,128)(2,1)S(1)}, bf16[4096,128]{1,0:T(8,128)(2,1)S(1)}, u32[]{:S(2)}, u32[]{:S(2)}) collective-permute-start(bf16[4096,128]{1,0:T(8,128)(2,1)S(1)} %shard_map.212), channel_id=1, source_target_pairs={{0,96},{1,97},{2,98},{3,99},{4,100},{5,101},{6,102},{7,103},{8,104... | collective-permute-start | bytes 3145736 | tf_op jit(solution)/shard_map/ppermute | solution.py:59
  25.1 1.1 copy-start.3
  92.1 25.1 %copy-start.9 = (bf16[256,128]{1,0:T(8,128)(2,1)S(1)}, bf16[256,128]{1,0:T(8,128)(2,1)}, u32[]{:S(2)}) copy-start(bf16[256,128]{1,0:T(8,128)(2,1)} %hidden.1) | copy-start | bytes 196612
  92.1 25.1 %copy-start.10 = (f32[256,64]{1,0:T(8,128)S(1)}, f32[256,64]{1,0:T(8,128)}, u32[]{:S(2)}) copy-start(f32[256,64]{1,0:T(8,128)} %constant.60.clone.cosine) | copy-start | bytes 196612
  92.1 25.1 %copy-start.11 = (f32[256,64]{1,0:T(8,128)S(1)}, f32[256,64]{1,0:T(8,128)}, u32[]{:S(2)}) copy-start(f32[256,64]{1,0:T(8,128)} %constant.61.clone.sine) | copy-start | bytes 196612
  92.1 25.1 %copy-start.13 = (f32[64,256]{1,0:T(8,128)S(1)}, f32[64,256]{1,0:T(8,128)}, u32[]{:S(2)}) copy-start(f32[64,256]{1,0:T(8,128)} %constant.62.clone.cosine_t) | copy-start | bytes 196612
  92.1 25.1 %copy-start.14 = (f32[64,256]{1,0:T(8,128)S(1)}, f32[64,256]{1,0:T(8,128)}, u32[]{:S(2)}) copy-start(f32[64,256]{1,0:T(8,128)} %constant.63.clone.sine_t) | copy-start | bytes 196612
  92.1 25.1 %copy-start.15 = (bf16[64,128]{1,0:T(8,128)(2,1)S(1)}, bf16[64,128]{1,0:T(8,128)(2,1)}, u32[]{:S(2)}) copy-start(bf16[64,128]{1,0:T(8,128)(2,1)} %query_up.1) | copy-start | bytes 49156
  92.1 25.1 %copy-start.16 = (bf16[128]{0:T(256)(128)(2,1)S(1)}, bf16[128]{0:T(256)(128)(2,1)}, u32[]{:S(2)}) copy-start(bf16[128]{0:T(256)(128)(2,1)} %param.22) | copy-start | bytes 772
  92.1 25.1 %copy-start.17 = (s32[1,256]{1,0:T(1,128)S(1)}, s32[1,256]{1,0:T(1,128)}, u32[]{:S(2)}) copy-start(s32[1,256]{1,0:T(1,128)} %snapshot.1) | copy-start | bytes 3076
  99.3 17.8 %all-to-all-start = ((bf16[16,64,128]{2,1,0:T(8,128)(2,1)}), bf16[16,64,128]{2,1,0:T(8,128)(2,1)S(1)}, u32[]{:S(2)}, u32[]{:S(2)}) async-start(bf16[16,64,128]{2,1,0:T(8,128)(2,1)} %get-tuple-element.27), calls=%async_computation | async-start | bytes 524288 | tf_op jit(solution)/shard_map/all_to_all | solution.py:63
  105.4 11.7 %collective-permute-start.2 = (bf16[784,128]{1,0:T(8,128)(2,1)S(1)}, bf16[784,128]{1,0:T(8,128)(2,1)S(1)}, u32[]{:S(2)}, u32[]{:S(2)}) collective-permute-start(bf16[784,128]{1,0:T(8,128)(2,1)S(1)} %get-tuple-element.26), channel_id=1, source_target_pairs={{0,32},{1,33},{2,34},{3,35},{4,36},{5,37},{6,38},{7,39},{8,40},{9,... | collective-permute-start | bytes 602120 | tf_op jit(solution)/shard_map/ppermute | solution.py:50
Sparse Core Ops, SparseCore 0:
  10.1 81.8 all-gather.1

commit v6 on v5

--- a/solution.py
+++ b/solution.py
@@ -18,6 +18,7 @@
 LENGTH, HEAD, RANK, KV = 256, 128, 64, 32
 FEATURES = NX * NZ * NC * HEAD
 HALF = FEATURES // NX
+PARTS = 8
 BLOCKS = NZ * NC
 DOWNS_AT = LENGTH
 SQUARES_AT = DOWNS_AT + 2 * RANK
@@ -213,34 +214,36 @@
 
 def product_kernel(place_ref, gathered_at, *refs):
     weights, outputs, (kept, sent, box, value_up), gathered, sems = refs[:2], refs[2:4], refs[4:8], refs[8], refs[9]
-
-    def start(source, target, i):
-        copy = pltpu.make_async_copy(source, target, sems.at[i])
-        copy.start()
-        return copy
-
-    def part(first, number):
-        return pl.ds(0, BLOCKS), pl.ds(first, number), slice(None)
-
-    x_copy = start(gathered_at.at[part(0, LENGTH)], gathered.at[part(0, LENGTH)], 0)
-    rest = part(LENGTH, GRADS_AT - LENGTH)
-    a_copy = start(gathered_at.at[rest], gathered.at[rest], 1)
-    g_copy = start(gathered_at.at[part(GRADS_AT, LENGTH)], gathered.at[part(GRADS_AT, LENGTH)], 2)
-
-    def rows(first, number):
-        return [gathered[b, first : first + number, :] for b in range(BLOCKS)]
-
-    x_copy.wait()
-    inputs = jnp.concatenate(rows(0, LENGTH), axis=1)
-    q = contract(inputs, jnp.concatenate([w[:HALF, :] for w in weights], axis=1), 1, 0)
-    a_copy.wait()
-    narrow = [jnp.concatenate(rows(DOWNS_AT, 2 * RANK), axis=1)]
-    for w in weights:
-        narrow.append(
-            jnp.concatenate([w[HALF + b * KV : HALF + (b + 1) * KV, :] for b in range(BLOCKS)], axis=1)
-        )
-    narrow = contract(inputs, jnp.concatenate(narrow, axis=0), 1, 1)
+    each = BLOCKS // PARTS
+    copies = []
+    for k in range(PARTS):
+        part = pl.ds(k * each, each)
+        copies.append(pltpu.make_async_copy(gathered_at.at[part], gathered.at[part], sems.at[k]))
+        copies[-1].start()
+    q = narrow = ctx = squares = 0.0
+    for k in range(PARTS):
+        copies[k].wait()
+        blocks = range(k * each, (k + 1) * each)
+
+        def rows(first, number, blocks=blocks):
+            return jnp.concatenate([gathered[b, first : first + number, :] for b in blocks], axis=1)
+
+        def block_rows(ref, first, number, blocks=blocks):
+            return jnp.concatenate(
+                [ref[first + b * number : first + (b + 1) * number, :] for b in blocks], axis=1
+            )
+
+        inputs = rows(0, LENGTH)
+        span = slice(k * each * 128, (k + 1) * each * 128)
+        q += contract(inputs, jnp.concatenate([w[span, :] for w in weights], axis=1), 1, 0)
+        slim = [rows(DOWNS_AT, 2 * RANK)] + [block_rows(w, HALF, KV) for w in weights]
+        narrow += contract(inputs, jnp.concatenate(slim, axis=0), 1, 1)
+        wide = jnp.concatenate([block_rows(w, 0, 128) for w in outputs], axis=0)
+        ctx += contract(rows(GRADS_AT, LENGTH), wide, 1, 1)
+        for b in blocks:
+            squares += gathered[b, SQUARES_AT : SQUARES_AT + 16, :].astype(F32)
     low, kv = narrow[:, : 2 * RANK], narrow[:, 2 * RANK :].T.astype(BF16)
+    squares = squares[0:2] + squares[2:4]
     at_zero = place_ref[0] == 0
     for a in range(NX):
         mine = at_zero if a == 0 else jnp.logical_not(at_zero)
@@ -248,20 +251,9 @@
         whole = jnp.concatenate([whole[:, :128], whole[:, 128:]], axis=0)
         for i in range(GROUP):
             box[GROUP * a + i] = whole
-    squares = sum(r.astype(F32) for r in rows(SQUARES_AT, 16))
-    squares = squares[0:2] + squares[2:4]
     group = place_ref[1] // 4 * GROUP
     for i in range(GROUP):
         value_up[16 * i : 16 * i + 16, :] = gathered[group + i, COLUMNS_AT:GRADS_AT, :]
-    g_copy.wait()
-    o_weights = jnp.concatenate(
-        [
-            jnp.concatenate([w[b * 128 : (b + 1) * 128, :] for b in range(BLOCKS)], axis=1)
-            for w in outputs
-        ],
-        axis=0,
-    )
-    ctx = contract(jnp.concatenate(rows(GRADS_AT, LENGTH), axis=1), o_weights, 1, 1)
     high, rest = two_terms(squares)
     shared = jnp.concatenate([high.astype(F32), rest.astype(F32), jnp.zeros((12, 128), F32)], axis=0)
     for i, (out, cast) in enumerate(((kept, F32), (sent, BF16))):
@@ -490,7 +482,7 @@
         got_output,
         scratch=[
             pltpu.VMEM((BLOCKS, PACKET, 128), BF16),
-            pltpu.SemaphoreType.DMA((3,)),
+            pltpu.SemaphoreType.DMA((PARTS,)),
         ],
         megabytes=50,
         held=(1,),

time: 174 us -> 173 us (level)
  no operation moved by 1% of the time
where the time goes in v6:
time: 173 us
  waiting for transfers between devices  71.7 us (41%)
  blocking collectives  46.5 us (27%)
  starting transfers between devices  18.2 us (11%)
  Pallas kernels  15.8 us (9%)
  between operations  14.3 us (8%)
  local copies, waits for them, and re-layouts  5.35 us (3%)
    all_to_all x4, blocking collectives, exchange(): return lax.all_to_all(value, axis, 0, 0, axis_index_groups=groups)  46.5 us
    ppermute x2, waiting for transfers between devices, swap_weights(): return lax.ppermute(value, ('dp', 'fsdp'), pairs)  40.7 us
    all_gather x1, waiting for transfers between devices, local(): lax.all_gather(packet, 'fsdp', axis=0, tiled=True, axis_index_groups=HALF...  24.1 us
    pallas_call x11, Pallas kernels, call(): pl.pallas_call(body, out_shape=outs, in_specs=specs, out_specs=[VMEM] * l...  15.8 us
    ppermute x2, starting transfers between devices, swap_weights(): return lax.ppermute(value, ('dp', 'fsdp'), pairs)  7.27 us
    ppermute x1, waiting for transfers between devices, swap(): lax.ppermute(value, 'fsdp', [(i, i ^ mask) for i in range(NX * NZ * NC)])  6.86 us
    all_to_all x1, starting transfers between devices, exchange(): return lax.all_to_all(value, axis, 0, 0, axis_index_groups=groups)  6.11 us
    unnamed x36, local copies, waits for them, and re-layouts  5.35 us
  transfers between devices with their start and end apart: 5, of which 3 were waited for; matrix products, arithmetic and copies ran while one was open for 0% of the time, Pallas kernels for 3%

profile of v6, /device:TPU:1, one launch (start us, length us, event | category | flops | bytes accessed | tf_op | source)
XLA Modules:
  0.0 172.7 jit_solution(5008633504538372482)
XLA Ops:
  7.2 1.8 %shard_map.210 = bf16[672,128]{1,0:T(8,128)(2,1)} custom-call(bf16[256,128]{1,0:T(8,128)(2,1)} %hidden.1, bf16[1,128]{1,0:T(2,128)(2,1)} %bitcast.15, bf16[64,128]{1,0:T(8,128)(2,1)} %a_query_at.1, bf16[64,128]{1,0:T(8,128)(2,1)} %a_value_at.1, bf16[16,64]{1,0:T(8,128)(2,1)} %bitcast.18, bf16[256,128]{1,0:T(8,128)(2,1)} %grad_at.1), custom_call_target="tpu_custom_call" | custom-call | tf_op jit(solution)/shard_map/pallas_call | solution.py:102
  9.1 0.7 fusion
  9.8 1.6 copy-done
  11.4 1.0 copy-done.4
  12.5 0.8 copy-done.6
  14.0 1.3 shard_map.211
  15.4 5.3 %collective-permute-start = (bf16[5120,128]{1,0:T(8,128)(2,1)S(1)}, bf16[5120,128]{1,0:T(8,128)(2,1)}, u32[]{:S(2)}, u32[]{:S(2)}) collective-permute-start(bf16[5120,128]{1,0:T(8,128)(2,1)S(1)} %shard_map.211), channel_id=1, source_target_pairs={{0,96},{1,97},{2,98},{3,99},{4,100},{5,101},{6,102},{7,103},{8,104... | collective-permute-start | bytes 3932168 | tf_op jit(solution)/shard_map/ppermute | solution.py:60
  20.8 1.0 shard_map.212
  21.8 1.9 %collective-permute-start.1 = (bf16[4096,128]{1,0:T(8,128)(2,1)S(1)}, bf16[4096,128]{1,0:T(8,128)(2,1)S(1)}, u32[]{:S(2)}, u32[]{:S(2)}) collective-permute-start(bf16[4096,128]{1,0:T(8,128)(2,1)S(1)} %shard_map.212), channel_id=1, source_target_pairs={{0,96},{1,97},{2,98},{3,99},{4,100},{5,101},{6,102},{7,103},{8,104... | collective-permute-start | bytes 3145736 | tf_op jit(solution)/shard_map/ppermute | solution.py:60
  23.8 1.3 shard_map.213.refs_0_
  25.1 1.1 copy-done.3
  26.2 1.0 shard_map.214.refs_2_
  27.3 40.7 %collective-permute-done.1.refs_3_ = bf16[4096,128]{1,0:T(8,128)(2,1)S(1)} collective-permute-done((bf16[4096,128]{1,0:T(8,128)(2,1)S(1)}, bf16[4096,128]{1,0:T(8,128)(2,1)S(1)}, u32[]{:S(2)}, u32[]{:S(2)}) %collective-permute-start.1) | collective-permute-done | bytes 1048608 | tf_op jit(solution)/shard_map/ppermute | solution.py:60
  68.0 24.1 %all-gather.2.cloned.1.call-done = bf16[21504,128]{1,0:T(8,128)(2,1)} async-done(((bf16[672,128]{1,0:T(8,128)(2,1)}), bf16[21504,128]{1,0:T(8,128)(2,1)}) %all-gather.2.cloned.1.call-update) | async-done | bytes 5505040 | tf_op jit(solution)/shard_map/all_gather | solution.py:419
  92.1 6.8 %shard_map.215 = (f32[784,128]{1,0:T(8,128)S(1)}, bf16[784,128]{1,0:T(8,128)(2,1)S(1)}, bf16[16,64,128]{2,1,0:T(8,128)(2,1)}, bf16[128,128]{1,0:T(8,128)(2,1)S(1)}) custom-call(s32[3]{0:T(128)S(1)} %get-tuple-element.24.place_ref, bf16[32,672,128]{2,1,0:T(8,128)(2,1)} %bitcast.17, bf16[5120,128]{1,0:T(8,128)(2,1)} %copy-done.3, ...), custom_call_target="tpu_custom_call" | custom-call | tf_op jit(solution)/shard_map/pallas_call | solution.py:102
  98.9 6.1 %all-to-all-start = ((bf16[16,64,128]{2,1,0:T(8,128)(2,1)}), bf16[16,64,128]{2,1,0:T(8,128)(2,1)S(1)}, u32[]{:S(2)}, u32[]{:S(2)}) async-start(bf16[16,64,128]{2,1,0:T(8,128)(2,1)} %get-tuple-element.27), calls=%async_computation | async-start | bytes 524288 | tf_op jit(solution)/shard_map/all_to_all | solution.py:64
  105.0 4.8 %collective-permute-start.2 = (bf16[784,128]{1,0:T(8,128)(2,1)S(1)}, bf16[784,128]{1,0:T(8,128)(2,1)S(1)}, u32[]{:S(2)}, u32[]{:S(2)}) collective-permute-start(bf16[784,128]{1,0:T(8,128)(2,1)S(1)} %get-tuple-element.26), channel_id=1, source_target_pairs={{0,32},{1,33},{2,34},{3,35},{4,36},{5,37},{6,38},{7,39},{8,40},{9,... | collective-permute-start | bytes 602120 | tf_op jit(solution)/shard_map/ppermute | solution.py:51
  109.8 6.9 %collective-permute-done.2.got = bf16[784,128]{1,0:T(8,128)(2,1)S(1)} collective-permute-done((bf16[784,128]{1,0:T(8,128)(2,1)S(1)}, bf16[784,128]{1,0:T(8,128)(2,1)S(1)}, u32[]{:S(2)}, u32[]{:S(2)}) %collective-permute-start.2) | collective-permute-done | bytes 200736 | tf_op jit(solution)/shard_map/ppermute | solution.py:51
  116.8 1.5 shard_map.216
  118.3 8.5 %all_to_all.25.parts = bf16[8,48,128]{2,1,0:T(8,128)(2,1)S(1)} all-to-all(bf16[8,48,128]{2,1,0:T(8,128)(2,1)S(1)} %get-tuple-element.30), channel_id=1, replica_groups={{7,6,5,4,3,2,1,0},{15,14,13,12,11,10,9,8},{23,22,21,20,19,18,17,16},{31..., dimensions={0} | all-to-all | bytes 196608 | tf_op jit(solution)/shard_map/all_to_all | solution.py:64
  126.9 17.2 %all_to_all.26.parts = bf16[8,32,128]{2,1,0:T(8,128)(2,1)S(1)} all-to-all(bf16[8,32,128]{2,1,0:T(8,128)(2,1)S(1)} %get-tuple-element.31), channel_id=1, replica_groups={{16,24,0,8,48,56,32,40},{17,25,1,9,49,57,33,41},{18,26,2,10,50,58,34,42..., dimensions={0} | all-to-all | bytes 131072 | tf_op jit(solution)/shard_map/all_to_all | solution.py:64
  144.0 9.2 %all_to_all.27.low = bf16[8,32,128]{2,1,0:T(8,128)(2,1)S(1)} all-to-all(bf16[8,32,128]{2,1,0:T(8,128)(2,1)S(1)} %shard_map.218), channel_id=1, replica_groups={{7,6,5,4,3,2,1,0},{15,14,13,12,11,10,9,8},{23,22,21,20,19,18,17,16},{31..., dimensions={0} | all-to-all | bytes 131072 | tf_op jit(solution)/shard_map/all_to_all | solution.py:64
  153.4 11.7 %all_to_all.28.parts = bf16[8,208,128]{2,1,0:T(8,128)(2,1)S(1)} all-to-all(bf16[8,208,128]{2,1,0:T(8,128)(2,1)S(1)} %shard_map.219), channel_id=1, replica_groups={{448,384,320,256,192,128,64,0},{449,385,321,257,193,129,65,1},{450,386,..., dimensions={0} | all-to-all | bytes 851968 | tf_op jit(solution)/shard_map/all_to_all | solution.py:64
  165.1 0.7 shard_map.220
  (39 shorter events, 1.1 us)
Async XLA Ops:
  7.2 84.9 %all-gather.2.cloned.1.call-start = ((), (), s32[]{:S(2)}) async-start(), calls=%async_computation.5 | async-start | bytes 5677056 | tf_op jit(solution)/shard_map/all_gather | solution.py:419
  9.0 11.7 %copy-start.8 = (bf16[4,8192]{1,0:T(4,128)(2,1)S(1)}, bf16[4,8192]{1,0:T(4,128)(2,1)}, u32[]{:S(2)}) copy-start(bf16[4,8192]{1,0:T(4,128)(2,1)} %rest_1_.7) | copy-start | bytes 196612
  9.8 1.6 copy-start
  11.4 1.0 copy-start.4
  12.5 0.8 copy-start.6
  13.3 0.7 copy-start.12
  14.0 6.7 %copy-start.2 = (bf16[128,8192]{1,0:T(8,128)(2,1)S(1)}, bf16[128,8192]{1,0:T(8,128)(2,1)}, u32[]{:S(2)}) copy-start(bf16[128,8192]{1,0:T(8,128)(2,1)} %rest_0_.7) | copy-start | bytes 6291460
  15.4 8.4 %copy-start.1 = (bf16[8192,128]{1,0:T(8,128)(2,1)S(1)}, bf16[8192,128]{1,0:T(8,128)(2,1)}, u32[]{:S(2)}) copy-start(bf16[8192,128]{1,0:T(8,128)(2,1)} %rest_0_.6) | copy-start | bytes 6291460
  15.4 8.4 %copy-start.5 = (bf16[8192,32]{0,1:T(8,128)(2,1)S(1)}, bf16[8192,32]{0,1:T(8,128)(2,1)}, u32[]{:S(2)}) copy-start(bf16[8192,32]{0,1:T(8,128)(2,1)} %param.25) | copy-start | bytes 1572868
  15.4 8.4 %copy-start.7 = (bf16[256,128]{1,0:T(8,128)(2,1)S(1)}, bf16[256,128]{1,0:T(8,128)(2,1)}, u32[]{:S(2)}) copy-start(bf16[256,128]{1,0:T(8,128)(2,1)} %rest_1_.6) | copy-start | bytes 196612
  15.4 52.6 %collective-permute-start = (bf16[5120,128]{1,0:T(8,128)(2,1)S(1)}, bf16[5120,128]{1,0:T(8,128)(2,1)}, u32[]{:S(2)}, u32[]{:S(2)}) collective-permute-start(bf16[5120,128]{1,0:T(8,128)(2,1)S(1)} %shard_map.211), channel_id=1, source_target_pairs={{0,96},{1,97},{2,98},{3,99},{4,100},{5,101},{6,102},{7,103},{8,104... | collective-permute-start | bytes 3932168 | tf_op jit(solution)/shard_map/ppermute | solution.py:60
  21.8 46.1 %collective-permute-start.1 = (bf16[4096,128]{1,0:T(8,128)(2,1)S(1)}, bf16[4096,128]{1,0:T(8,128)(2,1)S(1)}, u32[]{:S(2)}, u32[]{:S(2)}) collective-permute-start(bf16[4096,128]{1,0:T(8,128)(2,1)S(1)} %shard_map.212), channel_id=1, source_target_pairs={{0,96},{1,97},{2,98},{3,99},{4,100},{5,101},{6,102},{7,103},{8,104... | collective-permute-start | bytes 3145736 | tf_op jit(solution)/shard_map/ppermute | solution.py:60
  25.1 1.1 copy-start.3
  92.1 24.6 %copy-start.9 = (bf16[256,128]{1,0:T(8,128)(2,1)S(1)}, bf16[256,128]{1,0:T(8,128)(2,1)}, u32[]{:S(2)}) copy-start(bf16[256,128]{1,0:T(8,128)(2,1)} %hidden.1) | copy-start | bytes 196612
  92.1 24.6 %copy-start.10 = (f32[256,64]{1,0:T(8,128)S(1)}, f32[256,64]{1,0:T(8,128)}, u32[]{:S(2)}) copy-start(f32[256,64]{1,0:T(8,128)} %constant.60.clone.cosine) | copy-start | bytes 196612
  92.1 24.7 %copy-start.11 = (f32[256,64]{1,0:T(8,128)S(1)}, f32[256,64]{1,0:T(8,128)}, u32[]{:S(2)}) copy-start(f32[256,64]{1,0:T(8,128)} %constant.61.clone.sine) | copy-start | bytes 196612
  92.1 24.7 %copy-start.13 = (f32[64,256]{1,0:T(8,128)S(1)}, f32[64,256]{1,0:T(8,128)}, u32[]{:S(2)}) copy-start(f32[64,256]{1,0:T(8,128)} %constant.62.clone.cosine_t) | copy-start | bytes 196612
  92.1 24.7 %copy-start.14 = (f32[64,256]{1,0:T(8,128)S(1)}, f32[64,256]{1,0:T(8,128)}, u32[]{:S(2)}) copy-start(f32[64,256]{1,0:T(8,128)} %constant.63.clone.sine_t) | copy-start | bytes 196612
  92.1 24.7 %copy-start.15 = (bf16[64,128]{1,0:T(8,128)(2,1)S(1)}, bf16[64,128]{1,0:T(8,128)(2,1)}, u32[]{:S(2)}) copy-start(bf16[64,128]{1,0:T(8,128)(2,1)} %query_up.1) | copy-start | bytes 49156
  92.1 24.7 %copy-start.16 = (bf16[128]{0:T(256)(128)(2,1)S(1)}, bf16[128]{0:T(256)(128)(2,1)}, u32[]{:S(2)}) copy-start(bf16[128]{0:T(256)(128)(2,1)} %param.22) | copy-start | bytes 772
  92.1 24.7 %copy-start.17 = (s32[1,256]{1,0:T(1,128)S(1)}, s32[1,256]{1,0:T(1,128)}, u32[]{:S(2)}) copy-start(s32[1,256]{1,0:T(1,128)} %snapshot.1) | copy-start | bytes 3076
  98.9 17.8 %all-to-all-start = ((bf16[16,64,128]{2,1,0:T(8,128)(2,1)}), bf16[16,64,128]{2,1,0:T(8,128)(2,1)S(1)}, u32[]{:S(2)}, u32[]{:S(2)}) async-start(bf16[16,64,128]{2,1,0:T(8,128)(2,1)} %get-tuple-element.27), calls=%async_computation | async-start | bytes 524288 | tf_op jit(solution)/shard_map/all_to_all | solution.py:64
  105.0 11.7 %collective-permute-start.2 = (bf16[784,128]{1,0:T(8,128)(2,1)S(1)}, bf16[784,128]{1,0:T(8,128)(2,1)S(1)}, u32[]{:S(2)}, u32[]{:S(2)}) collective-permute-start(bf16[784,128]{1,0:T(8,128)(2,1)S(1)} %get-tuple-element.26), channel_id=1, source_target_pairs={{0,32},{1,33},{2,34},{3,35},{4,36},{5,37},{6,38},{7,39},{8,40},{9,... | collective-permute-start | bytes 602120 | tf_op jit(solution)/shard_map/ppermute | solution.py:51
Sparse Core Ops, SparseCore 0:
  10.1 81.8 all-gather.1

commit v7 on v6

--- a/solution.py
+++ b/solution.py
@@ -21,8 +21,7 @@
 PARTS = 8
 BLOCKS = NZ * NC
 DOWNS_AT = LENGTH
-SQUARES_AT = DOWNS_AT + 2 * RANK
-COLUMNS_AT = SQUARES_AT + 16
+COLUMNS_AT = DOWNS_AT + 2 * RANK
 GRADS_AT = COLUMNS_AT + 16
 PACKET = GRADS_AT + LENGTH
 PER_HEAD = 2 * LENGTH
@@ -155,9 +154,9 @@
     squares = jnp.sum(values * values, axis=1, keepdims=True)
     rows = jnp.concatenate([to_row(squares[:128]), to_row(squares[128:])], axis=0)
     high, low = two_terms(rows)
-    packet[SQUARES_AT:COLUMNS_AT] = jnp.concatenate([high, low, jnp.zeros((12, 128), BF16)], axis=0)
+    right = [high[:, :RANK], high[:, RANK:], low[:, :RANK], low[:, RANK:], jnp.zeros((8, 128 - RANK), BF16)]
     packet[COLUMNS_AT:GRADS_AT] = jnp.concatenate(
-        [value_up[...], jnp.zeros((16, 128 - RANK), BF16)], axis=1
+        [value_up[...], jnp.concatenate(right, axis=0)], axis=1
     )
 
 
@@ -241,9 +240,10 @@
         wide = jnp.concatenate([block_rows(w, 0, 128) for w in outputs], axis=0)
         ctx += contract(rows(GRADS_AT, LENGTH), wide, 1, 1)
         for b in blocks:
-            squares += gathered[b, SQUARES_AT : SQUARES_AT + 16, :].astype(F32)
+            squares += gathered[b, COLUMNS_AT:GRADS_AT, :].astype(F32)
     low, kv = narrow[:, : 2 * RANK], narrow[:, 2 * RANK :].T.astype(BF16)
-    squares = squares[0:2] + squares[2:4]
+    squares = squares[:4, RANK:] + squares[4:8, RANK:]
+    squares = jnp.concatenate([squares[0:2], squares[2:4]], axis=1)
     at_zero = place_ref[0] == 0
     for a in range(NX):
         mine = at_zero if a == 0 else jnp.logical_not(at_zero)

time: 173 us -> 173 us (level)
  no operation moved by 1% of the time
where the time goes in v7:
time: 173 us; the launch traced here: 172 us
  waiting for transfers between devices  71.5 us (41%)
  blocking collectives  46.6 us (27%)
  starting transfers between devices  18 us (10%)
  Pallas kernels  16 us (9%)
  between operations  14.3 us (8%)
  local copies, waits for them, and re-layouts  5.33 us (3%)
    all_to_all x4, blocking collectives, exchange(): return lax.all_to_all(value, axis, 0, 0, axis_index_groups=groups)  46.6 us
    ppermute x2, waiting for transfers between devices, swap_weights(): return lax.ppermute(value, ('dp', 'fsdp'), pairs)  40.7 us
    all_gather x1, waiting for transfers between devices, local(): lax.all_gather(packet, 'fsdp', axis=0, tiled=True, axis_index_groups=HALF...  23.9 us
    pallas_call x11, Pallas kernels, call(): pl.pallas_call(body, out_shape=outs, in_specs=specs, out_specs=[VMEM] * l...  16 us
    ppermute x2, starting transfers between devices, swap_weights(): return lax.ppermute(value, ('dp', 'fsdp'), pairs)  7.27 us
    ppermute x1, waiting for transfers between devices, swap(): lax.ppermute(value, 'fsdp', [(i, i ^ mask) for i in range(NX * NZ * NC)])  6.86 us
    all_to_all x1, starting transfers between devices, exchange(): return lax.all_to_all(value, axis, 0, 0, axis_index_groups=groups)  5.91 us
    unnamed x36, local copies, waits for them, and re-layouts  5.33 us
  transfers between devices with their start and end apart: 5, of which 3 were waited for; matrix products, arithmetic and copies ran while one was open for 0% of the time, Pallas kernels for 3%

profile of v7, /device:TPU:1, one launch (start us, length us, event | category | flops | bytes accessed | tf_op | source)
XLA Modules:
  0.0 172.4 jit_solution(17456789437229555130)
XLA Ops:
  7.2 1.9 %shard_map.210 = bf16[656,128]{1,0:T(8,128)(2,1)} custom-call(bf16[256,128]{1,0:T(8,128)(2,1)} %hidden.1, bf16[1,128]{1,0:T(2,128)(2,1)} %bitcast.15, bf16[64,128]{1,0:T(8,128)(2,1)} %a_query_at.1, bf16[64,128]{1,0:T(8,128)(2,1)} %a_value_at.1, bf16[16,64]{1,0:T(8,128)(2,1)} %bitcast.18, bf16[256,128]{1,0:T(8,128)(2,1)} %grad_at.1), custom_call_target="tpu_custom_call" | custom-call | tf_op jit(solution)/shard_map/pallas_call | solution.py:101
  9.2 0.7 fusion
  10.0 1.6 copy-done
  11.6 1.0 copy-done.4
  12.6 0.8 copy-done.6
  14.2 1.3 shard_map.211
  15.5 5.4 %collective-permute-start = (bf16[5120,128]{1,0:T(8,128)(2,1)S(1)}, bf16[5120,128]{1,0:T(8,128)(2,1)}, u32[]{:S(2)}, u32[]{:S(2)}) collective-permute-start(bf16[5120,128]{1,0:T(8,128)(2,1)S(1)} %shard_map.211), channel_id=1, source_target_pairs={{0,96},{1,97},{2,98},{3,99},{4,100},{5,101},{6,102},{7,103},{8,104... | collective-permute-start | bytes 3932168 | tf_op jit(solution)/shard_map/ppermute | solution.py:59
  20.9 1.0 shard_map.212
  22.0 1.9 %collective-permute-start.1 = (bf16[4096,128]{1,0:T(8,128)(2,1)S(1)}, bf16[4096,128]{1,0:T(8,128)(2,1)S(1)}, u32[]{:S(2)}, u32[]{:S(2)}) collective-permute-start(bf16[4096,128]{1,0:T(8,128)(2,1)S(1)} %shard_map.212), channel_id=1, source_target_pairs={{0,96},{1,97},{2,98},{3,99},{4,100},{5,101},{6,102},{7,103},{8,104... | collective-permute-start | bytes 3145736 | tf_op jit(solution)/shard_map/ppermute | solution.py:59
  23.9 1.3 shard_map.213.refs_0_
  25.3 1.1 copy-done.3
  26.4 1.0 shard_map.214.refs_2_
  27.4 40.7 %collective-permute-done.1.refs_3_ = bf16[4096,128]{1,0:T(8,128)(2,1)S(1)} collective-permute-done((bf16[4096,128]{1,0:T(8,128)(2,1)S(1)}, bf16[4096,128]{1,0:T(8,128)(2,1)S(1)}, u32[]{:S(2)}, u32[]{:S(2)}) %collective-permute-start.1) | collective-permute-done | bytes 1048608 | tf_op jit(solution)/shard_map/ppermute | solution.py:59
  68.1 23.9 %all-gather.2.cloned.1.call-done = bf16[20992,128]{1,0:T(8,128)(2,1)} async-done(((bf16[656,128]{1,0:T(8,128)(2,1)}), bf16[20992,128]{1,0:T(8,128)(2,1)}) %all-gather.2.cloned.1.call-update) | async-done | bytes 5373968 | tf_op jit(solution)/shard_map/all_gather | solution.py:419
  92.0 6.8 %shard_map.215 = (f32[784,128]{1,0:T(8,128)S(1)}, bf16[784,128]{1,0:T(8,128)(2,1)S(1)}, bf16[16,64,128]{2,1,0:T(8,128)(2,1)}, bf16[128,128]{1,0:T(8,128)(2,1)S(1)}) custom-call(s32[3]{0:T(128)S(1)} %get-tuple-element.24.place_ref, bf16[32,656,128]{2,1,0:T(8,128)(2,1)} %bitcast.17, bf16[5120,128]{1,0:T(8,128)(2,1)} %copy-done.3, ...), custom_call_target="tpu_custom_call" | custom-call | tf_op jit(solution)/shard_map/pallas_call | solution.py:101
  98.8 5.9 %all-to-all-start = ((bf16[16,64,128]{2,1,0:T(8,128)(2,1)}), bf16[16,64,128]{2,1,0:T(8,128)(2,1)S(1)}, u32[]{:S(2)}, u32[]{:S(2)}) async-start(bf16[16,64,128]{2,1,0:T(8,128)(2,1)} %get-tuple-element.27), calls=%async_computation | async-start | bytes 524288 | tf_op jit(solution)/shard_map/all_to_all | solution.py:63
  104.8 4.8 %collective-permute-start.2 = (bf16[784,128]{1,0:T(8,128)(2,1)S(1)}, bf16[784,128]{1,0:T(8,128)(2,1)S(1)}, u32[]{:S(2)}, u32[]{:S(2)}) collective-permute-start(bf16[784,128]{1,0:T(8,128)(2,1)S(1)} %get-tuple-element.26), channel_id=1, source_target_pairs={{0,32},{1,33},{2,34},{3,35},{4,36},{5,37},{6,38},{7,39},{8,40},{9,... | collective-permute-start | bytes 602120 | tf_op jit(solution)/shard_map/ppermute | solution.py:50
  109.6 6.9 %collective-permute-done.2.got = bf16[784,128]{1,0:T(8,128)(2,1)S(1)} collective-permute-done((bf16[784,128]{1,0:T(8,128)(2,1)S(1)}, bf16[784,128]{1,0:T(8,128)(2,1)S(1)}, u32[]{:S(2)}, u32[]{:S(2)}) %collective-permute-start.2) | collective-permute-done | bytes 200736 | tf_op jit(solution)/shard_map/ppermute | solution.py:50
  116.5 1.5 shard_map.216
  118.1 8.5 %all_to_all.25.parts = bf16[8,48,128]{2,1,0:T(8,128)(2,1)S(1)} all-to-all(bf16[8,48,128]{2,1,0:T(8,128)(2,1)S(1)} %get-tuple-element.30), channel_id=1, replica_groups={{7,6,5,4,3,2,1,0},{15,14,13,12,11,10,9,8},{23,22,21,20,19,18,17,16},{31..., dimensions={0} | all-to-all | bytes 196608 | tf_op jit(solution)/shard_map/all_to_all | solution.py:63
  126.6 17.2 %all_to_all.26.parts = bf16[8,32,128]{2,1,0:T(8,128)(2,1)S(1)} all-to-all(bf16[8,32,128]{2,1,0:T(8,128)(2,1)S(1)} %get-tuple-element.31), channel_id=1, replica_groups={{16,24,0,8,48,56,32,40},{17,25,1,9,49,57,33,41},{18,26,2,10,50,58,34,42..., dimensions={0} | all-to-all | bytes 131072 | tf_op jit(solution)/shard_map/all_to_all | solution.py:63
  143.8 9.2 %all_to_all.27.low = bf16[8,32,128]{2,1,0:T(8,128)(2,1)S(1)} all-to-all(bf16[8,32,128]{2,1,0:T(8,128)(2,1)S(1)} %shard_map.218), channel_id=1, replica_groups={{7,6,5,4,3,2,1,0},{15,14,13,12,11,10,9,8},{23,22,21,20,19,18,17,16},{31..., dimensions={0} | all-to-all | bytes 131072 | tf_op jit(solution)/shard_map/all_to_all | solution.py:63
  153.2 11.7 %all_to_all.28.parts = bf16[8,208,128]{2,1,0:T(8,128)(2,1)S(1)} all-to-all(bf16[8,208,128]{2,1,0:T(8,128)(2,1)S(1)} %shard_map.219), channel_id=1, replica_groups={{448,384,320,256,192,128,64,0},{449,385,321,257,193,129,65,1},{450,386,..., dimensions={0} | all-to-all | bytes 851968 | tf_op jit(solution)/shard_map/all_to_all | solution.py:63
  164.9 0.7 shard_map.220
  (39 shorter events, 1.1 us)
Async XLA Ops:
  7.2 84.8 %all-gather.2.cloned.1.call-start = ((), (), s32[]{:S(2)}) async-start(), calls=%async_computation.5 | async-start | bytes 5541888 | tf_op jit(solution)/shard_map/all_gather | solution.py:419
  9.2 11.7 %copy-start.8 = (bf16[4,8192]{1,0:T(4,128)(2,1)S(1)}, bf16[4,8192]{1,0:T(4,128)(2,1)}, u32[]{:S(2)}) copy-start(bf16[4,8192]{1,0:T(4,128)(2,1)} %rest_1_.7) | copy-start | bytes 196612
  10.0 1.6 copy-start
  11.6 1.0 copy-start.4
  12.6 0.8 copy-start.6
  13.4 0.7 copy-start.12
  14.2 6.7 %copy-start.2 = (bf16[128,8192]{1,0:T(8,128)(2,1)S(1)}, bf16[128,8192]{1,0:T(8,128)(2,1)}, u32[]{:S(2)}) copy-start(bf16[128,8192]{1,0:T(8,128)(2,1)} %rest_0_.7) | copy-start | bytes 6291460
  15.5 8.4 %copy-start.1 = (bf16[8192,128]{1,0:T(8,128)(2,1)S(1)}, bf16[8192,128]{1,0:T(8,128)(2,1)}, u32[]{:S(2)}) copy-start(bf16[8192,128]{1,0:T(8,128)(2,1)} %rest_0_.6) | copy-start | bytes 6291460
  15.5 8.4 %copy-start.5 = (bf16[8192,32]{0,1:T(8,128)(2,1)S(1)}, bf16[8192,32]{0,1:T(8,128)(2,1)}, u32[]{:S(2)}) copy-start(bf16[8192,32]{0,1:T(8,128)(2,1)} %param.25) | copy-start | bytes 1572868
  15.5 8.4 %copy-start.7 = (bf16[256,128]{1,0:T(8,128)(2,1)S(1)}, bf16[256,128]{1,0:T(8,128)(2,1)}, u32[]{:S(2)}) copy-start(bf16[256,128]{1,0:T(8,128)(2,1)} %rest_1_.6) | copy-start | bytes 196612
  15.5 52.6 %collective-permute-start = (bf16[5120,128]{1,0:T(8,128)(2,1)S(1)}, bf16[5120,128]{1,0:T(8,128)(2,1)}, u32[]{:S(2)}, u32[]{:S(2)}) collective-permute-start(bf16[5120,128]{1,0:T(8,128)(2,1)S(1)} %shard_map.211), channel_id=1, source_target_pairs={{0,96},{1,97},{2,98},{3,99},{4,100},{5,101},{6,102},{7,103},{8,104... | collective-permute-start | bytes 3932168 | tf_op jit(solution)/shard_map/ppermute | solution.py:59
  22.0 46.1 %collective-permute-start.1 = (bf16[4096,128]{1,0:T(8,128)(2,1)S(1)}, bf16[4096,128]{1,0:T(8,128)(2,1)S(1)}, u32[]{:S(2)}, u32[]{:S(2)}) collective-permute-start(bf16[4096,128]{1,0:T(8,128)(2,1)S(1)} %shard_map.212), channel_id=1, source_target_pairs={{0,96},{1,97},{2,98},{3,99},{4,100},{5,101},{6,102},{7,103},{8,104... | collective-permute-start | bytes 3145736 | tf_op jit(solution)/shard_map/ppermute | solution.py:59
  25.3 1.1 copy-start.3
  92.0 24.4 %copy-start.9 = (bf16[256,128]{1,0:T(8,128)(2,1)S(1)}, bf16[256,128]{1,0:T(8,128)(2,1)}, u32[]{:S(2)}) copy-start(bf16[256,128]{1,0:T(8,128)(2,1)} %hidden.1) | copy-start | bytes 196612
  92.0 24.4 %copy-start.10 = (f32[256,64]{1,0:T(8,128)S(1)}, f32[256,64]{1,0:T(8,128)}, u32[]{:S(2)}) copy-start(f32[256,64]{1,0:T(8,128)} %constant.60.clone.cosine) | copy-start | bytes 196612
  92.0 24.4 %copy-start.11 = (f32[256,64]{1,0:T(8,128)S(1)}, f32[256,64]{1,0:T(8,128)}, u32[]{:S(2)}) copy-start(f32[256,64]{1,0:T(8,128)} %constant.61.clone.sine) | copy-start | bytes 196612
  92.0 24.4 %copy-start.13 = (f32[64,256]{1,0:T(8,128)S(1)}, f32[64,256]{1,0:T(8,128)}, u32[]{:S(2)}) copy-start(f32[64,256]{1,0:T(8,128)} %constant.62.clone.cosine_t) | copy-start | bytes 196612
  92.0 24.5 %copy-start.14 = (f32[64,256]{1,0:T(8,128)S(1)}, f32[64,256]{1,0:T(8,128)}, u32[]{:S(2)}) copy-start(f32[64,256]{1,0:T(8,128)} %constant.63.clone.sine_t) | copy-start | bytes 196612
  92.0 24.5 %copy-start.15 = (bf16[64,128]{1,0:T(8,128)(2,1)S(1)}, bf16[64,128]{1,0:T(8,128)(2,1)}, u32[]{:S(2)}) copy-start(bf16[64,128]{1,0:T(8,128)(2,1)} %query_up.1) | copy-start | bytes 49156
  92.0 24.5 %copy-start.16 = (bf16[128]{0:T(256)(128)(2,1)S(1)}, bf16[128]{0:T(256)(128)(2,1)}, u32[]{:S(2)}) copy-start(bf16[128]{0:T(256)(128)(2,1)} %param.22) | copy-start | bytes 772
  92.0 24.5 %copy-start.17 = (s32[1,256]{1,0:T(1,128)S(1)}, s32[1,256]{1,0:T(1,128)}, u32[]{:S(2)}) copy-start(s32[1,256]{1,0:T(1,128)} %snapshot.1) | copy-start | bytes 3076
  98.8 17.6 %all-to-all-start = ((bf16[16,64,128]{2,1,0:T(8,128)(2,1)}), bf16[16,64,128]{2,1,0:T(8,128)(2,1)S(1)}, u32[]{:S(2)}, u32[]{:S(2)}) async-start(bf16[16,64,128]{2,1,0:T(8,128)(2,1)} %get-tuple-element.27), calls=%async_computation | async-start | bytes 524288 | tf_op jit(solution)/shard_map/all_to_all | solution.py:63
  104.8 11.7 %collective-permute-start.2 = (bf16[784,128]{1,0:T(8,128)(2,1)S(1)}, bf16[784,128]{1,0:T(8,128)(2,1)S(1)}, u32[]{:S(2)}, u32[]{:S(2)}) collective-permute-start(bf16[784,128]{1,0:T(8,128)(2,1)S(1)} %get-tuple-element.26), channel_id=1, source_target_pairs={{0,32},{1,33},{2,34},{3,35},{4,36},{5,37},{6,38},{7,39},{8,40},{9,... | collective-permute-start | bytes 602120 | tf_op jit(solution)/shard_map/ppermute | solution.py:50
Sparse Core Ops, SparseCore 0:
  10.1 81.8 all-gather.1
